TPU v7x, 32 devices: a whole 2x2x4 slice. The times are simulated.
32 devices in a mesh: batch: 2 (over core), inner: 4 (over y, x), outer: 4 (over z).
Axes of the slice: x: 2, y: 2, z: 4, core: 2. Of those that a mesh axis runs over, the one named last changes fastest.
Arguments:
- images: bfloat16 [32, 16, 32, 1024], P(('batch', 'inner'), None, None, 'outer'), may hold values from -6 to 6
- extents: int32 [32, 2], replicated, may hold values from 4 to 16, as said below
- first_reduce: bfloat16 [1024, 512], P('outer', 'inner'), may hold values from -0.1875 to 0.1875
- first_taps: bfloat16 [3, 3, 512, 512], P(None, None, None, ('inner', 'outer')), may hold values from -0.09375 to 0.09375
- first_expand: bfloat16 [512, 2048], P('inner', 'outer'), may hold values from -0.25 to 0.25
- first_shortcut: bfloat16 [1024, 2048], P('outer', 'inner'), may hold values from -0.1875 to 0.1875
- second_reduce: bfloat16 [2048, 512], P('outer', 'inner'), may hold values from -0.125 to 0.125
- second_taps: bfloat16 [3, 3, 512, 512], P(None, None, None, ('inner', 'outer')), may hold values from -0.09375 to 0.09375
- second_expand: bfloat16 [512, 2048], P('inner', 'outer'), may hold values from -0.25 to 0.25
- mid_gains: float32 [4, 512], replicated, may hold values from 0.1 to 1.9
- mid_shifts: float32 [4, 512], replicated, may hold values from -3 to 3
- wide_gains: float32 [3, 2048], replicated, may hold values from 0.1 to 1.9
- wide_shifts: float32 [3, 2048], replicated, may hold values from -3 to 3
- cotangent: bfloat16 [32, 8, 16, 2048], P(('batch', 'inner'), None, None, 'outer'), may hold values from -6 to 6
Outputs:
- block_output: bfloat16 [32, 8, 16, 2048], P(('batch', 'inner'), None, None, 'outer')
- grad_images: float32 [32, 16, 32, 1024], P(('batch', 'inner'), None, None, 'outer')
- grad_first_reduce: float32 [1024, 512], P('outer', 'inner')
- grad_first_taps: float32 [3, 3, 512, 512], P(None, None, None, ('inner', 'outer'))
- grad_first_expand: float32 [512, 2048], P('inner', 'outer')
- grad_first_shortcut: float32 [1024, 2048], P('outer', 'inner')
- grad_second_reduce: float32 [2048, 512], P('outer', 'inner')
- grad_second_taps: float32 [3, 3, 512, 512], P(None, None, None, ('inner', 'outer'))
- grad_second_expand: float32 [512, 2048], P('inner', 'outer')
- grad_mid_gains: float32 [4, 512], replicated
- grad_mid_shifts: float32 [4, 512], replicated
- grad_wide_gains: float32 [3, 2048], replicated
- grad_wide_shifts: float32 [3, 2048], replicated
Inputs may be any that keep to these rules, and one draw needn't show every extreme that they name: `extents`: row n holds image n's height (from 4 to 8) and width (from 8 to 16) in output cells; some image is exactly 8 by 16.
All inputs are finite; a program needn't handle non-finite values.
Results may differ from a plain program's by a relative error of at most 0.017.
Values may be sent and summed in bfloat16 or wider, within the bound.
No kernel may reach another device: no remote copies, remote signals or barrier semaphores. Data moves between devices by JAX's collectives and lax.ppermute only.
A program may use at most 192 MiB of HBM per device.

v0:
```python
import jax
import jax.numpy as jnp
from jax import lax
from jax.sharding import PartitionSpec as P

EPS = 1e-05


def valid_mask(extents, first_image, image_count, rows_all, cols_all, factor):
    picked = lax.dynamic_slice_in_dim(extents, first_image, image_count, 0)
    heights = picked[:, 0] * factor
    widths = picked[:, 1] * factor
    inside_rows = jnp.arange(rows_all, dtype=jnp.int32)[None, :, None] < heights[:, None, None]
    inside_cols = jnp.arange(cols_all, dtype=jnp.int32)[None, None, :] < widths[:, None, None]
    return jnp.logical_and(inside_rows, inside_cols).astype(jnp.float32)[..., None]


def dot_right(left_rows, matrix):
    return jnp.dot(left_rows, matrix, preferred_element_type=jnp.float32)


def dot_back(left_rows, matrix):
    return lax.dot_general(
        left_rows, matrix, (((1,), (1,)), ((), ())), preferred_element_type=jnp.float32
    )


def dot_outer(left_rows, right_rows):
    return lax.dot_general(
        left_rows, right_rows, (((0,), (0,)), ((), ())), preferred_element_type=jnp.float32
    )


def tap_window(padded, tap_row, tap_col, stride, rows_out, cols_out):
    return padded[
        :,
        tap_row : tap_row + stride * (rows_out - 1) + 1 : stride,
        tap_col : tap_col + stride * (cols_out - 1) + 1 : stride,
        :,
    ]


def taps_forward(activation, weight, stride, rows_out, cols_out):
    padded = jnp.pad(activation, ((0, 0), (1, 1), (1, 1), (0, 0)))
    summed = jnp.zeros((activation.shape[0], rows_out, cols_out, weight.shape[3]), jnp.float32)
    for tap_row in range(3):
        for tap_col in range(3):
            window = tap_window(padded, tap_row, tap_col, stride, rows_out, cols_out)
            summed = summed + jnp.einsum(
                "nhwc,cd->nhwd",
                window,
                weight[tap_row, tap_col],
                preferred_element_type=jnp.float32,
            )
    return summed


def taps_input(grad_low, weight, stride, rows_in, cols_in):
    rows_out = grad_low.shape[1]
    cols_out = grad_low.shape[2]
    reach_rows = stride * (rows_out - 1) + 1
    reach_cols = stride * (cols_out - 1) + 1
    summed = jnp.zeros((grad_low.shape[0], rows_in + 2, cols_in + 2, weight.shape[2]), jnp.float32)
    for tap_row in range(3):
        for tap_col in range(3):
            term = jnp.einsum(
                "nhwd,cd->nhwc",
                grad_low,
                weight[tap_row, tap_col],
                preferred_element_type=jnp.float32,
            )
            summed = summed + lax.pad(
                term,
                jnp.float32(0),
                (
                    (0, 0, 0),
                    (tap_row, rows_in + 2 - tap_row - reach_rows, stride - 1),
                    (tap_col, cols_in + 2 - tap_col - reach_cols, stride - 1),
                    (0, 0, 0),
                ),
            )
    return summed[:, 1:-1, 1:-1, :]


def taps_weight(activation, grad_low, stride):
    rows_out = grad_low.shape[1]
    cols_out = grad_low.shape[2]
    padded = jnp.pad(activation, ((0, 0), (1, 1), (1, 1), (0, 0)))
    tap_rows = []
    for tap_row in range(3):
        tap_cols = []
        for tap_col in range(3):
            window = tap_window(padded, tap_row, tap_col, stride, rows_out, cols_out)
            tap_cols.append(
                jnp.einsum("nhwc,nhwd->cd", window, grad_low, preferred_element_type=jnp.float32)
            )
        tap_rows.append(jnp.stack(tap_cols))
    return jnp.stack(tap_rows)


def join_blocks(grouped, n_inner, n_outer):
    block_rows = grouped.shape[1]
    block_cols = grouped.shape[2]
    grid = grouped.reshape(n_inner, n_outer, block_rows, block_cols)
    return grid.transpose(1, 2, 0, 3).reshape(n_outer * block_rows, n_inner * block_cols)


def split_blocks(whole, n_inner, n_outer):
    block_rows = whole.shape[0] // n_outer
    block_cols = whole.shape[1] // n_inner
    grid = whole.reshape(n_outer, block_rows, n_inner, block_cols).transpose(2, 0, 1, 3)
    return grid.reshape(n_inner * n_outer * block_rows, block_cols)


def gelu_back(tensor, grad):
    return jax.vjp(jax.nn.gelu, tensor)[1](grad)[0]


def global_sums(stacked):
    return lax.psum(stacked, ("batch", "inner", "outer"))


def placed(vector, offset, length):
    return lax.dynamic_update_slice(jnp.zeros((length,), jnp.float32), vector, (offset,))


def piece_of(vector, offset, width):
    return lax.dynamic_slice_in_dim(vector, offset, width, 0)


def moments(entries):
    sums = []
    for tensor, valid_cells, offset, length, cell_count in entries:
        sums.append(placed(jnp.sum(tensor * valid_cells, axis=(0, 1, 2)), offset, length))
        sums.append(placed(jnp.sum(tensor * tensor * valid_cells, axis=(0, 1, 2)), offset, length))
    summed = global_sums(jnp.stack(sums))
    results = []
    for position, (tensor, valid_cells, offset, length, cell_count) in enumerate(entries):
        width = tensor.shape[3]
        mean_row = piece_of(summed[2 * position], offset, width) / cell_count
        spread = (
            piece_of(summed[2 * position + 1], offset, width) / cell_count - mean_row * mean_row
        )
        results.append((mean_row, lax.rsqrt(spread + EPS)))
    return results


def norm_back(entries):
    sums = []
    normals = []
    for grad, tensor, stats, gain_row, valid_cells, offset, length, cell_count in entries:
        normal = (tensor - stats[0]) * stats[1]
        normals.append(normal)
        sums.append(placed(jnp.sum(grad, axis=(0, 1, 2)), offset, length))
        sums.append(placed(jnp.sum(grad * normal, axis=(0, 1, 2)), offset, length))
    summed = global_sums(jnp.stack(sums))
    results = []
    for position, (
        grad,
        tensor,
        stats,
        gain_row,
        valid_cells,
        offset,
        length,
        cell_count,
    ) in enumerate(entries):
        width = grad.shape[3]
        shift_sum = piece_of(summed[2 * position], offset, width)
        gain_sum = piece_of(summed[2 * position + 1], offset, width)
        tensor_grad = (
            gain_row
            * stats[1]
            * (grad - valid_cells * (shift_sum + normals[position] * gain_sum) / cell_count)
        )
        results.append(
            (tensor_grad.astype(jnp.bfloat16), summed[2 * position + 1], summed[2 * position])
        )
    return results


def shards(
    images,
    extents,
    first_reduce,
    first_taps,
    first_expand,
    first_shortcut,
    second_reduce,
    second_taps,
    second_expand,
    mid_gains,
    mid_shifts,
    wide_gains,
    wide_shifts,
    cotangent,
):
    batch_pos = lax.axis_index("batch")
    inner_pos = lax.axis_index("inner")
    outer_pos = lax.axis_index("outer")
    n_inner = lax.axis_size("inner")
    n_outer = lax.axis_size("outer")
    grid_count = n_inner * n_outer
    img_dev, high_in, broad_in, in_part = images.shape
    high_out = high_in // 2
    broad_out = broad_in // 2
    out_part = cotangent.shape[3]
    mid_total = mid_gains.shape[1]
    wide_total = wide_gains.shape[1]
    wide_offset = outer_pos * out_part
    wide_first = (batch_pos * n_inner + inner_pos) * img_dev
    count_out = jnp.sum(extents[:, 0] * extents[:, 1]).astype(jnp.float32)
    count_in = 4.0 * count_out
    valid_in = valid_mask(extents, wide_first, img_dev, high_in, broad_in, 2)
    valid_out = valid_mask(extents, wide_first, img_dev, high_out, broad_out, 1)

    def to_pixels(wide_rows):
        return lax.all_to_all(wide_rows, "outer", split_axis=0, concat_axis=1, tiled=True)

    def to_wide(pixel_rows):
        return lax.all_to_all(pixel_rows, "outer", split_axis=1, concat_axis=0, tiled=True)

    mid_count = n_inner * img_dev // n_outer
    mid_first = batch_pos * n_inner * img_dev + outer_pos * mid_count
    mid_offset = inner_pos * first_reduce.shape[1]
    gathered = lax.all_gather(
        first_shortcut.reshape(-1)[None], ("inner", "outer"), axis=0, tiled=True
    )
    shortcut_full = join_blocks(
        gathered.reshape((grid_count,) + first_shortcut.shape), n_inner, n_outer
    )
    taps_one, taps_two = (
        lax.all_gather(first_taps, "outer", axis=3, tiled=True),
        lax.all_gather(second_taps, "outer", axis=3, tiled=True),
    )
    weights = (first_reduce, taps_one, first_expand, second_reduce, taps_two, second_expand)

    def channels_down(rows_local, matrix):
        gathered_rows = lax.all_gather(rows_local, "inner", axis=0, tiled=True)
        share = gathered_rows.shape[0] // n_outer

        def partial_rows(begin_row, row_count):
            return dot_right(gathered_rows, matrix)

        return (
            lax.psum_scatter(
                partial_rows(jnp.int32(0), share * lax.axis_size("outer")),
                "outer",
                scatter_dimension=0,
                tiled=True,
            ),
            gathered_rows,
        )

    def channels_up(rows_local, matrix):
        gathered_rows = lax.all_gather(rows_local, "outer", axis=0, tiled=True)
        share = gathered_rows.shape[0] // n_inner

        def partial_rows(begin_row, row_count):
            return dot_right(gathered_rows, matrix)

        return (
            lax.psum_scatter(
                partial_rows(jnp.int32(0), share * lax.axis_size("inner")),
                "inner",
                scatter_dimension=0,
                tiled=True,
            ),
            gathered_rows,
        )

    def conv_reduce(wide, weight):
        mid, kept = channels_down(wide.reshape(-1, wide.shape[3]), weight)
        return (mid.reshape(mid_count, wide.shape[1], wide.shape[2], weight.shape[1]), kept)

    def conv_expand(mid, weight):
        wide, kept = channels_up(mid.reshape(-1, mid.shape[3]), weight)
        return (wide.reshape(img_dev, mid.shape[1], mid.shape[2], weight.shape[1]), kept)

    def conv_taps(activation, weight, stride):
        whole = lax.all_gather(activation, "inner", axis=3, tiled=True)
        return (taps_forward(whole, weight, stride, high_out, broad_out), whole)

    def back_expand(grad_low, weight, kept):
        mid_grad, grad_rows = channels_down(grad_low.reshape(-1, grad_low.shape[3]), weight.T)
        return (
            mid_grad.reshape(mid_count, grad_low.shape[1], grad_low.shape[2], weight.shape[0]),
            dot_outer(kept, grad_rows),
        )

    def back_taps(grad_low, weight, stride, kept):
        partial_grad = taps_input(grad_low, weight, stride, kept.shape[1], kept.shape[2])
        return (
            lax.psum_scatter(partial_grad, "inner", scatter_dimension=3, tiled=True),
            taps_weight(kept, grad_low, stride),
        )

    def back_reduce(grad_low, weight, kept):
        wide_grad, grad_rows = channels_up(grad_low.reshape(-1, grad_low.shape[3]), weight.T)
        return (
            wide_grad.reshape(img_dev, grad_low.shape[1], grad_low.shape[2], weight.shape[0]),
            dot_outer(kept, grad_rows),
        )

    reduce_one_w, taps_one_w, expand_one_w, reduce_two_w, taps_two_w, expand_two_w = weights
    mid_width = reduce_one_w.shape[1]
    valid_mid_in = valid_mask(extents, mid_first, mid_count, high_in, broad_in, 2)
    valid_mid_out = valid_mask(extents, mid_first, mid_count, high_out, broad_out, 1)

    def mid_part(vector):
        return piece_of(vector, mid_offset, mid_width)

    def wide_part(vector):
        return piece_of(vector, wide_offset, out_part)

    def normed_of(tensor, stats, gain_row, shift_row):
        return (tensor - stats[0]) * stats[1] * gain_row + shift_row

    masked = images * valid_in.astype(jnp.bfloat16)
    strided = masked[:, 0::2, 0::2, :]
    z_one, kept_one = conv_reduce(masked, reduce_one_w)
    (stats_one,) = moments([(z_one, valid_mid_in, mid_offset, mid_total, count_in)])
    normed_one = normed_of(z_one, stats_one, mid_part(mid_gains[0]), mid_part(mid_shifts[0]))
    act_one = (jax.nn.gelu(normed_one) * valid_mid_in).astype(jnp.bfloat16)
    z_two, kept_two = conv_taps(act_one, taps_one_w, 2)
    (stats_two,) = moments([(z_two, valid_mid_out, mid_offset, mid_total, count_out)])
    normed_two = normed_of(z_two, stats_two, mid_part(mid_gains[1]), mid_part(mid_shifts[1]))
    act_two = (jax.nn.gelu(normed_two) * valid_mid_out).astype(jnp.bfloat16)
    z_three, kept_three = conv_expand(act_two, expand_one_w)
    short_pixels = to_pixels(strided.reshape(-1, in_part))
    z_short = to_wide(dot_right(short_pixels, shortcut_full)).reshape(
        img_dev, high_out, broad_out, out_part
    )
    stats_three, stats_short = moments(
        [
            (z_three, valid_out, wide_offset, wide_total, count_out),
            (z_short, valid_out, wide_offset, wide_total, count_out),
        ]
    )
    joined_one = normed_of(
        z_three, stats_three, wide_part(wide_gains[0]), wide_part(wide_shifts[0])
    ) + normed_of(z_short, stats_short, wide_part(wide_gains[1]), wide_part(wide_shifts[1]))
    hidden = jax.nn.gelu(joined_one) * valid_out
    hidden_low = hidden.astype(jnp.bfloat16)
    z_four, kept_four = conv_reduce(hidden_low, reduce_two_w)
    (stats_four,) = moments([(z_four, valid_mid_out, mid_offset, mid_total, count_out)])
    normed_four = normed_of(z_four, stats_four, mid_part(mid_gains[2]), mid_part(mid_shifts[2]))
    act_four = (jax.nn.gelu(normed_four) * valid_mid_out).astype(jnp.bfloat16)
    z_five, kept_five = conv_taps(act_four, taps_two_w, 1)
    (stats_five,) = moments([(z_five, valid_mid_out, mid_offset, mid_total, count_out)])
    normed_five = normed_of(z_five, stats_five, mid_part(mid_gains[3]), mid_part(mid_shifts[3]))
    act_five = (jax.nn.gelu(normed_five) * valid_mid_out).astype(jnp.bfloat16)
    z_six, kept_six = conv_expand(act_five, expand_two_w)
    (stats_six,) = moments([(z_six, valid_out, wide_offset, wide_total, count_out)])
    joined_two = (
        normed_of(z_six, stats_six, wide_part(wide_gains[2]), wide_part(wide_shifts[2])) + hidden
    )
    block_output = (jax.nn.gelu(joined_two) * valid_out).astype(jnp.bfloat16)
    grad_joined_two = gelu_back(joined_two, cotangent.astype(jnp.float32) * valid_out)
    ((grad_z_six, gain_six, shift_six),) = norm_back(
        [
            (
                grad_joined_two,
                z_six,
                stats_six,
                wide_part(wide_gains[2]),
                valid_out,
                wide_offset,
                wide_total,
                count_out,
            )
        ]
    )
    grad_act_five, grad_expand_two = back_expand(grad_z_six, expand_two_w, kept_six)
    grad_normed_five = gelu_back(normed_five, grad_act_five * valid_mid_out)
    ((grad_z_five, gain_five, shift_five),) = norm_back(
        [
            (
                grad_normed_five,
                z_five,
                stats_five,
                mid_part(mid_gains[3]),
                valid_mid_out,
                mid_offset,
                mid_total,
                count_out,
            )
        ]
    )
    grad_act_four, grad_taps_two = back_taps(grad_z_five, taps_two_w, 1, kept_five)
    grad_normed_four = gelu_back(normed_four, grad_act_four * valid_mid_out)
    ((grad_z_four, gain_four, shift_four),) = norm_back(
        [
            (
                grad_normed_four,
                z_four,
                stats_four,
                mid_part(mid_gains[2]),
                valid_mid_out,
                mid_offset,
                mid_total,
                count_out,
            )
        ]
    )
    grad_hidden_conv, grad_reduce_two = back_reduce(grad_z_four, reduce_two_w, kept_four)
    grad_hidden = grad_joined_two + grad_hidden_conv
    grad_joined_one = gelu_back(joined_one, grad_hidden * valid_out)
    (grad_z_three, gain_three, shift_three), (grad_z_short, gain_short, shift_short) = norm_back(
        [
            (
                grad_joined_one,
                z_three,
                stats_three,
                wide_part(wide_gains[0]),
                valid_out,
                wide_offset,
                wide_total,
                count_out,
            ),
            (
                grad_joined_one,
                z_short,
                stats_short,
                wide_part(wide_gains[1]),
                valid_out,
                wide_offset,
                wide_total,
                count_out,
            ),
        ]
    )
    grad_act_two, grad_expand_one = back_expand(grad_z_three, expand_one_w, kept_three)
    grad_normed_two = gelu_back(normed_two, grad_act_two * valid_mid_out)
    ((grad_z_two, gain_two, shift_two),) = norm_back(
        [
            (
                grad_normed_two,
                z_two,
                stats_two,
                mid_part(mid_gains[1]),
                valid_mid_out,
                mid_offset,
                mid_total,
                count_out,
            )
        ]
    )
    grad_act_one, grad_taps_one = back_taps(grad_z_two, taps_one_w, 2, kept_two)
    grad_normed_one = gelu_back(normed_one, grad_act_one * valid_mid_in)
    ((grad_z_one, gain_one, shift_one),) = norm_back(
        [
            (
                grad_normed_one,
                z_one,
                stats_one,
                mid_part(mid_gains[0]),
                valid_mid_in,
                mid_offset,
                mid_total,
                count_in,
            )
        ]
    )
    grad_in_conv, grad_reduce_one = back_reduce(grad_z_one, reduce_one_w, kept_one)
    short_grad_pixels = to_pixels(grad_z_short.reshape(-1, out_part))
    grad_in_short = to_wide(dot_back(short_grad_pixels, shortcut_full)).reshape(
        img_dev, high_out, broad_out, in_part
    )
    grad_shortcut = dot_outer(short_pixels, short_grad_pixels)
    spread_short = lax.pad(
        grad_in_short, jnp.float32(0), ((0, 0, 0), (0, 1, 1), (0, 1, 1), (0, 0, 0))
    )
    grad_images = (grad_in_conv + spread_short) * valid_in
    taps_first = lax.psum_scatter(grad_taps_one, "outer", scatter_dimension=3, tiled=True)
    taps_second = lax.psum_scatter(grad_taps_two, "outer", scatter_dimension=3, tiled=True)
    short_sum = lax.psum_scatter(
        split_blocks(grad_shortcut, n_inner, n_outer).reshape(grid_count, -1),
        ("inner", "outer"),
        scatter_dimension=0,
        tiled=True,
    )[0]
    summed_grads = lax.psum(
        (
            grad_reduce_one,
            taps_first,
            grad_expand_one,
            short_sum.reshape(first_shortcut.shape),
            grad_reduce_two,
            taps_second,
            grad_expand_two,
        ),
        "batch",
    )
    grad_mid_gains = jnp.stack([gain_one, gain_two, gain_four, gain_five])
    grad_mid_shifts = jnp.stack([shift_one, shift_two, shift_four, shift_five])
    grad_wide_gains = jnp.stack([gain_three, gain_short, gain_six])
    grad_wide_shifts = jnp.stack([shift_three, shift_short, shift_six])
    return (
        block_output,
        grad_images,
        summed_grads[0],
        summed_grads[1],
        summed_grads[2],
        summed_grads[3],
        summed_grads[4],
        summed_grads[5],
        summed_grads[6],
        grad_mid_gains,
        grad_mid_shifts,
        grad_wide_gains,
        grad_wide_shifts,
    )


def solution(mesh):
    return jax.shard_map(
        shards,
        mesh=mesh,
        in_specs=(
            P(("batch", "inner"), None, None, "outer"),
            P(),
            P("outer", "inner"),
            P(None, None, None, ("inner", "outer")),
            P("inner", "outer"),
            P("outer", "inner"),
            P("outer", "inner"),
            P(None, None, None, ("inner", "outer")),
            P("inner", "outer"),
            P(),
            P(),
            P(),
            P(),
            P(("batch", "inner"), None, None, "outer"),
        ),
        out_specs=(
            P(("batch", "inner"), None, None, "outer"),
            P(("batch", "inner"), None, None, "outer"),
            P("outer", "inner"),
            P(None, None, None, ("inner", "outer")),
            P("inner", "outer"),
            P("outer", "inner"),
            P("outer", "inner"),
            P(None, None, None, ("inner", "outer")),
            P("inner", "outer"),
            P(),
            P(),
            P(),
            P(),
        ),
        check_vma=False,
    )
```

profile of v0, /device:TPU:0, one launch (start us, length us, event | category | flops | bytes accessed | tf_op | source)
XLA Modules:
  0.0 2193.8 jit_solution(18325802462476251589)
XLA Ops:
  11.6 55.5 %all-gather.11.cloned.1.call-done = bf16[8192,256]{1,0:T(8,128)(2,1)} async-done(((bf16[2048,256]{1,0:T(8,128)(2,1)}), bf16[8192,256]{1,0:T(8,128)(2,1)}) %all-gather.11.cloned.1.call-update) | async-done | bytes 4194320 | tf_op jit(solution)/shard_map/all_gather | solution.py:239
  76.0 73.5 %reduce-scatter.11.cloned.1.call-done = f32[2048,128]{1,0:T(8,128)} async-done(((f32[8192,128]{1,0:T(8,128)}), f32[2048,128]{1,0:T(8,128)}) %reduce-scatter.11.cloned.1.call-update) | async-done | bytes 1048592 | tf_op jit(solution)/shard_map/reduce_scatter | solution.py:246
  151.1 40.8 %psum.133 = f32[2,512]{1,0:T(2,128)S(1)} all-reduce(f32[2,512]{1,0:T(2,128)S(1)} %pad_maximum_fusion.10), channel_id=1, replica_groups=mesh['batch'=2,'inner'=4,'outer'=4] {'batch','inner','outer'}, use_global_device_ids=true, to_apply=%region_3.0 | all-reduce | flops 1024 | bytes 8192 | tf_op jit(solution)/shard_map/psum | solution.py:120
  196.9 33.2 %all-gather.13.cloned.1.call-done = bf16[4,16,32,512]{3,2,1,0:T(8,128)(2,1)} async-done(((bf16[4,16,32,128]{3,2,1,0:T(8,128)(2,1)}), bf16[4,16,32,512]{3,2,1,0:T(8,128)(2,1)}) %all-gather.13.cloned.1.call-update) | async-done | bytes 2097168 | tf_op jit(solution)/shard_map/all_gather | solution.py:281
  330.2 42.7 %psum.134 = f32[2,512]{1,0:T(2,128)S(1)} all-reduce(f32[2,512]{1,0:T(2,128)S(1)} %pad_maximum_fusion.11), channel_id=1, replica_groups=mesh['batch'=2,'inner'=4,'outer'=4] {'batch','inner','outer'}, use_global_device_ids=true, to_apply=%region_7.8 | all-reduce | flops 1024 | bytes 8192 | tf_op jit(solution)/shard_map/psum | solution.py:120
  415.8 25.7 %reduce.11 = bf16[16,131072]{1,0:T(8,128)(2,1)} reduce(bf16[16,1,131072]{2,1,0:T(2,128)(2,1)} %all-gather.27.cloned.1.call-done, bf16[]{:T(256)} %constant.192), dimensions={1}, to_apply=%all-gather.reduce_sub_computation | reduce | bytes 8388610 | tf_op jit(solution)/shard_map/all_gather | solution.py:226
  468.3 20.3 all-to-all-done.1
  490.5 37.6 %psum.135 = f32[4,2048]{1,0:T(4,128)S(1)} all-reduce(f32[4,2048]{1,0:T(4,128)S(1)} %pad_maximum_fusion.2), channel_id=1, replica_groups=mesh['batch'=2,'inner'=4,'outer'=4] {'batch','inner','outer'}, use_global_device_ids=true, to_apply=%region_13.14 | all-reduce | flops 8192 | bytes 65536 | tf_op jit(solution)/shard_map/psum | solution.py:120
  532.3 36.8 %all-gather.17.cloned.1.call-done = bf16[2048,512]{1,0:T(8,128)(2,1)} async-done(((bf16[512,512]{1,0:T(8,128)(2,1)}), bf16[2048,512]{1,0:T(8,128)(2,1)}) %all-gather.17.cloned.1.call-update) | async-done | bytes 2097168 | tf_op jit(solution)/shard_map/all_gather | solution.py:239
  575.1 24.6 %reduce-scatter.15.cloned.1.call-done = f32[512,128]{1,0:T(8,128)} async-done(((f32[2048,128]{1,0:T(8,128)}), f32[512,128]{1,0:T(8,128)}) %reduce-scatter.15.cloned.1.call-update) | async-done | bytes 262160 | tf_op jit(solution)/shard_map/reduce_scatter | solution.py:246
  600.9 40.3 %psum.136 = f32[2,512]{1,0:T(2,128)S(1)} all-reduce(f32[2,512]{1,0:T(2,128)S(1)} %pad_maximum_fusion.12), channel_id=1, replica_groups=mesh['batch'=2,'inner'=4,'outer'=4] {'batch','inner','outer'}, use_global_device_ids=true, to_apply=%region_17.18 | all-reduce | flops 1024 | bytes 8192 | tf_op jit(solution)/shard_map/psum | solution.py:120
  661.0 39.5 %psum.137 = f32[2,512]{1,0:T(2,128)S(1)} all-reduce(f32[2,512]{1,0:T(2,128)S(1)} %pad_maximum_fusion.13), channel_id=1, replica_groups=mesh['batch'=2,'inner'=4,'outer'=4] {'batch','inner','outer'}, use_global_device_ids=true, to_apply=%region_20.21 | all-reduce | flops 1024 | bytes 8192 | tf_op jit(solution)/shard_map/psum | solution.py:120
  722.2 51.2 %reduce-scatter.17.cloned.1.call-done = f32[512,512]{1,0:T(8,128)} async-done(((f32[2048,512]{1,0:T(8,128)}), f32[512,512]{1,0:T(8,128)}) %reduce-scatter.17.cloned.1.call-update) | async-done | bytes 1048592 | tf_op jit(solution)/shard_map/reduce_scatter | solution.py:263
  774.9 39.4 %psum.138 = f32[2,2048]{1,0:T(2,128)S(1)} all-reduce(f32[2,2048]{1,0:T(2,128)S(1)} %pad_maximum_fusion.6), channel_id=1, replica_groups=mesh['batch'=2,'inner'=4,'outer'=4] {'batch','inner','outer'}, use_global_device_ids=true, to_apply=%region_24.25 | all-reduce | flops 4096 | bytes 32768 | tf_op jit(solution)/shard_map/psum | solution.py:120
  819.9 41.2 %psum.139 = f32[2,2048]{1,0:T(2,128)S(1)} all-reduce(f32[2,2048]{1,0:T(2,128)S(1)} %pad_maximum_fusion.7), channel_id=1, replica_groups=mesh['batch'=2,'inner'=4,'outer'=4] {'batch','inner','outer'}, use_global_device_ids=true, to_apply=%region_27.28 | all-reduce | flops 4096 | bytes 32768 | tf_op jit(solution)/shard_map/psum | solution.py:120
  863.9 35.2 %all-gather.21.cloned.1.call-done = bf16[2048,512]{1,0:T(8,128)(2,1)} async-done(((bf16[512,512]{1,0:T(8,128)(2,1)}), bf16[2048,512]{1,0:T(8,128)(2,1)}) %all-gather.21.cloned.1.call-update) | async-done | bytes 2097168 | tf_op jit(solution)/shard_map/all_gather | solution.py:239
  902.5 27.2 %reduce-scatter.19.cloned.1.call-done = f32[512,128]{1,0:T(8,128)} async-done(((f32[2048,128]{1,0:T(8,128)}), f32[512,128]{1,0:T(8,128)}) %reduce-scatter.19.cloned.1.call-update) | async-done | bytes 262160 | tf_op jit(solution)/shard_map/reduce_scatter | solution.py:246
  931.8 38.9 %psum.140 = f32[2,512]{1,0:T(2,128)S(1)} all-reduce(f32[2,512]{1,0:T(2,128)S(1)} %pad_maximum_fusion.14), channel_id=1, replica_groups=mesh['batch'=2,'inner'=4,'outer'=4] {'batch','inner','outer'}, use_global_device_ids=true, to_apply=%region_31.32 | all-reduce | flops 1024 | bytes 8192 | tf_op jit(solution)/shard_map/psum | solution.py:120
  979.6 27.6 %reduce-scatter.21.cloned.1.call-done = f32[4,8,16,128]{3,2,1,0:T(8,128)} async-done(((f32[4,8,16,512]{3,2,1,0:T(8,128)}), f32[4,8,16,128]{3,2,1,0:T(8,128)}) %reduce-scatter.21.cloned.1.call-update) | async-done | bytes 262160 | tf_op jit(solution)/shard_map/reduce_scatter | solution.py:294
  1009.9 39.5 %psum.141 = f32[2,512]{1,0:T(2,128)} all-reduce(f32[2,512]{1,0:T(2,128)} %pad_maximum_fusion.15), channel_id=1, replica_groups=mesh['batch'=2,'inner'=4,'outer'=4] {'batch','inner','outer'}, use_global_device_ids=true, to_apply=%region_35.36 | all-reduce | flops 1024 | bytes 8192 | tf_op jit(solution)/shard_map/psum | solution.py:120
  1070.9 54.3 %reduce-scatter.23.cloned.1.call-done = f32[512,512]{1,0:T(8,128)} async-done(((f32[2048,512]{1,0:T(8,128)}), f32[512,512]{1,0:T(8,128)}) %reduce-scatter.23.cloned.1.call-update) | async-done | bytes 1048592 | tf_op jit(solution)/shard_map/reduce_scatter | solution.py:263
  1129.3 39.5 %psum.142 = f32[4,2048]{1,0:T(4,128)S(1)} all-reduce(f32[4,2048]{1,0:T(4,128)S(1)} %pad_maximum_fusion.3), channel_id=1, replica_groups=mesh['batch'=2,'inner'=4,'outer'=4] {'batch','inner','outer'}, use_global_device_ids=true, to_apply=%region_40.41 | all-reduce | flops 8192 | bytes 65536 | tf_op jit(solution)/shard_map/psum | solution.py:120
  1172.7 35.8 %all-gather.23.cloned.1.call-done = bf16[2048,512]{1,0:T(8,128)(2,1)} async-done(((bf16[512,512]{1,0:T(8,128)(2,1)}), bf16[2048,512]{1,0:T(8,128)(2,1)}) %all-gather.23.cloned.1.call-update) | async-done | bytes 2097168 | tf_op jit(solution)/shard_map/all_gather | solution.py:239
  1211.9 27.2 %reduce-scatter.25.cloned.1.call-done = f32[512,128]{1,0:T(8,128)} async-done(((f32[2048,128]{1,0:T(8,128)}), f32[512,128]{1,0:T(8,128)}) %reduce-scatter.25.cloned.1.call-update) | async-done | bytes 262160 | tf_op jit(solution)/shard_map/reduce_scatter | solution.py:246
  1240.5 38.9 %psum.143 = f32[2,512]{1,0:T(2,128)S(1)} all-reduce(f32[2,512]{1,0:T(2,128)S(1)} %pad_maximum_fusion.16), channel_id=1, replica_groups=mesh['batch'=2,'inner'=4,'outer'=4] {'batch','inner','outer'}, use_global_device_ids=true, to_apply=%region_44.45 | all-reduce | flops 1024 | bytes 8192 | tf_op jit(solution)/shard_map/psum | solution.py:120
  1394.5 18.2 pad.78
  1433.3 18.2 pad.80
  1528.1 42.2 %psum.144 = f32[2,512]{1,0:T(2,128)S(1)} all-reduce(f32[2,512]{1,0:T(2,128)S(1)} %pad_maximum_fusion.17), channel_id=1, replica_groups=mesh['batch'=2,'inner'=4,'outer'=4] {'batch','inner','outer'}, use_global_device_ids=true, to_apply=%region_48.49 | all-reduce | flops 1024 | bytes 8192 | tf_op jit(solution)/shard_map/psum | solution.py:120
  1579.3 210.9 %all-reduce.30.cloned.1.call-done = f32[16,131072]{1,0:T(8,128)} async-done(((f32[16,131072]{1,0:T(8,128)}), f32[16,131072]{1,0:T(8,128)}) %all-reduce.30.cloned.1.call-update) | async-done | bytes 8388624
  1795.4 219.6 %all-reduce.32.cloned.1.call-done = (f32[3,3,512,128]{2,1,0,3:T(4,128)}, f32[3,3,512,128]{2,1,0,3:T(4,128)}) async-done(((f32[3,3,512,128]{2,1,0,3:T(4,128)}, f32[3,3,512,128]{2,1,0,3:T(4,128)}), (f32[3,3,512,128]{2,1,0,3:T(4,128)}, f32[3,3,512,128]{2,1,0,3:T(4,128)})) %all-reduce.32.cloned.1.call-update) | async-done | bytes 4718608
  2019.3 42.7 %all-gather.25.cloned.1.call-done = bf16[8192,128]{1,0:T(8,128)(2,1)} async-done(((bf16[2048,128]{1,0:T(8,128)(2,1)}), bf16[8192,128]{1,0:T(8,128)(2,1)}) %all-gather.25.cloned.1.call-update) | async-done | bytes 2097168 | tf_op jit(solution)/shard_map/all_gather | solution.py:256
  2103.7 76.0 %reduce-scatter.29.cloned.1.call-done = f32[2048,256]{1,0:T(8,128)} async-done(((f32[8192,256]{1,0:T(8,128)}), f32[2048,256]{1,0:T(8,128)}) %reduce-scatter.29.cloned.1.call-update) | async-done | bytes 2097168 | tf_op jit(solution)/shard_map/reduce_scatter | solution.py:263
  (588 shorter events, 581.8 us)
Async XLA Ops:
  7.2 711.5 %copy-start = (bf16[128,512]{1,0:T(8,128)(2,1)S(1)}, bf16[128,512]{1,0:T(8,128)(2,1)}, u32[]{:S(2)}) copy-start(bf16[128,512]{1,0:T(8,128)(2,1)} %param.22) | copy-start | bytes 393220
  7.2 59.9 %all-gather.11.cloned.1.call-start = ((), (), s32[]{:S(2)}) async-start(), calls=%async_computation.14 | async-start | bytes 5242880 | tf_op jit(solution)/shard_map/all_gather | solution.py:239
  11.5 137.9 %reduce-scatter.11.cloned.1.call-start = ((), (), s32[]{:S(2)}) async-start(), calls=%async_computation.15 | async-start | bytes 5242880 | tf_op jit(solution)/shard_map/reduce_scatter | solution.py:246
  72.5 123.1 %copy-start.45 = (bf16[256,512]{1,0:T(8,128)(2,1)S(1)}, bf16[256,512]{1,0:T(8,128)(2,1)}, u32[]{:S(2)}) copy-start(bf16[256,512]{1,0:T(8,128)(2,1)} %param.19) | copy-start | bytes 786436
  72.5 157.6 %all-gather.13.cloned.1.call-start = ((), (), s32[]{:S(2)}) async-start(), calls=%async_computation.16 | async-start | bytes 2621440 | tf_op jit(solution)/shard_map/all_gather | solution.py:281
  75.4 121.2 %copy-start.105 = (f32[128]{0:T(128)}, f32[128]{0:T(128)S(1)}, u32[]{:S(2)}) copy-start(f32[128]{0:T(128)S(1)} %fusion.134) | copy-start | bytes 1540
  195.0 128.7 %all-gather.15.cloned.1.call-start = ((), (), s32[]{:S(2)}) async-start(), calls=%async_computation.17 | async-start | bytes 1474560 | tf_op jit(solution)/shard_map/all_gather | solution.py:233
  195.6 220.2 %all-gather.27.cloned.1.call-start = ((), (), s32[]{:S(2)}) async-start(), calls=%async_computation.32 | async-start | bytes 8912896 | tf_op jit(solution)/shard_map/all_gather | solution.py:226
  196.6 292.3 %reduce-scatter.13.cloned.1.call-start = ((), (), s32[]{:S(2)}) async-start(), calls=%async_computation.18 | async-start | bytes 5242880 | tf_op jit(solution)/shard_map/reduce_scatter | solution.py:263
  196.7 176.8 %copy-start.107 = (f32[128]{0:T(128)}, f32[128]{0:T(128)S(1)}, u32[]{:S(2)}) copy-start(f32[128]{0:T(128)S(1)} %fusion.138) | copy-start | bytes 1540
  462.9 25.7 %all-to-all-start.1 = ((f32[128,4,512]{2,0,1:T(8,128)}), f32[128,4,512]{2,0,1:T(8,128)S(1)}, u32[]{:S(2)}, u32[]{:S(2)}) async-start(f32[128,4,512]{2,0,1:T(8,128)} %fusion.211), calls=%async_computation.3 | async-start | bytes 2097152 | tf_op jit(solution)/shard_map/all_to_all | solution.py:221
  466.6 102.5 %all-gather.17.cloned.1.call-start = ((), (), s32[]{:S(2)}) async-start(), calls=%async_computation.19 | async-start | bytes 2621440 | tf_op jit(solution)/shard_map/all_gather | solution.py:239
  532.3 67.4 %reduce-scatter.15.cloned.1.call-start = ((), (), s32[]{:S(2)}) async-start(), calls=%async_computation.20 | async-start | bytes 1310720 | tf_op jit(solution)/shard_map/reduce_scatter | solution.py:246
  572.4 83.2 %all-gather.19.cloned.1.call-start = ((), (), s32[]{:S(2)}) async-start(), calls=%async_computation.21 | async-start | bytes 1474560 | tf_op jit(solution)/shard_map/all_gather | solution.py:234
  573.1 200.2 %reduce-scatter.17.cloned.1.call-start = ((), (), s32[]{:S(2)}) async-start(), calls=%async_computation.22 | async-start | bytes 5242880 | tf_op jit(solution)/shard_map/reduce_scatter | solution.py:263
  721.3 93.1 %copy-start.55 = (f32[1,512]{1,0:T(1,128)S(1)}, f32[1,512]{1,0:T(1,128)}, u32[]{:S(2)}) copy-start(f32[1,512]{1,0:T(1,128)} %copy-done.54) | copy-start | bytes 6148
  721.3 93.1 %copy-start.70 = (f32[1,512]{1,0:T(1,128)S(1)}, f32[1,512]{1,0:T(1,128)}, u32[]{:S(2)}) copy-start(f32[1,512]{1,0:T(1,128)} %copy-done.69) | copy-start | bytes 6148
  721.4 177.7 %all-gather.21.cloned.1.call-start = ((), (), s32[]{:S(2)}) async-start(), calls=%async_computation.23 | async-start | bytes 2621440 | tf_op jit(solution)/shard_map/all_gather | solution.py:239
  863.8 65.9 %reduce-scatter.19.cloned.1.call-start = ((), (), s32[]{:S(2)}) async-start(), calls=%async_computation.24 | async-start | bytes 1310720 | tf_op jit(solution)/shard_map/reduce_scatter | solution.py:246
  902.4 104.8 %reduce-scatter.21.cloned.1.call-start = ((), (), s32[]{:S(2)}) async-start(), calls=%async_computation.25 | async-start | bytes 1310720 | tf_op jit(solution)/shard_map/reduce_scatter | solution.py:294
  979.6 145.6 %reduce-scatter.23.cloned.1.call-start = ((), (), s32[]{:S(2)}) async-start(), calls=%async_computation.26 | async-start | bytes 5242880 | tf_op jit(solution)/shard_map/reduce_scatter | solution.py:263
  1070.8 137.7 %all-gather.23.cloned.1.call-start = ((), (), s32[]{:S(2)}) async-start(), calls=%async_computation.27 | async-start | bytes 2621440 | tf_op jit(solution)/shard_map/all_gather | solution.py:239
  1172.4 106.9 %copy-start.111 = (f32[128]{0:T(128)S(1)}, f32[128]{0:T(128)}, u32[]{:S(2)}) copy-start(f32[128]{0:T(128)} %get-tuple-element.93) | copy-start | bytes 1540
  1172.5 66.7 %reduce-scatter.25.cloned.1.call-start = ((), (), s32[]{:S(2)}) async-start(), calls=%async_computation.28 | async-start | bytes 1310720 | tf_op jit(solution)/shard_map/reduce_scatter | solution.py:246
  1211.8 314.0 %reduce-scatter.27.cloned.1.call-start = ((), (), s32[]{:S(2)}) async-start(), calls=%async_computation.29 | async-start | bytes 5242880 | tf_op jit(solution)/shard_map/reduce_scatter | solution.py:294
  1473.2 17.5 all-to-all-start.2
  1476.9 313.4 %all-reduce.30.cloned.1.call-start = ((), (), s32[]{:S(2)}) async-start(), calls=%async_computation.33 | async-start | bytes 16777216
  1501.8 513.2 %all-reduce.32.cloned.1.call-start = ((), (), s32[]{:S(2)}) async-start(), calls=%async_computation.34 | async-start | bytes 12582912
  1521.7 540.3 %all-gather.25.cloned.1.call-start = ((), (), s32[]{:S(2)}) async-start(), calls=%async_computation.30 | async-start | bytes 2621440 | tf_op jit(solution)/shard_map/all_gather | solution.py:256
  1571.5 527.7 %all-reduce.34.cloned.1.call-start = ((), (), s32[]{:S(2)}) async-start(), calls=%async_computation.35 | async-start | bytes 6029312 | tf_op jit(solution)/shard_map/psum | solution.py:483
  2066.8 112.9 %reduce-scatter.29.cloned.1.call-start = ((), (), s32[]{:S(2)}) async-start(), calls=%async_computation.31 | async-start | bytes 10485760 | tf_op jit(solution)/shard_map/reduce_scatter | solution.py:263
  2079.4 18.2 all-to-all-start.3
  (108 other events, 2481.1 us)
Sparse Core Ops, SparseCore 0:
  11.6 55.3 all-gather.10
  72.6 76.7 reduce-scatter.10
  195.1 34.9 all-gather.12
  231.6 30.4 all-gather.14
  265.7 114.4 all-gather.26
  392.6 51.3 reduce-scatter.12
  532.4 36.6 all-gather.16
  572.5 27.1 reduce-scatter.14
  601.4 30.0 all-gather.18
  721.5 51.8 reduce-scatter.16
  864.0 35.1 all-gather.20
  902.6 27.1 reduce-scatter.18
  979.7 27.4 reduce-scatter.20
  1070.9 54.1 reduce-scatter.22
  1172.5 35.9 all-gather.22
  1212.0 27.1 reduce-scatter.24
  1473.3 52.4 reduce-scatter.26
  1532.7 257.5 all-reduce.29
  1792.8 222.1 all-reduce.31
  2017.1 44.8 all-gather.24
  2067.0 22.0 all-reduce.33
  2092.2 87.5 reduce-scatter.28
where the time goes:
time: 2220 us; the launch traced here: 2190 us
  waiting for transfers between devices  1080 us (49%)
  blocking collectives  549 us (25%)
  local copies, waits for them, and re-layouts  341 us (15%)
  other arithmetic  105 us (5%)
  matrix products  83.8 us (4%)
    psum x12, blocking collectives, global_sums(): return lax.psum(stacked, ('batch', 'inner', 'outer'))  480 us
    unnamed x24, waiting for transfers between devices  432 us
    reduce_scatter x4, waiting for transfers between devices, channels_up(): lax.psum_scatter(partial_rows(jnp.int32(0), share * lax.axis_size('inner'...  181 us
    all_gather x4, waiting for transfers between devices, channels_down(): gathered_rows = lax.all_gather(rows_local, 'inner', axis=0, tiled=True)  163 us
    reduce_scatter x4, waiting for transfers between devices, channels_down(): lax.psum_scatter(partial_rows(jnp.int32(0), share * lax.axis_size('outer'...  153 us
    slice x10, local copies, waits for them, and re-layouts, tap_window(): padded[:, tap_row:tap_row + stride * (rows_out - 1) + 1:stride, tap_col:t...  91.1 us
    unnamed x248, local copies, waits for them, and re-layouts  83.1 us
    slice x4, local copies, waits for them, and re-layouts, taps_input(): return summed[:, 1:-1, 1:-1, :]  70.2 us
  transfers between devices with their start and end apart: 25, of which 20 were waited for; matrix products, arithmetic and copies ran while one was open for 11% of the time, Pallas kernels for 0%

commit v1 on v0

v1 whole, which is shorter than its diff:
```python
import math

import jax
import jax.numpy as jnp
from jax import lax
from jax.sharding import PartitionSpec as P

EPS = 1e-05
ROOT = math.sqrt(2.0 / math.pi)
CUBE = 0.044715
F32 = jnp.float32
BF16 = jnp.bfloat16


def mm(left, right):
    return jnp.dot(left, right, preferred_element_type=F32)


def mm_nt(left, right):
    return lax.dot_general(left, right, (((1,), (1,)), ((), ())), preferred_element_type=F32)


def mm_tn(left, right):
    return lax.dot_general(left, right, (((0,), (0,)), ((), ())), preferred_element_type=F32)


def gelu(v):
    return 0.5 * v * (1.0 + jnp.tanh(ROOT * (v + CUBE * v * v * v)))


def gelu_both(v):
    t = jnp.tanh(ROOT * (v + CUBE * v * v * v))
    half = 0.5 * (1.0 + t)
    return v * half, half + 0.5 * v * (1.0 - t * t) * (ROOT * (1.0 + 3.0 * CUBE * v * v))


def gelu_slope(v):
    return gelu_both(v)[1]


def shards(
    images,
    extents,
    first_reduce,
    first_taps,
    first_expand,
    first_shortcut,
    second_reduce,
    second_taps,
    second_expand,
    mid_gains,
    mid_shifts,
    wide_gains,
    wide_shifts,
    cotangent,
):
    nb = lax.axis_size("batch")
    ni = lax.axis_size("inner")
    no = lax.axis_size("outer")
    b = lax.axis_index("batch")
    i = lax.axis_index("inner")
    o = lax.axis_index("outer")
    c = b % 2
    img_dev, hi, wi, in_part = images.shape
    ho, wo = hi // 2, wi // 2
    out_part = cotangent.shape[3]
    m = img_dev // no
    pair = 2 * m
    cells_in, cells_out = hi * wi, ho * wo
    mid = mid_gains.shape[1]
    mid_h = mid // 2
    in_h = in_part // 2
    out_h = out_part // 2
    kin_h = no * in_h
    wide_h = no * out_h

    def core_swap(x):
        return lax.ppermute(x, "batch", [(k, k ^ 1) for k in range(nb)])

    def pick(low, high):
        return jnp.where(c == 0, low, high)

    def mine(x, axis):
        h = x.shape[axis] // 2
        return pick(lax.slice_in_dim(x, 0, h, axis=axis), lax.slice_in_dim(x, h, 2 * h, axis=axis))

    def other(x, axis):
        h = x.shape[axis] // 2
        return pick(lax.slice_in_dim(x, h, 2 * h, axis=axis), lax.slice_in_dim(x, 0, h, axis=axis))

    def swap_add(x, axis):
        return mine(x, axis) + core_swap(other(x, axis))

    def join(own, recv, axis):
        return pick(jnp.concatenate([own, recv], axis), jnp.concatenate([recv, own], axis))

    def swap_full(x, axis):
        return join(x, core_swap(x), axis)

    def over_batch(x):
        total = x
        for k in range(1, nb // 2):
            total = total + lax.ppermute(x, "batch", [(j, (j + 2 * k) % nb) for j in range(nb)])
        return total

    def sums_of(rows):
        sizes = [r.shape[0] for r in rows]
        flat = jnp.concatenate(rows).reshape(-1, 128)
        copies = jnp.broadcast_to(flat[None], (ni * no,) + flat.shape)
        got = lax.all_to_all(copies, ("inner", "outer"), split_axis=0, concat_axis=0, tiled=True)
        total = over_batch(jnp.sum(got, axis=0)).reshape(-1)
        out, start = [], 0
        for s in sizes:
            out.append(total[start : start + s])
            start += s
        return out

    def to_images(x):
        return lax.all_to_all(x, "outer", split_axis=0, concat_axis=0, tiled=True)

    def gather_blocks(shard):
        rows, cols = shard.shape
        ring = [(k, (k + 1) % no) for k in range(no)]
        piece = shard
        whole = jnp.zeros((no, rows, cols), shard.dtype)
        whole = lax.dynamic_update_slice(whole, piece[None], (o, 0, 0))
        for step in range(1, no):
            piece = lax.ppermute(piece, "outer", ring)
            whole = lax.dynamic_update_slice(whole, piece[None], ((o + no - step) % no, 0, 0))
        if ni != 4:
            return lax.all_gather(whole, "inner", axis=0, tiled=False)
        h = rows // 2
        xs = [(k, k ^ 1) for k in range(4)]
        ys = [(k, k ^ 2) for k in range(4)]
        by_x = lax.ppermute(whole, "inner", xs)
        by_y = lax.ppermute(whole, "inner", ys)
        low = lax.ppermute(by_x[:, :h], "inner", ys)
        high = lax.ppermute(by_y[:, h:], "inner", xs)
        full = jnp.zeros((4, no, rows, cols), shard.dtype)
        full = lax.dynamic_update_slice(full, whole[None], (i, 0, 0, 0))
        full = lax.dynamic_update_slice(full, by_x[None], (i ^ 1, 0, 0, 0))
        full = lax.dynamic_update_slice(full, by_y[None], (i ^ 2, 0, 0, 0))
        full = lax.dynamic_update_slice(full, low[None], (i ^ 3, 0, 0, 0))
        return lax.dynamic_update_slice(full, high[None], (i ^ 3, 0, h, 0))

    def scatter_blocks(blocks):
        rows, cols = blocks.shape[2:]
        if ni != 4:
            mine_i = lax.psum_scatter(blocks.astype(F32), "inner", scatter_dimension=0, tiled=True)[0]
        else:
            h = rows // 2
            xs = [(k, k ^ 1) for k in range(4)]
            ys = [(k, k ^ 2) for k in range(4)]

            def block(k):
                return lax.dynamic_index_in_dim(blocks, k, 0, keepdims=False)

            far = block(i ^ 3)
            low = lax.ppermute(far[:, :h], "inner", xs)
            high = lax.ppermute(far[:, h:], "inner", ys)
            for_x, for_y = block(i ^ 1), block(i ^ 2)
            for_x = jnp.concatenate(
                [for_x[:, :h], (for_x[:, h:].astype(F32) + high.astype(F32)).astype(BF16)], 1
            )
            for_y = jnp.concatenate(
                [(for_y[:, :h].astype(F32) + low.astype(F32)).astype(BF16), for_y[:, h:]], 1
            )
            by_x = lax.ppermute(for_x, "inner", xs)
            by_y = lax.ppermute(for_y, "inner", ys)
            mine_i = block(i).astype(F32) + by_x.astype(F32) + by_y.astype(F32)
        parts = lax.all_to_all(
            mine_i.astype(BF16), "outer", split_axis=0, concat_axis=0, tiled=True
        )
        return over_batch(jnp.sum(parts.astype(F32), axis=0))

    def masks():
        first = ((b - c) * ni + i) * img_dev + o * m
        lows = lax.dynamic_slice_in_dim(extents, first, m, 0)
        highs = lax.dynamic_slice_in_dim(extents, first + ni * img_dev, m, 0)
        ext = jnp.concatenate([lows, highs], 0)
        return ext[:, 0], ext[:, 1]

    heights, widths = masks()
    out_cell = jnp.arange(cells_out, dtype=jnp.int32)
    out_row, out_col = out_cell // wo, out_cell % wo
    valid_out = (
        ((out_row[None] < heights[:, None]) & (out_col[None] < widths[:, None]))
        .astype(F32)
        .reshape(pair * cells_out, 1)
    )
    in_cell = jnp.arange(cells_in, dtype=jnp.int32)
    phase = in_cell // cells_out
    ph_row = 2 * (in_cell % cells_out // wo) + phase // 2
    ph_col = 2 * (in_cell % wo) + phase % 2
    valid_ph = (ph_row[None] < 2 * heights[:, None]) & (ph_col[None] < 2 * widths[:, None])
    valid_in = valid_ph.astype(F32).reshape(pair * cells_in, 1)
    source = ph_row * wi + ph_col
    order = ((source[None, :, None] == in_cell[None, None, :]) & valid_ph[:, :, None]).astype(BF16)
    count_out = jnp.sum(extents[:, 0] * extents[:, 1]).astype(F32)
    count_in = 4.0 * count_out

    def shift_matrix(dr, dc):
        rr, cc = out_row + dr, out_col + dc
        inside = (rr >= 0) & (rr < ho) & (cc >= 0) & (cc < wo)
        return ((rr * wo + cc)[:, None] == out_cell[None, :]) & inside[:, None]

    def selected(matrix, x):
        return jnp.einsum("ps,msk->mpk", matrix, x, preferred_element_type=F32).astype(BF16)

    got = to_images(images.reshape(img_dev, cells_in, in_part))
    shard_r1 = mine(first_reduce, 0)

    def taps_shard(w):
        k_half = mine(w, 2).reshape(9, mid_h, -1)
        return k_half.transpose(2, 0, 1).reshape(-1, 9 * mid_h)

    full_r1 = gather_blocks(shard_r1)
    full_t1 = gather_blocks(taps_shard(first_taps))
    full_es = gather_blocks(jnp.concatenate([mine(first_expand, 1), mine(first_shortcut, 1)], 0))
    rows_e = first_expand.shape[0]
    full_e1, full_s = full_es[:, :, :rows_e], full_es[:, :, rows_e:]
    full_r2 = gather_blocks(mine(second_reduce, 0))
    full_t2 = gather_blocks(taps_shard(second_taps))
    full_e2 = gather_blocks(mine(second_expand, 1))

    def outer_rows(full):
        r, k = full.shape[2:]
        return full.transpose(1, 2, 0, 3).reshape(no * r, ni * k)

    def inner_rows(full):
        r, k = full.shape[2:]
        return full.transpose(0, 2, 1, 3).reshape(ni * r, no * k)

    def outer_blocks(whole, r, k):
        return whole.reshape(no, r, ni, k).transpose(2, 0, 1, 3)

    def inner_blocks(whole, r, k):
        return whole.reshape(ni, r, no, k).transpose(0, 2, 1, 3)

    w_r1 = outer_rows(full_r1)
    w_t1 = full_t1.reshape(mid, 9 * mid_h)
    w_e1 = inner_rows(full_e1)
    w_s = outer_rows(full_s)
    w_r2 = outer_rows(full_r2)
    w_t2 = full_t2.reshape(mid, 9 * mid_h)
    w_e2 = inner_rows(full_e2)

    def both_images(x, lanes):
        own = mine(x, 3)
        recv = core_swap(other(x, 3))
        low, high = pick(own, recv), pick(recv, own)
        stacked = jnp.concatenate([low, high], 1)
        return stacked.transpose(1, 2, 0, 3).reshape(pair, x.shape[2], no * lanes)

    def own_images(x, lanes):
        low, high = x[:m], x[m:]
        own = pick(low, high)
        recv = core_swap(pick(high, low))
        cells = x.shape[1]
        own = own.reshape(m, cells, no, lanes)
        recv = recv.reshape(m, cells, no, lanes)
        return join(own, recv, 3).transpose(2, 0, 1, 3)

    raw = both_images(got.reshape(no, m, cells_in, in_part), in_h)
    masked = jnp.einsum("mps,msk->mpk", order, raw, preferred_element_type=F32).astype(BF16)
    masked_rows = masked.reshape(pair * cells_in, kin_h)
    strided_h = masked[:, :cells_out].reshape(pair * cells_out, kin_h)
    recv = core_swap(strided_h)
    s_low, s_high = pick(strided_h, recv), pick(recv, strided_h)
    strided = jnp.stack(
        [s_low.reshape(-1, no, in_h), s_high.reshape(-1, no, in_h)], 2
    ).reshape(pair * cells_out, no * in_part)

    def mid_half(vector):
        return mine(vector, 0)

    def wide_half(vector):
        return mine(vector.reshape(no, out_part), 1).reshape(wide_h)

    def stats(total, squares, count):
        mean = total / count
        return mean, lax.rsqrt(squares / count - mean * mean + EPS)

    def col_sums(z, valid):
        zv = z * valid
        return [jnp.sum(zv, 0), jnp.sum(zv * z, 0)]

    def xhat_of(z, st):
        return (z - st[0]) * st[1]

    gm = [mid_half(mid_gains[k]) for k in range(4)]
    sm = [mid_half(mid_shifts[k]) for k in range(4)]
    gw = [wide_half(wide_gains[k]) for k in range(3)]
    sw = [wide_half(wide_shifts[k]) for k in range(3)]

    z_one = swap_add(mm(masked_rows, w_r1), 1)
    t, q = sums_of(col_sums(z_one, valid_in))
    st_one = stats(t, q, count_in)
    act_one = (gelu(xhat_of(z_one, st_one) * gm[0] + sm[0]) * valid_in).astype(BF16)

    planes = act_one.reshape(pair, 4, cells_out, mid_h)
    shifts_down = {
        (dr, dc): shift_matrix(dr, dc).astype(BF16) for dr in (-1, 0, 1) for dc in (-1, 0, 1)
    }
    windows = []
    for p in range(3):
        for r in range(3):
            plane = planes[:, 2 * int(p != 1) + int(r != 1)]
            key = (-int(p == 0), -int(r == 0))
            windows.append(plane if key == (0, 0) else selected(shifts_down[key], plane))
    win_one = jnp.concatenate(windows, -1).reshape(pair * cells_out, 9 * mid_h)
    z_two = swap_add(mm_nt(win_one, w_t1), 1)
    t, q = sums_of(col_sums(z_two, valid_out))
    st_two = stats(t, q, count_out)
    act_two_h = (gelu(xhat_of(z_two, st_two) * gm[1] + sm[1]) * valid_out).astype(BF16)
    act_two = swap_full(act_two_h, 1)
    z_three = mm(act_two, w_e1)
    z_short = mm(strided, w_s)
    t, q, ts, qs = sums_of(col_sums(z_three, valid_out) + col_sums(z_short, valid_out))
    st_three, st_short = stats(t, q, count_out), stats(ts, qs, count_out)
    joined_one = (xhat_of(z_three, st_three) * gw[0] + sw[0]) + (
        xhat_of(z_short, st_short) * gw[1] + sw[1]
    )
    hidden = gelu(joined_one) * valid_out
    hidden_low = hidden.astype(BF16)
    z_four = swap_add(mm(hidden_low, w_r2), 1)
    t, q = sums_of(col_sums(z_four, valid_out))
    st_four = stats(t, q, count_out)
    act_four = (gelu(xhat_of(z_four, st_four) * gm[2] + sm[2]) * valid_out).astype(BF16)
    plane = act_four.reshape(pair, cells_out, mid_h)
    windows = []
    for p in range(3):
        for r in range(3):
            key = (p - 1, r - 1)
            windows.append(plane if key == (0, 0) else selected(shifts_down[key], plane))
    win_two = jnp.concatenate(windows, -1).reshape(pair * cells_out, 9 * mid_h)
    z_five = swap_add(mm_nt(win_two, w_t2), 1)
    t, q = sums_of(col_sums(z_five, valid_out))
    st_five = stats(t, q, count_out)
    act_five_h = (gelu(xhat_of(z_five, st_five) * gm[3] + sm[3]) * valid_out).astype(BF16)
    act_five = swap_full(act_five_h, 1)
    z_six = mm(act_five, w_e2)
    t, q = sums_of(col_sums(z_six, valid_out))
    st_six = stats(t, q, count_out)
    xhat_six = xhat_of(z_six, st_six)
    joined_two = xhat_six * gw[2] + sw[2] + hidden

    cot = both_images(
        to_images(cotangent.reshape(img_dev, cells_out, out_part)).reshape(
            no, m, cells_out, out_part
        ),
        out_h,
    ).reshape(pair * cells_out, wide_h)
    value, slope = gelu_both(joined_two)
    out_pair = (value * valid_out).astype(BF16).reshape(pair, cells_out, wide_h)
    block_output = to_images(
        own_images(out_pair, out_h).reshape(img_dev, cells_out, out_part)
    ).reshape(img_dev, ho, wo, out_part)
    dy_six = cot.astype(F32) * valid_out * slope

    def back(dy, xhat, gain, st, valid, shift_sum, gain_sum, count):
        return (gain * st[1] * (dy - valid * ((shift_sum + xhat * gain_sum) / count))).astype(BF16)

    def dy_sums(dy, *xhats):
        return [jnp.sum(dy, 0)] + [jnp.sum(dy * x, 0) for x in xhats]

    def to_bf16(x):
        return x.astype(BF16)

    s6, g6 = sums_of(dy_sums(dy_six, xhat_six))
    dz_six = back(dy_six, xhat_six, gw[2], st_six, valid_out, s6, g6, count_out)
    grad_e2 = scatter_blocks(
        inner_blocks(to_bf16(mm_tn(act_five, dz_six)), second_expand.shape[0], out_h)
    )
    da_five = swap_add(mm_nt(dz_six, w_e2), 1)

    xhat_five = xhat_of(z_five, st_five)
    dy_five = da_five * valid_out * gelu_slope(xhat_five * gm[3] + sm[3])
    s5, g5 = sums_of(dy_sums(dy_five, xhat_five))
    dz_five = swap_full(
        back(dy_five, xhat_five, gm[3], st_five, valid_out, s5, g5, count_out), 1
    )
    grad_t2 = scatter_blocks(
        to_bf16(mm_tn(dz_five, win_two)).reshape(ni, no, mid // (ni * no), 9 * mid_h)
    )
    dz_cells = dz_five.reshape(pair, cells_out, mid)
    da_four = 0.0
    for p in range(3):
        for r in range(3):
            key = (1 - p, 1 - r)
            moved = dz_cells if key == (0, 0) else selected(shifts_down[key], dz_cells)
            tap = 3 * p + r
            da_four = da_four + mm(
                moved.reshape(pair * cells_out, mid), w_t2[:, tap * mid_h : (tap + 1) * mid_h]
            )
    xhat_four = xhat_of(z_four, st_four)
    dy_four = da_four * valid_out * gelu_slope(xhat_four * gm[2] + sm[2])
    s4, g4 = sums_of(dy_sums(dy_four, xhat_four))
    dz_four = swap_full(
        back(dy_four, xhat_four, gm[2], st_four, valid_out, s4, g4, count_out), 1
    )
    grad_r2 = scatter_blocks(
        outer_blocks(to_bf16(mm_tn(hidden_low, dz_four)), out_h, second_reduce.shape[1])
    )
    grad_hidden = dy_six + mm_nt(dz_four, w_r2)
    dy_joined = grad_hidden * valid_out * gelu_slope(joined_one)
    xhat_three, xhat_short = xhat_of(z_three, st_three), xhat_of(z_short, st_short)
    s3, g3, gs = sums_of(dy_sums(dy_joined, xhat_three, xhat_short))
    dz_three = back(dy_joined, xhat_three, gw[0], st_three, valid_out, s3, g3, count_out)
    dz_short = back(dy_joined, xhat_short, gw[1], st_short, valid_out, s3, gs, count_out)
    grad_es = scatter_blocks(
        jnp.concatenate(
            [
                inner_blocks(to_bf16(mm_tn(act_two, dz_three)), rows_e, out_h),
                outer_blocks(to_bf16(mm_tn(strided, dz_short)), in_part, out_h),
            ],
            2,
        )
    )
    da_two = swap_add(mm_nt(dz_three, w_e1), 1)
    d_short = mm_nt(dz_short, w_s).reshape(pair * cells_out, no, in_part)
    d_short = swap_add(d_short, 2).reshape(pair, cells_out, kin_h)

    xhat_two = xhat_of(z_two, st_two)
    dy_two = da_two * valid_out * gelu_slope(xhat_two * gm[1] + sm[1])
    s2, g2 = sums_of(dy_sums(dy_two, xhat_two))
    dz_two = swap_full(back(dy_two, xhat_two, gm[1], st_two, valid_out, s2, g2, count_out), 1)
    grad_t1 = scatter_blocks(
        to_bf16(mm_tn(dz_two, win_one)).reshape(ni, no, mid // (ni * no), 9 * mid_h)
    )
    dz_cells = dz_two.reshape(pair, cells_out, mid)
    moved = {}
    for dr in (0, 1):
        for dc in (0, 1):
            y = dz_cells if (dr, dc) == (0, 0) else selected(shifts_down[(dr, dc)], dz_cells)
            moved[(dr, dc)] = y.reshape(pair * cells_out, mid)
    plane_grads = []
    for pr in range(2):
        for pc in range(2):
            total = 0.0
            for p in (1,) if pr == 0 else (0, 2):
                for r in (1,) if pc == 0 else (0, 2):
                    tap = 3 * p + r
                    total = total + mm(
                        moved[(int(p == 0), int(r == 0))],
                        w_t1[:, tap * mid_h : (tap + 1) * mid_h],
                    )
            plane_grads.append(total.reshape(pair, cells_out, mid_h))
    da_one = jnp.concatenate(plane_grads, 1).reshape(pair * cells_in, mid_h)
    xhat_one = xhat_of(z_one, st_one)
    dy_one = da_one * valid_in * gelu_slope(xhat_one * gm[0] + sm[0])
    s1, g1 = sums_of(dy_sums(dy_one, xhat_one))
    dz_one = swap_full(back(dy_one, xhat_one, gm[0], st_one, valid_in, s1, g1, count_in), 1)
    grad_r1 = scatter_blocks(
        outer_blocks(to_bf16(mm_tn(masked_rows, dz_one)), in_h, first_reduce.shape[1])
    )
    d_in = mm_nt(dz_one, w_r1).reshape(pair, cells_in, kin_h)
    d_in = jnp.concatenate([d_in[:, :cells_out] + d_short, d_in[:, cells_out:]], 1)
    d_raw = jnp.einsum(
        "mps,mpk->msk", order, d_in.astype(BF16), preferred_element_type=F32
    ).astype(BF16)
    grad_images = (
        to_images(own_images(d_raw, in_h).reshape(img_dev, cells_in, in_part))
        .astype(F32)
        .reshape(images.shape)
    )

    def taps_out(half):
        rows = half.reshape(-1, 9, mid_h).transpose(1, 0, 2)
        both = swap_full(rows, 2)
        return both.transpose(0, 2, 1).reshape(first_taps.shape)

    grad_e1_s = swap_full(grad_es, 1)
    mids = jnp.concatenate([g1, g2, g4, g5, s1, s2, s4, s5]).reshape(8, mid_h)
    mids = swap_full(mids, 1)
    wides = jnp.concatenate([g3, gs, g6, s3, s6]).reshape(5, no, out_h)
    wides = swap_full(wides, 2).reshape(5, no * out_part)
    return (
        block_output,
        grad_images,
        swap_full(grad_r1, 0),
        taps_out(grad_t1),
        grad_e1_s[:rows_e],
        grad_e1_s[rows_e:],
        swap_full(grad_r2, 0),
        taps_out(grad_t2),
        swap_full(grad_e2, 1),
        mids[:4],
        mids[4:],
        wides[:3],
        jnp.stack([wides[3], wides[3], wides[4]]),
    )


def solution(mesh):
    wide = P(("batch", "inner"), None, None, "outer")
    down = P("outer", "inner")
    up = P("inner", "outer")
    taps = P(None, None, None, ("inner", "outer"))
    whole = P()
    return jax.shard_map(
        shards,
        mesh=mesh,
        in_specs=(wide, whole, down, taps, up, down, down, taps, up)
        + (whole, whole, whole, whole, wide),
        out_specs=(wide, wide, down, taps, up, down, down, taps, up, whole, whole, whole, whole),
        check_vma=False,
    )
```

time: 2220 us -> 893 us (0.40)
  waiting for transfers between devices: 1080 us -> 135 us
  blocking collectives: 549 us -> 0 us
  starting transfers between devices: 12.7 us -> 189 us
  local copies, waits for them, and re-layouts: 341 us -> 377 us
    psum x12 -> x0, blocking collectives: 480 us -> none  [global_sums(): return lax.psum(stacked, ('batch', 'inner', 'outer'))]
    unnamed x24 -> x0, waiting for transfers between devices: 432 us -> none
    reduce_scatter x10 -> x0, waiting for transfers between devices: 366 us -> none  [the longest x4 181 us: channels_up(): lax.psum_scatter(partial_rows(jnp.int32(0), share * lax.axis_size('inner'...]
    dynamic_update_slice x27 -> x51, local copies, waits for them, and re-layouts: 0.35 us -> 243 us  [the longest x6 54.6 us: gather_blocks(): full = lax.dynamic_update_slice(full, by_y[None], (i ^ 2, 0, 0, 0))]
    all_gather x9 -> x0, waiting for transfers between devices: 239 us -> none  [the longest x4 163 us: channels_down(): gathered_rows = lax.all_gather(rows_local, 'inner', axis=0, tiled=True)]
    slice x31 -> x40, local copies, waits for them, and re-layouts: 177 us -> 30.1 us  [the longest x6 6.87 us: gather_blocks(): high = lax.ppermute(by_y[:, h:], 'inner', xs)]
    ppermute x0 -> x92, starting transfers between devices: none -> 92.3 us  [the longest x18 34.2 us: gather_blocks(): piece = lax.ppermute(piece, 'outer', ring)]
    all_to_all x3 -> x22, starting transfers between devices: 10.8 us -> 96.3 us  [the longest x12 54.4 us: sums_of(): lax.all_to_all(copies, ('inner', 'outer'), split_axis=0, concat_axis=0, t...]
  transfers between devices with their start and end apart: 25 -> 114, of which waited for: 20 -> 31; matrix products, arithmetic and copies ran while one was open for 11% -> 59% of each run, Pallas kernels for 0% -> 0%
where the time goes in v1:
time: 893 us; the launch traced here: 877 us
  local copies, waits for them, and re-layouts  377 us (42%)
  starting transfers between devices  189 us (21%)
  waiting for transfers between devices  135 us (15%)
  other arithmetic  102 us (11%)
  matrix products  68 us (8%)
    dynamic_update_slice x6, local copies, waits for them, and re-layouts, gather_blocks(): full = lax.dynamic_update_slice(full, by_y[None], (i ^ 2, 0, 0, 0))  54.6 us
    all_to_all x12, starting transfers between devices, sums_of(): lax.all_to_all(copies, ('inner', 'outer'), split_axis=0, concat_axis=0, t...  54.4 us
    dynamic_update_slice x6, local copies, waits for them, and re-layouts, gather_blocks(): full = lax.dynamic_update_slice(full, by_x[None], (i ^ 1, 0, 0, 0))  54.1 us
    dynamic_update_slice x6, local copies, waits for them, and re-layouts, gather_blocks(): full = lax.dynamic_update_slice(full, whole[None], (i, 0, 0, 0))  50.9 us
    all_to_all x12, waiting for transfers between devices, sums_of(): lax.all_to_all(copies, ('inner', 'outer'), split_axis=0, concat_axis=0, t...  44.6 us
    ppermute x18, starting transfers between devices, gather_blocks(): piece = lax.ppermute(piece, 'outer', ring)  34.2 us
    dot_general x23, matrix products, mm(): return jnp.dot(left, right, preferred_element_type=F32)  32.3 us
    dynamic_update_slice x6, local copies, waits for them, and re-layouts, gather_blocks(): full = lax.dynamic_update_slice(full, low[None], (i ^ 3, 0, 0, 0))  31.7 us
  transfers between devices with their start and end apart: 114, of which 31 were waited for; matrix products, arithmetic and copies ran while one was open for 59% of the time, Pallas kernels for 0%

profile of v1, /device:TPU:0, one launch (start us, length us, event | category | flops | bytes accessed | tf_op | source)
XLA Modules:
  0.0 876.5 jit_solution(11019069288946217361)
XLA Ops:
  33.7 7.0 collective-permute-done.43
  52.9 5.9 dynamic_update_slice.166
  73.5 11.7 %dynamic_update_slice.193 = bf16[4,4,256,128]{3,0,2,1:T(4,128)(2,1)S(1)} dynamic-update-slice(bf16[4,4,256,128]{3,0,2,1:T(4,128)(2,1)S(1)} %broadcast_in_dim.177, bf16[1,4,256,128]{3,0,2,1:T(2,128)(2,1)S(1)} %copy.250, s32[]{:T(128)S(6)} %select_n.886, s32[]{:T(128)} %constant.298.clone.1, s32[]{:T(128)} %constant.298.clone.1, s32[]{:T(128)} %constant.298.clone.1) | dynamic-update-slice | bytes 524292 | tf_op jit(solution)/shard_map/dynamic_update_slice | solution.py:140
  93.2 13.8 %collective-permute-start.19 = (bf16[384,256]{1,0:T(8,128)(2,1)}, bf16[384,256]{1,0:T(8,128)(2,1)}, u32[]{:S(2)}, u32[]{:S(2)}) collective-permute-start(bf16[384,256]{1,0:T(8,128)(2,1)} %collective-permute-done.18), channel_id=1, source_target_pairs={{0,1},{1,2},{2,3},{3,0},{4,5},{5,6},{6,7},{7,4},{8,9},{9,10},{10,1... | collective-permute-start | bytes 589832 | tf_op jit(solution)/shard_map/ppermute | solution.py:128
  108.1 5.9 dynamic_update_slice.167
  113.9 5.9 dynamic_update_slice.168
  139.0 4.6 collective-permute-done.11
  161.8 11.7 %dynamic_update_slice.194 = bf16[4,4,256,128]{3,0,2,1:T(4,128)(2,1)S(1)} dynamic-update-slice(bf16[4,4,256,128]{3,0,2,1:T(4,128)(2,1)S(1)} %dynamic_update_slice.193, bf16[1,4,256,128]{3,0,2,1:T(2,128)(2,1)S(1)} %copy.251, s32[]{:T(128)S(6)} %select_n.887, s32[]{:T(128)} %constant.298.clone.1, s32[]{:T(128)} %constant.298.clone.1, s32[]{:T(128)} %constant.298.clone.1) | dynamic-update-slice | bytes 524292 | tf_op jit(solution)/shard_map/dynamic_update_slice | solution.py:141
  173.5 11.7 %dynamic_update_slice.195 = bf16[4,4,256,128]{3,0,2,1:T(4,128)(2,1)S(1)} dynamic-update-slice(bf16[4,4,256,128]{3,0,2,1:T(4,128)(2,1)S(1)} %dynamic_update_slice.194, bf16[1,4,256,128]{3,0,2,1:T(2,128)(2,1)S(1)} %copy.252, s32[]{:T(128)S(6)} %select_n.888, s32[]{:T(128)} %constant.298.clone.1, s32[]{:T(128)} %constant.298.clone.1, s32[]{:T(128)} %constant.298.clone.1) | dynamic-update-slice | bytes 524292 | tf_op jit(solution)/shard_map/dynamic_update_slice | solution.py:142
  201.6 28.7 %dynamic_update_slice.184 = bf16[4,4,384,256]{3,0,2,1:T(4,128)(2,1)S(1)} dynamic-update-slice(bf16[4,4,384,256]{3,0,2,1:T(4,128)(2,1)S(1)} %broadcast_in_dim.165, bf16[1,4,384,256]{3,0,2,1:T(2,128)(2,1)} %copy.242, s32[]{:T(128)S(6)} %select_n.886, s32[]{:T(128)} %constant.298.clone.1, s32[]{:T(128)} %constant.298.clone.1, s32[]{:T(128)} %constant.298.clone.1) | dynamic-update-slice | bytes 1572868 | tf_op jit(solution)/shard_map/dynamic_update_slice | solution.py:140
  230.3 7.7 dynamic_update_slice.196
  238.0 7.6 dynamic_update_slice.197
  281.8 32.0 %dynamic_update_slice.185 = bf16[4,4,384,256]{3,0,2,1:T(4,128)(2,1)} dynamic-update-slice(bf16[4,4,384,256]{3,0,2,1:T(4,128)(2,1)} %copy-done.2, bf16[1,4,384,256]{3,0,2,1:T(2,128)(2,1)} %copy.243, s32[]{:T(128)S(6)} %select_n.887, s32[]{:T(128)} %constant.298.clone.1, s32[]{:T(128)} %constant.298.clone.1, s32[]{:T(128)} %constant.298.clone.1) | dynamic-update-slice | bytes 1572868 | tf_op jit(solution)/shard_map/dynamic_update_slice | solution.py:141
  313.8 32.4 %dynamic_update_slice.186 = bf16[4,4,384,256]{3,0,2,1:T(4,128)(2,1)} dynamic-update-slice(bf16[4,4,384,256]{3,0,2,1:T(4,128)(2,1)} %dynamic_update_slice.185, bf16[1,4,384,256]{3,0,2,1:T(2,128)(2,1)} %copy.244, s32[]{:T(128)S(6)} %select_n.888, s32[]{:T(128)} %constant.298.clone.1, s32[]{:T(128)} %constant.298.clone.1, s32[]{:T(128)} %constant.298.clone.1) | dynamic-update-slice | bytes 1572868 | tf_op jit(solution)/shard_map/dynamic_update_slice | solution.py:142
  351.6 16.5 %dynamic_update_slice.187 = bf16[4,4,384,256]{3,0,2,1:T(4,128)(2,1)} dynamic-update-slice(bf16[4,4,384,256]{3,0,2,1:T(4,128)(2,1)} %dynamic_update_slice.186, bf16[1,4,192,256]{3,0,2,1:T(2,128)(2,1)S(1)} %copy.245, s32[]{:T(128)S(6)} %select_n.889, s32[]{:T(128)} %constant.298.clone.1, s32[]{:T(128)} %constant.298.clone.1, s32[]{:T(128)} %constant.298.clone.1) | dynamic-update-slice | bytes 786436 | tf_op jit(solution)/shard_map/dynamic_update_slice | solution.py:143
  368.1 16.6 %dynamic_update_slice.188 = bf16[4,4,384,256]{3,0,2,1:T(4,128)(2,1)} dynamic-update-slice(bf16[4,4,384,256]{3,0,2,1:T(4,128)(2,1)} %dynamic_update_slice.187, bf16[1,4,192,256]{3,0,2,1:T(2,128)(2,1)} %copy.246, s32[]{:T(128)S(6)} %select_n.889, s32[]{:T(128)} %constant.298.clone.1, s32[]{:T(128)} %constant.323.clone.1, s32[]{:T(128)} %constant.298.clone.1) | dynamic-update-slice | bytes 786436 | tf_op jit(solution)/shard_map/dynamic_update_slice | solution.py:144
  386.8 6.1 all-to-all-start.1
  416.0 5.3 all-to-all-start.2
  421.4 7.3 all-to-all-done.2
  440.9 9.5 %all-to-all-done.3 = f32[16,32,128]{2,1,0:T(8,128)S(1)} async-done(((f32[16,32,128]{2,1,0:T(8,128)}), f32[16,32,128]{2,1,0:T(8,128)S(1)}, u32[]{:S(2)}, u32[]{:S(2)}) %all-to-all-start.3) | async-done | bytes 262176 | tf_op jit(solution)/shard_map/all_to_all | solution.py:110
  462.8 5.6 all-to-all-done.4
  495.2 12.5 %all-to-all-done.8 = bf16[4,128,512]{2,1,0:T(8,128)(2,1)} async-done(((bf16[4,128,512]{2,1,0:T(8,128)(2,1)}), bf16[4,128,512]{2,1,0:T(8,128)(2,1)}, u32[]{:S(2)}, u32[]{:S(2)}) %all-to-all-start.8) | async-done | bytes 524320 | tf_op jit(solution)/shard_map/all_to_all | solution.py:119
  519.6 5.2 all-to-all-done.6
  573.7 5.9 all-to-all-start.10
  608.1 6.5 all-to-all-start.11
  651.1 5.1 all-to-all-start.7
  662.8 7.1 all-to-all-done.7
  752.3 4.7 all-to-all-start.19
  773.7 5.1 all-to-all-start.20
  815.5 6.0 all-to-all-done.17
  830.4 13.7 %all-to-all-done.18 = bf16[4,384,256]{2,1,0:T(8,128)(2,1)S(1)} async-done(((bf16[4,384,256]{2,1,0:T(8,128)(2,1)}), bf16[4,384,256]{2,1,0:T(8,128)(2,1)S(1)}, u32[]{:S(2)}, u32[]{:S(2)}) %all-to-all-start.18) | async-done | bytes 786464 | tf_op jit(solution)/shard_map/all_to_all | solution.py:171
  861.2 11.7 %all-to-all-done.15 = bf16[4,512,256]{1,2,0:T(8,128)(2,1)S(1)} async-done(((bf16[4,512,256]{1,2,0:T(8,128)(2,1)}), bf16[4,512,256]{1,2,0:T(8,128)(2,1)S(1)}, u32[]{:S(2)}, u32[]{:S(2)}) %all-to-all-start.15) | async-done | bytes 1048608 | tf_op jit(solution)/shard_map/all_to_all | solution.py:119
  (1035 shorter events, 533.9 us)
Async XLA Ops:
  1.6 30.1 %collective-permute-start.1 = (bf16[128,128]{1,0:T(8,128)(2,1)S(1)}, bf16[128,128]{1,0:T(8,128)(2,1)S(1)}, u32[]{:S(2)}, u32[]{:S(2)}) collective-permute-start(bf16[128,128]{1,0:T(8,128)(2,1)S(1)} %get-tuple-element.90), channel_id=1, source_target_pairs={{0,1},{1,2},{2,3},{3,0},{4,5},{5,6},{6,7},{7,4},{8,9},{9,10},{10,1... | collective-permute-start | bytes 98312 | tf_op jit(solution)/shard_map/ppermute | solution.py:128
  4.7 254.3 %all-to-all-start = ((bf16[4,512,256]{2,1,0:T(8,128)(2,1)}), bf16[4,512,256]{2,1,0:T(8,128)(2,1)}, u32[]{:S(2)}, u32[]{:S(2)}) async-start(bf16[4,512,256]{2,1,0:T(8,128)(2,1)} %bitcast.738), calls=%async_computation | async-start | bytes 2097152 | tf_op jit(solution)/shard_map/all_to_all | solution.py:119
  9.1 54.7 %collective-permute-start.9 = (bf16[32,2304]{1,0:T(8,128)(2,1)S(1)}, bf16[32,2304]{1,0:T(8,128)(2,1)}, u32[]{:S(2)}, u32[]{:S(2)}) collective-permute-start(bf16[32,2304]{1,0:T(8,128)(2,1)S(1)} %bitcast.802), channel_id=1, source_target_pairs={{0,1},{1,2},{2,3},{3,0},{4,5},{5,6},{6,7},{7,4},{8,9},{9,10},{10,1... | collective-permute-start | bytes 442376 | tf_op jit(solution)/shard_map/ppermute | solution.py:128
  11.9 78.1 %collective-permute-start.18 = (bf16[384,256]{1,0:T(8,128)(2,1)}, bf16[384,256]{1,0:T(8,128)(2,1)}, u32[]{:S(2)}, u32[]{:S(2)}) collective-permute-start(bf16[384,256]{1,0:T(8,128)(2,1)} %pad_maximum_fusion.12), channel_id=1, source_target_pairs={{0,1},{1,2},{2,3},{3,0},{4,5},{5,6},{6,7},{7,4},{8,9},{9,10},{10,1... | collective-permute-start | bytes 589832 | tf_op jit(solution)/shard_map/ppermute | solution.py:128
  13.5 34.9 %collective-permute-start.26 = (bf16[256,128]{1,0:T(8,128)(2,1)S(1)}, bf16[256,128]{1,0:T(8,128)(2,1)S(1)}, u32[]{:S(2)}, u32[]{:S(2)}) collective-permute-start(bf16[256,128]{1,0:T(8,128)(2,1)S(1)} %get-tuple-element.84), channel_id=1, source_target_pairs={{0,1},{1,2},{2,3},{3,0},{4,5},{5,6},{6,7},{7,4},{8,9},{9,10},{10,1... | collective-permute-start | bytes 196616 | tf_op jit(solution)/shard_map/ppermute | solution.py:128
  58.8 32.6 %collective-permute-start.4 = (bf16[4,128,128]{2,1,0:T(8,128)(2,1)S(1)}, bf16[4,128,128]{2,1,0:T(8,128)(2,1)}, u32[]{:S(2)}, u32[]{:S(2)}) collective-permute-start(bf16[4,128,128]{2,1,0:T(8,128)(2,1)S(1)} %bitcast_dynamic-update-slice_fusion.29), channel_id=1, source_target_pairs={{0,4},{4,0},{8,12},{12,8},{1,5},{5,1},{9,13},{13,9},{2,6},{6,2},{1... | collective-permute-start | bytes 393224 | tf_op jit(solution)/shard_map/ppermute | solution.py:135
  62.2 30.9 %collective-permute-start.5 = (bf16[4,128,128]{2,1,0:T(8,128)(2,1)S(1)}, bf16[4,128,128]{2,1,0:T(8,128)(2,1)}, u32[]{:S(2)}, u32[]{:S(2)}) collective-permute-start(bf16[4,128,128]{2,1,0:T(8,128)(2,1)S(1)} %bitcast_dynamic-update-slice_fusion.29), channel_id=1, source_target_pairs={{0,8},{4,12},{8,0},{12,4},{1,9},{5,13},{9,1},{13,5},{2,10},{6,14},... | collective-permute-start | bytes 393224 | tf_op jit(solution)/shard_map/ppermute | solution.py:136
  70.6 50.9 %collective-permute-start.10 = (bf16[32,2304]{1,0:T(8,128)(2,1)}, bf16[32,2304]{1,0:T(8,128)(2,1)}, u32[]{:S(2)}, u32[]{:S(2)}) collective-permute-start(bf16[32,2304]{1,0:T(8,128)(2,1)} %collective-permute-done.9), channel_id=1, source_target_pairs={{0,1},{1,2},{2,3},{3,0},{4,5},{5,6},{6,7},{7,4},{8,9},{9,10},{10,1... | collective-permute-start | bytes 442376 | tf_op jit(solution)/shard_map/ppermute | solution.py:128
  72.3 52.2 %collective-permute-start.35 = (bf16[32,2304]{1,0:T(8,128)(2,1)}, bf16[32,2304]{1,0:T(8,128)(2,1)}, u32[]{:S(2)}, u32[]{:S(2)}) collective-permute-start(bf16[32,2304]{1,0:T(8,128)(2,1)} %collective-permute-done.34), channel_id=1, source_target_pairs={{0,1},{1,2},{2,3},{3,0},{4,5},{5,6},{6,7},{7,4},{8,9},{9,10},{10,1... | collective-permute-start | bytes 442376 | tf_op jit(solution)/shard_map/ppermute | solution.py:128
  90.0 61.4 %collective-permute-start.29 = (bf16[4,256,128]{2,1,0:T(8,128)(2,1)S(1)}, bf16[4,256,128]{2,1,0:T(8,128)(2,1)}, u32[]{:S(2)}, u32[]{:S(2)}) collective-permute-start(bf16[4,256,128]{2,1,0:T(8,128)(2,1)S(1)} %bitcast_dynamic-update-slice_fusion.25), channel_id=1, source_target_pairs={{0,4},{4,0},{8,12},{12,8},{1,5},{5,1},{9,13},{13,9},{2,6},{6,2},{1... | collective-permute-start | bytes 786440 | tf_op jit(solution)/shard_map/ppermute | solution.py:135
  91.5 61.2 %collective-permute-start.30 = (bf16[4,256,128]{2,1,0:T(8,128)(2,1)S(1)}, bf16[4,256,128]{2,1,0:T(8,128)(2,1)}, u32[]{:S(2)}, u32[]{:S(2)}) collective-permute-start(bf16[4,256,128]{2,1,0:T(8,128)(2,1)S(1)} %bitcast_dynamic-update-slice_fusion.25), channel_id=1, source_target_pairs={{0,8},{4,12},{8,0},{12,4},{1,9},{5,13},{9,1},{13,5},{2,10},{6,14},... | collective-permute-start | bytes 786440 | tf_op jit(solution)/shard_map/ppermute | solution.py:136
  93.2 43.2 %collective-permute-start.19 = (bf16[384,256]{1,0:T(8,128)(2,1)}, bf16[384,256]{1,0:T(8,128)(2,1)}, u32[]{:S(2)}, u32[]{:S(2)}) collective-permute-start(bf16[384,256]{1,0:T(8,128)(2,1)} %collective-permute-done.18), channel_id=1, source_target_pairs={{0,1},{1,2},{2,3},{3,0},{4,5},{5,6},{6,7},{7,4},{8,9},{9,10},{10,1... | collective-permute-start | bytes 589832 | tf_op jit(solution)/shard_map/ppermute | solution.py:128
  150.7 37.9 %collective-permute-start.20 = (bf16[384,256]{1,0:T(8,128)(2,1)}, bf16[384,256]{1,0:T(8,128)(2,1)}, u32[]{:S(2)}, u32[]{:S(2)}) collective-permute-start(bf16[384,256]{1,0:T(8,128)(2,1)} %collective-permute-done.19), channel_id=1, source_target_pairs={{0,1},{1,2},{2,3},{3,0},{4,5},{5,6},{6,7},{7,4},{8,9},{9,10},{10,1... | collective-permute-start | bytes 589832 | tf_op jit(solution)/shard_map/ppermute | solution.py:128
  151.4 94.2 %collective-permute-start.12 = (bf16[4,32,2304]{2,1,0:T(8,128)(2,1)}, bf16[4,32,2304]{2,1,0:T(8,128)(2,1)}, u32[]{:S(2)}, u32[]{:S(2)}) collective-permute-start(bf16[4,32,2304]{2,1,0:T(8,128)(2,1)} %bitcast_dynamic-update-slice_fusion.20), channel_id=1, source_target_pairs={{0,4},{4,0},{8,12},{12,8},{1,5},{5,1},{9,13},{13,9},{2,6},{6,2},{1... | collective-permute-start | bytes 1769480 | tf_op jit(solution)/shard_map/ppermute | solution.py:135
  152.7 95.3 %collective-permute-start.13 = (bf16[4,32,2304]{2,1,0:T(8,128)(2,1)}, bf16[4,32,2304]{2,1,0:T(8,128)(2,1)}, u32[]{:S(2)}, u32[]{:S(2)}) collective-permute-start(bf16[4,32,2304]{2,1,0:T(8,128)(2,1)} %bitcast_dynamic-update-slice_fusion.20), channel_id=1, source_target_pairs={{0,8},{4,12},{8,0},{12,4},{1,9},{5,13},{9,1},{13,5},{2,10},{6,14},... | collective-permute-start | bytes 1769480 | tf_op jit(solution)/shard_map/ppermute | solution.py:136
  154.1 96.2 %collective-permute-start.37 = (bf16[4,32,2304]{2,1,0:T(8,128)(2,1)}, bf16[4,32,2304]{2,1,0:T(8,128)(2,1)}, u32[]{:S(2)}, u32[]{:S(2)}) collective-permute-start(bf16[4,32,2304]{2,1,0:T(8,128)(2,1)} %bitcast_dynamic-update-slice_fusion.17), channel_id=1, source_target_pairs={{0,4},{4,0},{8,12},{12,8},{1,5},{5,1},{9,13},{13,9},{2,6},{6,2},{1... | collective-permute-start | bytes 1769480 | tf_op jit(solution)/shard_map/ppermute | solution.py:135
  154.6 98.8 %collective-permute-start.38 = (bf16[4,32,2304]{2,1,0:T(8,128)(2,1)}, bf16[4,32,2304]{2,1,0:T(8,128)(2,1)}, u32[]{:S(2)}, u32[]{:S(2)}) collective-permute-start(bf16[4,32,2304]{2,1,0:T(8,128)(2,1)} %bitcast_dynamic-update-slice_fusion.17), channel_id=1, source_target_pairs={{0,8},{4,12},{8,0},{12,4},{1,9},{5,13},{9,1},{13,5},{2,10},{6,14},... | collective-permute-start | bytes 1769480 | tf_op jit(solution)/shard_map/ppermute | solution.py:136
  198.5 276.8 %collective-permute-start.48 = (bf16[4,64,256]{2,0,1:T(4,128)(2,1)}, bf16[4,64,256]{2,0,1:T(4,128)(2,1)}, u32[]{:S(2)}, u32[]{:S(2)}) collective-permute-start(bf16[4,64,256]{2,0,1:T(4,128)(2,1)} %slice.877), channel_id=1, source_target_pairs={{0,8},{4,12},{8,0},{12,4},{1,9},{5,13},{9,1},{13,5},{2,10},{6,14},... | collective-permute-start | bytes 393224 | tf_op jit(solution)/shard_map/ppermute | solution.py:137
  267.2 117.6 %collective-permute-start.8 = (f32[1024,256]{1,0:T(8,128)}, f32[1024,256]{1,0:T(8,128)}, u32[]{:S(2)}, u32[]{:S(2)}) collective-permute-start(f32[1024,256]{1,0:T(8,128)} %slice_select_fusion), channel_id=1, source_target_pairs={{0,16},{16,0},{1,17},{17,1},{2,18},{18,2},{3,19},{19,3},{4,20},{20... | collective-permute-start | bytes 3145736 | tf_op jit(solution)/shard_map/ppermute | solution.py:78
  269.1 212.8 %collective-permute-start.49 = (bf16[4,64,256]{2,0,1:T(4,128)(2,1)}, bf16[4,64,256]{2,0,1:T(4,128)(2,1)}, u32[]{:S(2)}, u32[]{:S(2)}) collective-permute-start(bf16[4,64,256]{2,0,1:T(4,128)(2,1)} %slice.878), channel_id=1, source_target_pairs={{0,4},{4,0},{8,12},{12,8},{1,5},{5,1},{9,13},{13,9},{2,6},{6,2},{1... | collective-permute-start | bytes 393224 | tf_op jit(solution)/shard_map/ppermute | solution.py:138
  271.5 74.6 %collective-permute-start.23 = (bf16[4,192,256]{2,1,0:T(8,128)(2,1)S(1)}, bf16[4,192,256]{2,1,0:T(8,128)(2,1)S(1)}, u32[]{:S(2)}, u32[]{:S(2)}) collective-permute-start(bf16[4,192,256]{2,1,0:T(8,128)(2,1)S(1)} %slice.852), channel_id=1, source_target_pairs={{0,8},{4,12},{8,0},{12,4},{1,9},{5,13},{9,1},{13,5},{2,10},{6,14},... | collective-permute-start | bytes 1179656 | tf_op jit(solution)/shard_map/ppermute | solution.py:137
  273.2 76.0 %collective-permute-start.24 = (bf16[4,192,256]{2,1,0:T(8,128)(2,1)S(1)}, bf16[4,192,256]{2,1,0:T(8,128)(2,1)}, u32[]{:S(2)}, u32[]{:S(2)}) collective-permute-start(bf16[4,192,256]{2,1,0:T(8,128)(2,1)S(1)} %slice.853), channel_id=1, source_target_pairs={{0,4},{4,0},{8,12},{12,8},{1,5},{5,1},{9,13},{13,9},{2,6},{6,2},{1... | collective-permute-start | bytes 1179656 | tf_op jit(solution)/shard_map/ppermute | solution.py:138
  346.2 108.6 %collective-permute-start.39 = (bf16[4,16,2304]{2,1,0:T(8,128)(2,1)}, bf16[4,16,2304]{2,1,0:T(8,128)(2,1)}, u32[]{:S(2)}, u32[]{:S(2)}) collective-permute-start(bf16[4,16,2304]{2,1,0:T(8,128)(2,1)} %slice.873), channel_id=1, source_target_pairs={{0,8},{4,12},{8,0},{12,4},{1,9},{5,13},{9,1},{13,5},{2,10},{6,14},... | collective-permute-start | bytes 884744 | tf_op jit(solution)/shard_map/ppermute | solution.py:137
  412.2 48.8 %collective-permute-start.40 = (bf16[4,16,2304]{2,1,0:T(8,128)(2,1)}, bf16[4,16,2304]{2,1,0:T(8,128)(2,1)}, u32[]{:S(2)}, u32[]{:S(2)}) collective-permute-start(bf16[4,16,2304]{2,1,0:T(8,128)(2,1)} %slice.874), channel_id=1, source_target_pairs={{0,4},{4,0},{8,12},{12,8},{1,5},{5,1},{9,13},{13,9},{2,6},{6,2},{1... | collective-permute-start | bytes 884744 | tf_op jit(solution)/shard_map/ppermute | solution.py:138
  622.0 29.0 %all-to-all-start.21 = ((bf16[4,128,256]{2,1,0:T(8,128)(2,1)}), bf16[4,128,256]{2,1,0:T(8,128)(2,1)}, u32[]{:S(2)}, u32[]{:S(2)}) async-start(bf16[4,128,256]{2,1,0:T(8,128)(2,1)} %fusion.89), calls=%async_computation.21 | async-start | bytes 524288 | tf_op jit(solution)/shard_map/all_to_all | solution.py:171
  641.9 32.9 %collective-permute-start.77 = (bf16[4,128,128]{2,1,0:T(8,128)(2,1)}, bf16[4,128,128]{2,1,0:T(8,128)(2,1)}, u32[]{:S(2)}, u32[]{:S(2)}) collective-permute-start(bf16[4,128,128]{2,1,0:T(8,128)(2,1)} %get-tuple-element.140), channel_id=1, source_target_pairs={{0,4},{4,0},{8,12},{12,8},{1,5},{5,1},{9,13},{13,9},{2,6},{6,2},{1... | collective-permute-start | bytes 393224 | tf_op jit(solution)/shard_map/ppermute | solution.py:159
  649.4 69.9 %collective-permute-start.81 = (bf16[4,32,2304]{2,1,0:T(8,128)(2,1)}, bf16[4,32,2304]{2,1,0:T(8,128)(2,1)}, u32[]{:S(2)}, u32[]{:S(2)}) collective-permute-start(bf16[4,32,2304]{2,1,0:T(8,128)(2,1)} %pad_maximum_fusion.5), channel_id=1, source_target_pairs={{0,4},{4,0},{8,12},{12,8},{1,5},{5,1},{9,13},{13,9},{2,6},{6,2},{1... | collective-permute-start | bytes 1769480 | tf_op jit(solution)/shard_map/ppermute | solution.py:168
  657.0 62.3 %collective-permute-start.83 = (bf16[4,32,2304]{2,1,0:T(8,128)(2,1)}, bf16[4,32,2304]{2,1,0:T(8,128)(2,1)}, u32[]{:S(2)}, u32[]{:S(2)}) collective-permute-start(bf16[4,32,2304]{2,1,0:T(8,128)(2,1)} %pad_maximum_fusion.6), channel_id=1, source_target_pairs={{0,8},{4,12},{8,0},{12,4},{1,9},{5,13},{9,1},{13,5},{2,10},{6,14},... | collective-permute-start | bytes 1769480 | tf_op jit(solution)/shard_map/ppermute | solution.py:169
  660.4 49.6 %collective-permute-start.76 = (bf16[4,256,128]{2,1,0:T(8,128)(2,1)}, bf16[4,256,128]{2,1,0:T(8,128)(2,1)}, u32[]{:S(2)}, u32[]{:S(2)}) collective-permute-start(bf16[4,256,128]{2,1,0:T(8,128)(2,1)} %pad_maximum_fusion.8), channel_id=1, source_target_pairs={{0,4},{4,0},{8,12},{12,8},{1,5},{5,1},{9,13},{13,9},{2,6},{6,2},{1... | collective-permute-start | bytes 786440 | tf_op jit(solution)/shard_map/ppermute | solution.py:168
  677.5 34.5 %collective-permute-start.78 = (bf16[4,256,128]{2,1,0:T(8,128)(2,1)}, bf16[4,256,128]{2,1,0:T(8,128)(2,1)}, u32[]{:S(2)}, u32[]{:S(2)}) collective-permute-start(bf16[4,256,128]{2,1,0:T(8,128)(2,1)} %pad_maximum_fusion.9), channel_id=1, source_target_pairs={{0,8},{4,12},{8,0},{12,4},{1,9},{5,13},{9,1},{13,5},{2,10},{6,14},... | collective-permute-start | bytes 786440 | tf_op jit(solution)/shard_map/ppermute | solution.py:169
  712.0 95.2 %collective-permute-start.58 = (f32[256,4,128]{2,0,1:T(8,128)}, f32[256,4,128]{2,0,1:T(8,128)}, u32[]{:S(2)}, u32[]{:S(2)}) collective-permute-start(f32[256,4,128]{2,0,1:T(8,128)} %slice_select_fusion.1), channel_id=1, source_target_pairs={{0,16},{16,0},{1,17},{17,1},{2,18},{18,2},{3,19},{19,3},{4,20},{20... | collective-permute-start | bytes 1572872 | tf_op jit(solution)/shard_map/ppermute | solution.py:78
  761.9 35.3 %collective-permute-start.66 = (bf16[4,32,2304]{2,1,0:T(8,128)(2,1)}, bf16[4,32,2304]{2,1,0:T(8,128)(2,1)}, u32[]{:S(2)}, u32[]{:S(2)}) collective-permute-start(bf16[4,32,2304]{2,1,0:T(8,128)(2,1)} %pad_maximum_fusion.3), channel_id=1, source_target_pairs={{0,4},{4,0},{8,12},{12,8},{1,5},{5,1},{9,13},{13,9},{2,6},{6,2},{1... | collective-permute-start | bytes 1769480 | tf_op jit(solution)/shard_map/ppermute | solution.py:168
  (269 other events, 3111.2 us)

commit v2 on v1

--- a/solution.py
+++ b/solution.py
@@ -3,6 +3,8 @@
 import jax
 import jax.numpy as jnp
 from jax import lax
+from jax.experimental import pallas as pl
+from jax.experimental.pallas import tpu as pltpu
 from jax.sharding import PartitionSpec as P
 
 EPS = 1e-05
@@ -10,6 +12,8 @@
 CUBE = 0.044715
 F32 = jnp.float32
 BF16 = jnp.bfloat16
+XS = [(k, k ^ 1) for k in range(4)]
+YS = [(k, k ^ 2) for k in range(4)]
 
 
 def mm(left, right):
@@ -118,30 +122,50 @@
     def to_images(x):
         return lax.all_to_all(x, "outer", split_axis=0, concat_axis=0, tiled=True)
 
-    def gather_blocks(shard):
-        rows, cols = shard.shape
+    def gather_pieces(shard):
         ring = [(k, (k + 1) % no) for k in range(no)]
-        piece = shard
-        whole = jnp.zeros((no, rows, cols), shard.dtype)
-        whole = lax.dynamic_update_slice(whole, piece[None], (o, 0, 0))
-        for step in range(1, no):
-            piece = lax.ppermute(piece, "outer", ring)
-            whole = lax.dynamic_update_slice(whole, piece[None], ((o + no - step) % no, 0, 0))
-        if ni != 4:
-            return lax.all_gather(whole, "inner", axis=0, tiled=False)
+        pieces = [shard]
+        for _ in range(1, no):
+            pieces.append(lax.ppermute(pieces[-1], "outer", ring))
+        whole = jnp.stack(pieces)
+        h = shard.shape[0] // 2
+        by_x = lax.ppermute(whole, "inner", XS)
+        by_y = lax.ppermute(whole, "inner", YS)
+        low = lax.ppermute(by_x[:, :h], "inner", YS)
+        high = lax.ppermute(by_y[:, h:], "inner", XS)
+        return whole, by_x, by_y, low, high
+
+    def assemble(pieces, segments):
+        rows, cols = pieces[0].shape[1:]
         h = rows // 2
-        xs = [(k, k ^ 1) for k in range(4)]
-        ys = [(k, k ^ 2) for k in range(4)]
-        by_x = lax.ppermute(whole, "inner", xs)
-        by_y = lax.ppermute(whole, "inner", ys)
-        low = lax.ppermute(by_x[:, :h], "inner", ys)
-        high = lax.ppermute(by_y[:, h:], "inner", xs)
-        full = jnp.zeros((4, no, rows, cols), shard.dtype)
-        full = lax.dynamic_update_slice(full, whole[None], (i, 0, 0, 0))
-        full = lax.dynamic_update_slice(full, by_x[None], (i ^ 1, 0, 0, 0))
-        full = lax.dynamic_update_slice(full, by_y[None], (i ^ 2, 0, 0, 0))
-        full = lax.dynamic_update_slice(full, low[None], (i ^ 3, 0, 0, 0))
-        return lax.dynamic_update_slice(full, high[None], (i ^ 3, 0, h, 0))
+        spans = [(0, 0, rows), (1, 0, rows), (2, 0, rows), (3, 0, h), (3, h, rows)]
+        plan = []
+        for src, (far, lo, hi_row) in enumerate(spans):
+            for d in range(no):
+                for dst, (first, count, _, place) in enumerate(segments):
+                    a, z = max(lo, first), min(hi_row, first + count)
+                    if a < z:
+                        plan.append((src, far, d, a - lo, z - a, dst, a - first, place))
+        n_src, n_dst = len(spans), len(segments)
+
+        def kernel(where, *refs):
+            sources, targets = refs[:n_src], refs[n_src:]
+            me_i, me_o = where[0], where[1]
+            for src, far, d, begin, count, dst, offset, place in plan:
+                row, col, row_unit, col_unit = place(me_i ^ far, lax.rem(me_o + (no - d), no))
+                targets[dst][
+                    pl.ds(pl.multiple_of(row * row_unit, row_unit) + offset, count),
+                    pl.ds(pl.multiple_of(col * col_unit, col_unit), cols),
+                ] = sources[src][d, begin : begin + count, :]
+
+        return pl.pallas_call(
+            kernel,
+            out_shape=[jax.ShapeDtypeStruct(seg[2], BF16) for seg in segments],
+            in_specs=[pl.BlockSpec(memory_space=pltpu.SMEM)]
+            + [pl.BlockSpec(memory_space=pltpu.VMEM)] * n_src,
+            out_specs=[pl.BlockSpec(memory_space=pltpu.VMEM)] * n_dst,
+            compiler_params=pltpu.CompilerParams(vmem_limit_bytes=24 << 20),
+        )(jnp.stack([i, o]).astype(jnp.int32), *pieces)
 
     def scatter_blocks(blocks):
         rows, cols = blocks.shape[2:]
@@ -149,15 +173,12 @@
             mine_i = lax.psum_scatter(blocks.astype(F32), "inner", scatter_dimension=0, tiled=True)[0]
         else:
             h = rows // 2
-            xs = [(k, k ^ 1) for k in range(4)]
-            ys = [(k, k ^ 2) for k in range(4)]
-
             def block(k):
                 return lax.dynamic_index_in_dim(blocks, k, 0, keepdims=False)
 
             far = block(i ^ 3)
-            low = lax.ppermute(far[:, :h], "inner", xs)
-            high = lax.ppermute(far[:, h:], "inner", ys)
+            low = lax.ppermute(far[:, :h], "inner", XS)
+            high = lax.ppermute(far[:, h:], "inner", YS)
             for_x, for_y = block(i ^ 1), block(i ^ 2)
             for_x = jnp.concatenate(
                 [for_x[:, :h], (for_x[:, h:].astype(F32) + high.astype(F32)).astype(BF16)], 1
@@ -165,8 +186,8 @@
             for_y = jnp.concatenate(
                 [(for_y[:, :h].astype(F32) + low.astype(F32)).astype(BF16), for_y[:, h:]], 1
             )
-            by_x = lax.ppermute(for_x, "inner", xs)
-            by_y = lax.ppermute(for_y, "inner", ys)
+            by_x = lax.ppermute(for_x, "inner", XS)
+            by_y = lax.ppermute(for_y, "inner", YS)
             mine_i = block(i).astype(F32) + by_x.astype(F32) + by_y.astype(F32)
         parts = lax.all_to_all(
             mine_i.astype(BF16), "outer", split_axis=0, concat_axis=0, tiled=True
@@ -208,42 +229,46 @@
         return jnp.einsum("ps,msk->mpk", matrix, x, preferred_element_type=F32).astype(BF16)
 
     got = to_images(images.reshape(img_dev, cells_in, in_part))
-    shard_r1 = mine(first_reduce, 0)
 
     def taps_shard(w):
         k_half = mine(w, 2).reshape(9, mid_h, -1)
         return k_half.transpose(2, 0, 1).reshape(-1, 9 * mid_h)
 
-    full_r1 = gather_blocks(shard_r1)
-    full_t1 = gather_blocks(taps_shard(first_taps))
-    full_es = gather_blocks(jnp.concatenate([mine(first_expand, 1), mine(first_shortcut, 1)], 0))
+    def down_place(r, k):
+        return lambda at_i, at_o: (at_o, at_i, r, k)
+
+    def up_place(r, k):
+        return lambda at_i, at_o: (at_i, at_o, r, k)
+
+    def taps_place(r, k):
+        return lambda at_i, at_o: (at_i * no + at_o, 0, r, k)
+
+    def gathered(*entries):
+        shard = entries[0][0] if len(entries) == 1 else jnp.concatenate([e[0] for e in entries], 0)
+        segments, first = [], 0
+        for part, place in entries:
+            r, k = part.shape
+            at = place(r, k)
+            shape = {down_place: (no * r, ni * k), up_place: (ni * r, no * k)}.get(
+                place, (ni * no * r, k)
+            )
+            segments.append((first, r, shape, at))
+            first += r
+        return assemble(gather_pieces(shard), segments)
+
+    (w_r1,) = gathered((mine(first_reduce, 0), down_place))
+    (w_t1,) = gathered((taps_shard(first_taps), taps_place))
+    w_e1, w_s = gathered((mine(first_expand, 1), up_place), (mine(first_shortcut, 1), down_place))
+    (w_r2,) = gathered((mine(second_reduce, 0), down_place))
+    (w_t2,) = gathered((taps_shard(second_taps), taps_place))
+    (w_e2,) = gathered((mine(second_expand, 1), up_place))
     rows_e = first_expand.shape[0]
-    full_e1, full_s = full_es[:, :, :rows_e], full_es[:, :, rows_e:]
-    full_r2 = gather_blocks(mine(second_reduce, 0))
-    full_t2 = gather_blocks(taps_shard(second_taps))
-    full_e2 = gather_blocks(mine(second_expand, 1))
-
-    def outer_rows(full):
-        r, k = full.shape[2:]
-        return full.transpose(1, 2, 0, 3).reshape(no * r, ni * k)
-
-    def inner_rows(full):
-        r, k = full.shape[2:]
-        return full.transpose(0, 2, 1, 3).reshape(ni * r, no * k)
 
     def outer_blocks(whole, r, k):
         return whole.reshape(no, r, ni, k).transpose(2, 0, 1, 3)
 
     def inner_blocks(whole, r, k):
         return whole.reshape(ni, r, no, k).transpose(0, 2, 1, 3)
-
-    w_r1 = outer_rows(full_r1)
-    w_t1 = full_t1.reshape(mid, 9 * mid_h)
-    w_e1 = inner_rows(full_e1)
-    w_s = outer_rows(full_s)
-    w_r2 = outer_rows(full_r2)
-    w_t2 = full_t2.reshape(mid, 9 * mid_h)
-    w_e2 = inner_rows(full_e2)
 
     def both_images(x, lanes):
         own = mine(x, 3)

time: 893 us -> 629 us (0.70)
  local copies, waits for them, and re-layouts: 377 us -> 122 us
  matrix products: 68 us -> 46.8 us
  other arithmetic: 102 us -> 119 us
    dynamic_update_slice x51 -> x0, local copies, waits for them, and re-layouts: 243 us -> none  [the longest x6 54.6 us: gather_blocks(): full = lax.dynamic_update_slice(full, by_y[None], (i ^ 2, 0, 0, 0))]
    broadcast_in_dim x27 -> x0, local copies, waits for them, and re-layouts: 24.7 us -> none  [the longest x3 6.01 us: gather_blocks(): full = lax.dynamic_update_slice(full, by_x[None], (i ^ 1, 0, 0, 0))]
    unnamed x428 -> x501, local copies, waits for them, and re-layouts: 21.1 us -> 42.7 us
    dot_general x23, matrix products: 32.3 us -> 12.3 us  [mm(): return jnp.dot(left, right, preferred_element_type=F32)]
    all_to_all x12, waiting for transfers between devices: 44.6 us -> 29.1 us  [sums_of(): lax.all_to_all(copies, ('inner', 'outer'), split_axis=0, concat_axis=0, t...]
    ppermute x66, waiting for transfers between devices: 32.1 us -> 46.5 us  [the longest x18 24.6 us: gather_pieces(): pieces.append(lax.ppermute(pieces[-1], 'outer', ring))]
    ppermute x66, starting transfers between devices: 88.6 us -> 77.5 us  [the longest x18 24.9 us: gather_pieces(): pieces.append(lax.ppermute(pieces[-1], 'outer', ring))]
    another operation x1 -> x12, other arithmetic: 0.1 us -> 9.35 us  [the longest x10 7.32 us: gather_pieces(): whole = jnp.stack(pieces)]
  transfers between devices with their start and end apart: 114 -> 114, of which waited for: 31 -> 30; matrix products, arithmetic and copies ran while one was open for 59% -> 39% of each run, Pallas kernels for 0% -> 1%
where the time goes in v2:
time: 629 us; the launch traced here: 617 us
  starting transfers between devices  186 us (30%)
  waiting for transfers between devices  130 us (21%)
  local copies, waits for them, and re-layouts  122 us (19%)
  other arithmetic  119 us (19%)
  matrix products  46.8 us (7%)
  Pallas kernels  6.52 us (1%)
    all_to_all x12, starting transfers between devices, sums_of(): lax.all_to_all(copies, ('inner', 'outer'), split_axis=0, concat_axis=0, t...  59.6 us
    unnamed x501, local copies, waits for them, and re-layouts  42.7 us
    all_to_all x4, waiting for transfers between devices, to_images(): return lax.all_to_all(x, 'outer', split_axis=0, concat_axis=0, tiled=True)  33 us
    all_to_all x12, waiting for transfers between devices, sums_of(): lax.all_to_all(copies, ('inner', 'outer'), split_axis=0, concat_axis=0, t...  29.1 us
    all_to_all x6, starting transfers between devices, scatter_blocks(): lax.all_to_all(mine_i.astype(BF16), 'outer', split_axis=0, concat_axis=0,...  26.4 us
    ppermute x18, starting transfers between devices, gather_pieces(): pieces.append(lax.ppermute(pieces[-1], 'outer', ring))  24.9 us
    ppermute x18, waiting for transfers between devices, gather_pieces(): pieces.append(lax.ppermute(pieces[-1], 'outer', ring))  24.6 us
    all_to_all x6, waiting for transfers between devices, scatter_blocks(): lax.all_to_all(mine_i.astype(BF16), 'outer', split_axis=0, concat_axis=0,...  20.2 us
  transfers between devices with their start and end apart: 114, of which 30 were waited for; matrix products, arithmetic and copies ran while one was open for 39% of the time, Pallas kernels for 1%

profile of v2, /device:TPU:0, one launch (start us, length us, event | category | flops | bytes accessed | tf_op | source)
XLA Modules:
  0.0 617.1 jit_solution(4041093729650717362)
XLA Ops:
  0.7 6.5 %all-to-all-start = ((bf16[4,512,256]{2,1,0:T(8,128)(2,1)}), bf16[4,512,256]{2,1,0:T(8,128)(2,1)S(1)}, u32[]{:S(2)}, u32[]{:S(2)}) async-start(bf16[4,512,256]{2,1,0:T(8,128)(2,1)} %bitcast.638), calls=%async_computation | async-start | bytes 2097152 | tf_op jit(solution)/shard_map/all_to_all | solution.py:123
  18.1 12.3 %collective-permute-done.1 = bf16[128,128]{1,0:T(8,128)(2,1)S(1)} collective-permute-done((bf16[128,128]{1,0:T(8,128)(2,1)S(1)}, bf16[128,128]{1,0:T(8,128)(2,1)S(1)}, u32[]{:S(2)}, u32[]{:S(2)}) %collective-permute-start.1) | collective-permute-done | bytes 32800 | tf_op jit(solution)/shard_map/ppermute | solution.py:129
  78.7 3.8 collective-permute-done.12.refs_1_
  90.2 6.3 %all-to-all-start.1 = ((f32[16,4,128]{2,1,0:T(4,128)}), f32[16,4,128]{2,1,0:T(4,128)S(1)}, u32[]{:S(2)}, u32[]{:S(2)}) async-start(f32[16,4,128]{2,1,0:T(4,128)} %broadcast_in_dim.24), calls=%async_computation.1 | async-start | bytes 65536 | tf_op jit(solution)/shard_map/all_to_all | solution.py:114
  99.0 4.3 collective-permute-done.14.refs_3_
  143.3 5.3 all-to-all-start.2
  150.5 5.5 all-to-all-done.2
  161.9 3.5 all-to-all-start.3
  184.9 4.5 collective-permute-done.44
  193.8 6.1 all-to-all-start.4
  229.2 7.0 %all-to-all-start.5 = ((f32[16,4,128]{2,1,0:T(4,128)}), f32[16,4,128]{2,1,0:T(4,128)}, u32[]{:S(2)}, u32[]{:S(2)}) async-start(f32[16,4,128]{2,1,0:T(4,128)} %broadcast_in_dim.28), calls=%async_computation.5 | async-start | bytes 65536 | tf_op jit(solution)/shard_map/all_to_all | solution.py:114
  243.5 4.1 all-to-all-start.8
  251.0 10.2 %all-to-all-done.8 = bf16[4,128,512]{2,1,0:T(8,128)(2,1)} async-done(((bf16[4,128,512]{2,1,0:T(8,128)(2,1)}), bf16[4,128,512]{2,1,0:T(8,128)(2,1)}, u32[]{:S(2)}, u32[]{:S(2)}) %all-to-all-start.8) | async-done | bytes 524320 | tf_op jit(solution)/shard_map/all_to_all | solution.py:123
  273.1 5.2 all-to-all-done.6
  281.0 4.2 fusion.298
  285.8 3.7 all-to-all-start.9
  324.3 4.7 all-to-all-start.10
  332.5 4.0 all-to-all-done.10
  348.9 6.0 all-to-all-start.11
  362.9 4.0 all-to-all-start.21
  392.5 5.1 all-to-all-start.7
  402.3 9.0 %all-to-all-done.7 = bf16[4,128,512]{2,1,0:T(8,128)(2,1)S(1)} async-done(((bf16[4,128,512]{2,1,0:T(8,128)(2,1)}), bf16[4,128,512]{2,1,0:T(8,128)(2,1)S(1)}, u32[]{:S(2)}, u32[]{:S(2)}) %all-to-all-start.7) | async-done | bytes 524320 | tf_op jit(solution)/shard_map/all_to_all | solution.py:123
  412.0 4.1 all-to-all-start.12
  452.1 3.5 all-to-all-start.13
  477.6 5.7 all-to-all-start.14
  492.1 4.5 all-to-all-start.19
  513.2 5.1 all-to-all-start.20
  543.3 4.2 all-to-all-start.17
  563.2 5.2 all-to-all-start.18
  572.7 13.6 %all-to-all-done.18 = bf16[4,384,256]{2,1,0:T(8,128)(2,1)S(1)} async-done(((bf16[4,384,256]{2,1,0:T(8,128)(2,1)}), bf16[4,384,256]{2,1,0:T(8,128)(2,1)S(1)}, u32[]{:S(2)}, u32[]{:S(2)}) %all-to-all-start.18) | async-done | bytes 786464 | tf_op jit(solution)/shard_map/all_to_all | solution.py:192
  586.3 3.5 all-to-all-start.15
  602.3 12.2 %all-to-all-done.15 = bf16[4,512,256]{1,2,0:T(8,128)(2,1)S(1)} async-done(((bf16[4,512,256]{1,2,0:T(8,128)(2,1)}), bf16[4,512,256]{1,2,0:T(8,128)(2,1)S(1)}, u32[]{:S(2)}, u32[]{:S(2)}) %all-to-all-start.15) | async-done | bytes 1048608 | tf_op jit(solution)/shard_map/all_to_all | solution.py:123
  (1037 shorter events, 424.5 us)
Async XLA Ops:
  0.7 41.3 %all-to-all-start = ((bf16[4,512,256]{2,1,0:T(8,128)(2,1)}), bf16[4,512,256]{2,1,0:T(8,128)(2,1)S(1)}, u32[]{:S(2)}, u32[]{:S(2)}) async-start(bf16[4,512,256]{2,1,0:T(8,128)(2,1)} %bitcast.638), calls=%async_computation | async-start | bytes 2097152 | tf_op jit(solution)/shard_map/all_to_all | solution.py:123
  7.2 23.2 %collective-permute-start.1 = (bf16[128,128]{1,0:T(8,128)(2,1)S(1)}, bf16[128,128]{1,0:T(8,128)(2,1)S(1)}, u32[]{:S(2)}, u32[]{:S(2)}) collective-permute-start(bf16[128,128]{1,0:T(8,128)(2,1)S(1)} %slice_select_fusion.13), channel_id=1, source_target_pairs={{0,1},{1,2},{2,3},{3,0},{4,5},{5,6},{6,7},{7,4},{8,9},{9,10},{10,1... | collective-permute-start | bytes 98312 | tf_op jit(solution)/shard_map/ppermute | solution.py:129
  10.0 36.5 %collective-permute-start.9 = (bf16[32,2304]{1,0:T(8,128)(2,1)}, bf16[32,2304]{1,0:T(8,128)(2,1)S(1)}, u32[]{:S(2)}, u32[]{:S(2)}) collective-permute-start(bf16[32,2304]{1,0:T(8,128)(2,1)} %bitcast.287), channel_id=1, source_target_pairs={{0,1},{1,2},{2,3},{3,0},{4,5},{5,6},{6,7},{7,4},{8,9},{9,10},{10,1... | collective-permute-start | bytes 442376 | tf_op jit(solution)/shard_map/ppermute | solution.py:129
  12.2 35.9 %collective-permute-start.18 = (bf16[384,256]{1,0:T(8,128)(2,1)S(1)}, bf16[384,256]{1,0:T(8,128)(2,1)}, u32[]{:S(2)}, u32[]{:S(2)}) collective-permute-start(bf16[384,256]{1,0:T(8,128)(2,1)S(1)} %get-tuple-element.140), channel_id=1, source_target_pairs={{0,1},{1,2},{2,3},{3,0},{4,5},{5,6},{6,7},{7,4},{8,9},{9,10},{10,1... | collective-permute-start | bytes 589832 | tf_op jit(solution)/shard_map/ppermute | solution.py:129
  62.8 21.8 %collective-permute-start.8 = (f32[1024,256]{1,0:T(8,128)S(1)}, f32[1024,256]{1,0:T(8,128)}, u32[]{:S(2)}, u32[]{:S(2)}) collective-permute-start(f32[1024,256]{1,0:T(8,128)S(1)} %slice_select_fusion), channel_id=1, source_target_pairs={{0,16},{16,0},{1,17},{17,1},{2,18},{18,2},{3,19},{19,3},{4,20},{20... | collective-permute-start | bytes 3145736 | tf_op jit(solution)/shard_map/ppermute | solution.py:82
  70.5 39.7 %collective-permute-start.21 = (bf16[4,384,256]{2,1,0:T(8,128)(2,1)}, bf16[4,384,256]{2,1,0:T(8,128)(2,1)}, u32[]{:S(2)}, u32[]{:S(2)}) collective-permute-start(bf16[4,384,256]{2,1,0:T(8,128)(2,1)} %pad_maximum_fusion.1.refs_0_), channel_id=1, source_target_pairs={{0,4},{4,0},{8,12},{12,8},{1,5},{5,1},{9,13},{13,9},{2,6},{6,2},{1... | collective-permute-start | bytes 2359304 | tf_op jit(solution)/shard_map/ppermute | solution.py:132
  72.0 40.8 %collective-permute-start.22 = (bf16[4,384,256]{2,1,0:T(8,128)(2,1)}, bf16[4,384,256]{2,1,0:T(8,128)(2,1)}, u32[]{:S(2)}, u32[]{:S(2)}) collective-permute-start(bf16[4,384,256]{2,1,0:T(8,128)(2,1)} %pad_maximum_fusion.1.refs_0_), channel_id=1, source_target_pairs={{0,8},{4,12},{8,0},{12,4},{1,9},{5,13},{9,1},{13,5},{2,10},{6,14},... | collective-permute-start | bytes 2359304 | tf_op jit(solution)/shard_map/ppermute | solution.py:133
  84.6 21.1 %collective-permute-start.15 = (bf16[4,16,2304]{2,1,0:T(8,128)(2,1)}, bf16[4,16,2304]{2,1,0:T(8,128)(2,1)S(1)}, u32[]{:S(2)}, u32[]{:S(2)}) collective-permute-start(bf16[4,16,2304]{2,1,0:T(8,128)(2,1)} %slice.841), channel_id=1, source_target_pairs={{0,4},{4,0},{8,12},{12,8},{1,5},{5,1},{9,13},{13,9},{2,6},{6,2},{1... | collective-permute-start | bytes 884744 | tf_op jit(solution)/shard_map/ppermute | solution.py:135
  90.2 27.6 %all-to-all-start.1 = ((f32[16,4,128]{2,1,0:T(4,128)}), f32[16,4,128]{2,1,0:T(4,128)S(1)}, u32[]{:S(2)}, u32[]{:S(2)}) async-start(f32[16,4,128]{2,1,0:T(4,128)} %broadcast_in_dim.24), calls=%async_computation.1 | async-start | bytes 65536 | tf_op jit(solution)/shard_map/all_to_all | solution.py:114
  97.1 27.0 %collective-permute-start.28 = (bf16[256,128]{1,0:T(8,128)(2,1)}, bf16[256,128]{1,0:T(8,128)(2,1)}, u32[]{:S(2)}, u32[]{:S(2)}) collective-permute-start(bf16[256,128]{1,0:T(8,128)(2,1)} %copy-done.116), channel_id=1, source_target_pairs={{0,1},{1,2},{2,3},{3,0},{4,5},{5,6},{6,7},{7,4},{8,9},{9,10},{10,1... | collective-permute-start | bytes 196616 | tf_op jit(solution)/shard_map/ppermute | solution.py:129
  103.3 29.1 %collective-permute-start.35 = (bf16[32,2304]{1,0:T(8,128)(2,1)}, bf16[32,2304]{1,0:T(8,128)(2,1)}, u32[]{:S(2)}, u32[]{:S(2)}) collective-permute-start(bf16[32,2304]{1,0:T(8,128)(2,1)} %collective-permute-done.34), channel_id=1, source_target_pairs={{0,1},{1,2},{2,3},{3,0},{4,5},{5,6},{6,7},{7,4},{8,9},{9,10},{10,1... | collective-permute-start | bytes 442376 | tf_op jit(solution)/shard_map/ppermute | solution.py:129
  126.2 56.7 %collective-permute-start.43 = (bf16[128,256]{1,0:T(8,128)(2,1)}, bf16[128,256]{1,0:T(8,128)(2,1)}, u32[]{:S(2)}, u32[]{:S(2)}) collective-permute-start(bf16[128,256]{1,0:T(8,128)(2,1)} %slice_select_fusion.10), channel_id=1, source_target_pairs={{0,1},{1,2},{2,3},{3,0},{4,5},{5,6},{6,7},{7,4},{8,9},{9,10},{10,1... | collective-permute-start | bytes 196616 | tf_op jit(solution)/shard_map/ppermute | solution.py:129
  127.9 37.6 %collective-permute-start.29 = (bf16[4,256,128]{2,1,0:T(8,128)(2,1)S(1)}, bf16[4,256,128]{2,1,0:T(8,128)(2,1)}, u32[]{:S(2)}, u32[]{:S(2)}) collective-permute-start(bf16[4,256,128]{2,1,0:T(8,128)(2,1)S(1)} %pad_maximum_fusion.11.refs_0_), channel_id=1, source_target_pairs={{0,4},{4,0},{8,12},{12,8},{1,5},{5,1},{9,13},{13,9},{2,6},{6,2},{1... | collective-permute-start | bytes 786440 | tf_op jit(solution)/shard_map/ppermute | solution.py:132
  132.5 35.9 %collective-permute-start.30 = (bf16[4,256,128]{2,1,0:T(8,128)(2,1)S(1)}, bf16[4,256,128]{2,1,0:T(8,128)(2,1)}, u32[]{:S(2)}, u32[]{:S(2)}) collective-permute-start(bf16[4,256,128]{2,1,0:T(8,128)(2,1)S(1)} %pad_maximum_fusion.11.refs_0_), channel_id=1, source_target_pairs={{0,8},{4,12},{8,0},{12,4},{1,9},{5,13},{9,1},{13,5},{2,10},{6,14},... | collective-permute-start | bytes 786440 | tf_op jit(solution)/shard_map/ppermute | solution.py:133
  134.1 36.7 %collective-permute-start.36 = (bf16[32,2304]{1,0:T(8,128)(2,1)}, bf16[32,2304]{1,0:T(8,128)(2,1)}, u32[]{:S(2)}, u32[]{:S(2)}) collective-permute-start(bf16[32,2304]{1,0:T(8,128)(2,1)} %collective-permute-done.35), channel_id=1, source_target_pairs={{0,1},{1,2},{2,3},{3,0},{4,5},{5,6},{6,7},{7,4},{8,9},{9,10},{10,1... | collective-permute-start | bytes 442376 | tf_op jit(solution)/shard_map/ppermute | solution.py:129
  201.5 21.4 %collective-permute-start.46 = (bf16[4,128,256]{2,1,0:T(8,128)(2,1)}, bf16[4,128,256]{2,1,0:T(8,128)(2,1)}, u32[]{:S(2)}, u32[]{:S(2)}) collective-permute-start(bf16[4,128,256]{2,1,0:T(8,128)(2,1)} %pad_maximum_fusion.12.refs_0_), channel_id=1, source_target_pairs={{0,4},{4,0},{8,12},{12,8},{1,5},{5,1},{9,13},{13,9},{2,6},{6,2},{1... | collective-permute-start | bytes 786440 | tf_op jit(solution)/shard_map/ppermute | solution.py:132
  203.4 21.6 %collective-permute-start.47 = (bf16[4,128,256]{2,1,0:T(8,128)(2,1)}, bf16[4,128,256]{2,1,0:T(8,128)(2,1)}, u32[]{:S(2)}, u32[]{:S(2)}) collective-permute-start(bf16[4,128,256]{2,1,0:T(8,128)(2,1)} %pad_maximum_fusion.12.refs_0_), channel_id=1, source_target_pairs={{0,8},{4,12},{8,0},{12,4},{1,9},{5,13},{9,1},{13,5},{2,10},{6,14},... | collective-permute-start | bytes 786440 | tf_op jit(solution)/shard_map/ppermute | solution.py:133
  291.4 26.2 %collective-permute-start.50 = (bf16[1,128,1024]{2,1,0:T(8,128)(2,1)}, bf16[1,128,1024]{2,1,0:T(8,128)(2,1)}, u32[]{:S(2)}, u32[]{:S(2)}) collective-permute-start(bf16[1,128,1024]{2,1,0:T(8,128)(2,1)} %get-tuple-element.128), channel_id=1, source_target_pairs={{0,16},{16,0},{1,17},{17,1},{2,18},{18,2},{3,19},{19,3},{4,20},{20... | collective-permute-start | bytes 786440 | tf_op jit(solution)/shard_map/ppermute | solution.py:82
  362.9 29.6 %all-to-all-start.21 = ((bf16[4,128,256]{2,1,0:T(8,128)(2,1)}), bf16[4,128,256]{2,1,0:T(8,128)(2,1)}, u32[]{:S(2)}, u32[]{:S(2)}) async-start(bf16[4,128,256]{2,1,0:T(8,128)(2,1)} %fusion.75), calls=%async_computation.21 | async-start | bytes 524288 | tf_op jit(solution)/shard_map/all_to_all | solution.py:192
  383.8 32.4 %collective-permute-start.77 = (bf16[4,128,128]{2,1,0:T(8,128)(2,1)}, bf16[4,128,128]{2,1,0:T(8,128)(2,1)}, u32[]{:S(2)}, u32[]{:S(2)}) collective-permute-start(bf16[4,128,128]{2,1,0:T(8,128)(2,1)} %get-tuple-element.138), channel_id=1, source_target_pairs={{0,4},{4,0},{8,12},{12,8},{1,5},{5,1},{9,13},{13,9},{2,6},{6,2},{1... | collective-permute-start | bytes 393224 | tf_op jit(solution)/shard_map/ppermute | solution.py:180
  390.8 72.5 %collective-permute-start.81 = (bf16[4,32,2304]{2,1,0:T(8,128)(2,1)}, bf16[4,32,2304]{2,1,0:T(8,128)(2,1)}, u32[]{:S(2)}, u32[]{:S(2)}) collective-permute-start(bf16[4,32,2304]{2,1,0:T(8,128)(2,1)} %pad_maximum_fusion.8), channel_id=1, source_target_pairs={{0,4},{4,0},{8,12},{12,8},{1,5},{5,1},{9,13},{13,9},{2,6},{6,2},{1... | collective-permute-start | bytes 1769480 | tf_op jit(solution)/shard_map/ppermute | solution.py:189
  398.4 65.0 %collective-permute-start.83 = (bf16[4,32,2304]{2,1,0:T(8,128)(2,1)}, bf16[4,32,2304]{2,1,0:T(8,128)(2,1)}, u32[]{:S(2)}, u32[]{:S(2)}) collective-permute-start(bf16[4,32,2304]{2,1,0:T(8,128)(2,1)} %pad_maximum_fusion.9), channel_id=1, source_target_pairs={{0,8},{4,12},{8,0},{12,4},{1,9},{5,13},{9,1},{13,5},{2,10},{6,14},... | collective-permute-start | bytes 1769480 | tf_op jit(solution)/shard_map/ppermute | solution.py:190
  399.8 55.8 %collective-permute-start.76 = (bf16[4,256,128]{2,1,0:T(8,128)(2,1)}, bf16[4,256,128]{2,1,0:T(8,128)(2,1)}, u32[]{:S(2)}, u32[]{:S(2)}) collective-permute-start(bf16[4,256,128]{2,1,0:T(8,128)(2,1)} %pad_maximum_fusion.13), channel_id=1, source_target_pairs={{0,4},{4,0},{8,12},{12,8},{1,5},{5,1},{9,13},{13,9},{2,6},{6,2},{1... | collective-permute-start | bytes 786440 | tf_op jit(solution)/shard_map/ppermute | solution.py:189
  417.9 39.8 %collective-permute-start.78 = (bf16[4,256,128]{2,1,0:T(8,128)(2,1)}, bf16[4,256,128]{2,1,0:T(8,128)(2,1)}, u32[]{:S(2)}, u32[]{:S(2)}) collective-permute-start(bf16[4,256,128]{2,1,0:T(8,128)(2,1)} %pad_maximum_fusion.14), channel_id=1, source_target_pairs={{0,8},{4,12},{8,0},{12,4},{1,9},{5,13},{9,1},{13,5},{2,10},{6,14},... | collective-permute-start | bytes 786440 | tf_op jit(solution)/shard_map/ppermute | solution.py:190
  457.6 89.9 %collective-permute-start.58 = (f32[256,4,128]{2,1,0:T(4,128)}, f32[256,4,128]{2,1,0:T(4,128)}, u32[]{:S(2)}, u32[]{:S(2)}) collective-permute-start(f32[256,4,128]{2,1,0:T(4,128)} %slice_select_fusion.1), channel_id=1, source_target_pairs={{0,16},{16,0},{1,17},{17,1},{2,18},{18,2},{3,19},{19,3},{4,20},{20... | collective-permute-start | bytes 1572872 | tf_op jit(solution)/shard_map/ppermute | solution.py:82
  501.5 36.0 %collective-permute-start.66 = (bf16[4,32,2304]{2,1,0:T(8,128)(2,1)}, bf16[4,32,2304]{2,1,0:T(8,128)(2,1)}, u32[]{:S(2)}, u32[]{:S(2)}) collective-permute-start(bf16[4,32,2304]{2,1,0:T(8,128)(2,1)} %pad_maximum_fusion.6), channel_id=1, source_target_pairs={{0,4},{4,0},{8,12},{12,8},{1,5},{5,1},{9,13},{13,9},{2,6},{6,2},{1... | collective-permute-start | bytes 1769480 | tf_op jit(solution)/shard_map/ppermute | solution.py:189
  509.9 27.5 %collective-permute-start.68 = (bf16[4,32,2304]{2,1,0:T(8,128)(2,1)}, bf16[4,32,2304]{2,1,0:T(8,128)(2,1)}, u32[]{:S(2)}, u32[]{:S(2)}) collective-permute-start(bf16[4,32,2304]{2,1,0:T(8,128)(2,1)} %pad_maximum_fusion.7), channel_id=1, source_target_pairs={{0,8},{4,12},{8,0},{12,4},{1,9},{5,13},{9,1},{13,5},{2,10},{6,14},... | collective-permute-start | bytes 1769480 | tf_op jit(solution)/shard_map/ppermute | solution.py:190
  523.4 37.2 %collective-permute-start.71 = (bf16[4,384,256]{2,1,0:T(8,128)(2,1)}, bf16[4,384,256]{2,1,0:T(8,128)(2,1)}, u32[]{:S(2)}, u32[]{:S(2)}) collective-permute-start(bf16[4,384,256]{2,1,0:T(8,128)(2,1)} %pad_maximum_fusion.2), channel_id=1, source_target_pairs={{0,4},{4,0},{8,12},{12,8},{1,5},{5,1},{9,13},{13,9},{2,6},{6,2},{1... | collective-permute-start | bytes 2359304 | tf_op jit(solution)/shard_map/ppermute | solution.py:189
  528.3 32.3 %collective-permute-start.73 = (bf16[4,384,256]{2,1,0:T(8,128)(2,1)}, bf16[4,384,256]{2,1,0:T(8,128)(2,1)}, u32[]{:S(2)}, u32[]{:S(2)}) collective-permute-start(bf16[4,384,256]{2,1,0:T(8,128)(2,1)} %pad_maximum_fusion.3), channel_id=1, source_target_pairs={{0,8},{4,12},{8,0},{12,4},{1,9},{5,13},{9,1},{13,5},{2,10},{6,14},... | collective-permute-start | bytes 2359304 | tf_op jit(solution)/shard_map/ppermute | solution.py:190
  563.2 23.1 %all-to-all-start.18 = ((bf16[4,384,256]{2,1,0:T(8,128)(2,1)}), bf16[4,384,256]{2,1,0:T(8,128)(2,1)S(1)}, u32[]{:S(2)}, u32[]{:S(2)}) async-start(bf16[4,384,256]{2,1,0:T(8,128)(2,1)} %fusion.5), calls=%async_computation.18 | async-start | bytes 1572864 | tf_op jit(solution)/shard_map/all_to_all | solution.py:192
  569.5 21.4 %collective-permute-start.90 = (f32[8,256]{1,0:T(8,128)S(1)}, f32[8,256]{1,0:T(8,128)S(1)}, u32[]{:S(2)}, u32[]{:S(2)}) collective-permute-start(f32[8,256]{1,0:T(8,128)S(1)} %reshape.1298), channel_id=1, source_target_pairs={{0,16},{16,0},{1,17},{17,1},{2,18},{18,2},{3,19},{19,3},{4,20},{20... | collective-permute-start | bytes 24584 | tf_op jit(solution)/shard_map/ppermute | solution.py:82
  586.3 28.2 %all-to-all-start.15 = ((bf16[4,512,256]{1,2,0:T(8,128)(2,1)}), bf16[4,512,256]{1,2,0:T(8,128)(2,1)S(1)}, u32[]{:S(2)}, u32[]{:S(2)}) async-start(bf16[4,512,256]{1,2,0:T(8,128)(2,1)} %fusion.58), calls=%async_computation.15 | async-start | bytes 2097152 | tf_op jit(solution)/shard_map/all_to_all | solution.py:123
  (306 other events, 2231.5 us)

commit v3 on v2

v3 whole, which is shorter than its diff:
```python
import math

import jax
import jax.numpy as jnp
from jax import lax
from jax.experimental import pallas as pl
from jax.experimental.pallas import tpu as pltpu
from jax.sharding import PartitionSpec as P

EPS = 1e-05
ROOT = math.sqrt(2.0 / math.pi)
CUBE = 0.044715
F32 = jnp.float32
BF16 = jnp.bfloat16
XS = [(k, k ^ 1) for k in range(4)]
YS = [(k, k ^ 2) for k in range(4)]
FAR = 3
GEO = 3
TAPS = [(p, r) for p in range(3) for r in range(3)]


def mm(left, right):
    return lax.dot_general(left, right, (((1,), (0,)), ((), ())), preferred_element_type=F32)


def mm_nt(left, right):
    return lax.dot_general(left, right, (((1,), (1,)), ((), ())), preferred_element_type=F32)


def mm_tn(left, right):
    return lax.dot_general(left, right, (((0,), (0,)), ((), ())), preferred_element_type=F32)


def gelu(v):
    return 0.5 * v * (1.0 + jnp.tanh(ROOT * (v + CUBE * v * v * v)))


def gelu_both(v):
    t = jnp.tanh(ROOT * (v + CUBE * v * v * v))
    half = 0.5 * (1.0 + t)
    return v * half, half + 0.5 * v * (1.0 - t * t) * (ROOT * (1.0 + 3.0 * CUBE * v * v))


def gelu_slope(v):
    return gelu_both(v)[1]


def halves(x, k):
    if k & (k - 1) == 0:
        s = k.bit_length() - 1
        return lax.shift_right_logical(x, jnp.int32(s)), lax.bitwise_and(x, jnp.int32(k - 1))
    return lax.div(x, jnp.int32(k)), lax.rem(x, jnp.int32(k))


def at(unit, index, size=None):
    return pl.ds(pl.multiple_of(index * unit, unit), unit if size is None else size)


def run(kernel, outs, smem, *arrays, scratch=(), flops=0, limit=40 << 20):
    shapes = [jax.ShapeDtypeStruct(s, d) for s, d in outs]
    moved = sum(a.size * a.dtype.itemsize for a in arrays)
    moved += sum(math.prod(s) * jnp.dtype(d).itemsize for s, d in outs)
    return pl.pallas_call(
        kernel,
        out_shape=shapes,
        in_specs=[pl.BlockSpec(memory_space=pltpu.SMEM)] * len(smem)
        + [pl.BlockSpec(memory_space=pltpu.VMEM)] * len(arrays),
        out_specs=[pl.BlockSpec(memory_space=pltpu.VMEM)] * len(outs),
        scratch_shapes=list(scratch),
        compiler_params=pltpu.CompilerParams(vmem_limit_bytes=limit),
        cost_estimate=pl.CostEstimate(flops=flops, bytes_accessed=moved, transcendentals=0),
    )(*smem, *arrays)


def shards(
    images,
    extents,
    first_reduce,
    first_taps,
    first_expand,
    first_shortcut,
    second_reduce,
    second_taps,
    second_expand,
    mid_gains,
    mid_shifts,
    wide_gains,
    wide_shifts,
    cotangent,
):
    nb = lax.axis_size("batch")
    ni = lax.axis_size("inner")
    no = lax.axis_size("outer")
    b = lax.axis_index("batch")
    i = lax.axis_index("inner")
    o = lax.axis_index("outer")
    c = b % 2
    img_dev, hi, wi, in_part = images.shape
    ho, wo = hi // 2, wi // 2
    out_part = cotangent.shape[3]
    m = img_dev // no
    pair = 2 * m
    cin, cout = hi * wi, ho * wo
    rin, rout = pair * cin, pair * cout
    mid = mid_gains.shape[1]
    mh = mid // 2
    in_h = in_part // 2
    out_h = out_part // 2
    kin = no * in_h
    wide = no * out_h
    mid_i = mid // ni
    mid_io = mid // (ni * no)
    peers = ni * no
    lanes = out_h

    def core_swap(x):
        return lax.ppermute(x, "batch", [(k, k ^ 1) for k in range(nb)])

    def pick(low, high):
        return jnp.where(c == 0, low, high)

    def mine(x, axis):
        h = x.shape[axis] // 2
        return pick(lax.slice_in_dim(x, 0, h, axis=axis), lax.slice_in_dim(x, h, 2 * h, axis=axis))

    def other(x, axis):
        h = x.shape[axis] // 2
        return pick(lax.slice_in_dim(x, h, 2 * h, axis=axis), lax.slice_in_dim(x, 0, h, axis=axis))

    def swap_full(x, axis):
        recv = core_swap(x)
        return pick(jnp.concatenate([x, recv], axis), jnp.concatenate([recv, x], axis))

    def over_batch(x):
        total = x
        for k in range(1, nb // 2):
            total = total + lax.ppermute(x, "batch", [(j, (j + 2 * k) % nb) for j in range(nb)])
        return total

    def sync(copies):
        got = lax.all_to_all(copies, ("inner", "outer"), split_axis=0, concat_axis=0, tiled=True)
        return got if nb == 2 else over_batch(jnp.sum(got, 0, keepdims=True))

    def to_images(x):
        return lax.all_to_all(x, "outer", split_axis=0, concat_axis=0, tiled=True)

    def taps_entries(first, w):
        def entry(tap):
            place = lambda pi, po: (pi * no + po, mid_io, 0, tap, mh)
            return (first + tap * mid_io, mid_io, 0, mh, w, place)

        return [entry(tap) for tap in range(9)], 9 * mid_io

    def up_entries(first, w):
        place = lambda pi, po: (pi, mid_i, 0, po, out_h)
        return [(first, mid_i, 0, out_h, w, place)], mid_i

    def short_entries(first, w):
        place = lambda pi, po: (po, in_part, 0, pi, out_h)
        return [(first, in_part, 0, out_h, w, place)], in_part

    def down_entries(rows):
        def make(first, w):
            half = rows // 2

            def entry(side):
                place = lambda pi, po: (po, rows, side * half, pi, mid_i)
                return (first, half, side * mid_i, mid_i, w, place)

            return [entry(0), entry(1)], half

        return make

    def table(makers):
        entries, first = [], 0
        for w, make in enumerate(makers):
            got, used = make(first, w)
            entries += got
            first += used
        return entries, first

    def cuts(entries, lo, hi_row):
        for first, count, lane, width, w, place in entries:
            a, z = max(lo, first), min(hi_row, first + count)
            if a < z:
                yield a, z, a - first, lane, width, w, place

    def spans(rows):
        h = rows // 2
        return [(0, 0, rows), (1, 0, rows), (2, 0, rows), (FAR, 0, h), (FAR, h, rows)]

    def region(place, pi, po, offset, count, width):
        row, row_unit, plus, col, col_unit = place(pi, po)
        return (
            pl.ds(pl.multiple_of(row * row_unit, row_unit) + (plus + offset), count),
            pl.ds(pl.multiple_of(col * col_unit, col_unit), width),
        )

    place_io = jnp.stack([i, o]).astype(jnp.int32)

    def gather(shard, makers, shapes):
        entries, rows = table(makers)
        ring = [(k, (k + 1) % no) for k in range(no)]
        pieces = [shard]
        for _ in range(1, no):
            pieces.append(lax.ppermute(pieces[-1], "outer", ring))
        whole = jnp.stack(pieces)
        h = rows // 2
        by_x = lax.ppermute(whole, "inner", XS)
        by_y = lax.ppermute(whole, "inner", YS)
        low = lax.ppermute(by_x[:, :h], "inner", YS)
        high = lax.ppermute(by_y[:, h:], "inner", XS)

        def kernel(where, *refs):
            sources, targets = refs[:5], refs[5:]
            for src, (far, lo, hi_row) in enumerate(spans(rows)):
                for d in range(no):
                    pi, po = where[0] ^ far, lax.rem(where[1] + (no - d), no)
                    for a, z, offset, lane, width, w, place in cuts(entries, lo, hi_row):
                        targets[w][region(place, pi, po, offset, z - a, width)] = sources[src][
                            d, a - lo : z - lo, lane : lane + width
                        ]

        return run(
            kernel, [(s, BF16) for s in shapes], [place_io], whole, by_x, by_y, low, high
        )

    def blocks_of(products, makers, operands):
        entries, rows = table(makers)
        h = rows // 2
        shapes = [prod[0] for prod in products]

        def kernel(where, *refs):
            ins, outs = refs[: len(operands)], refs[len(operands) : len(operands) + 5]
            grads = refs[len(operands) + 5 :]
            for grad, (shape, left, right) in zip(grads, products, strict=True):
                grad[...] = mm_tn(ins[left][...], ins[right][...]).astype(BF16)
            for dst, (far, lo, hi_row) in enumerate(spans(rows)):
                for po in range(no):
                    pi = where[0] ^ far
                    for a, z, offset, lane, width, w, place in cuts(entries, lo, hi_row):
                        outs[dst][po, a - lo : z - lo, lane : lane + width] = grads[w][
                            region(place, pi, po, offset, z - a, width)
                        ]

        sizes = [rows, rows, rows, h, rows - h]
        return run(
            kernel,
            [((no, r, lanes), BF16) for r in sizes],
            [place_io],
            *operands,
            scratch=[pltpu.VMEM(s, BF16) for s in shapes],
        )

    def scatter(own, to_x, to_y, low, high):
        h = low.shape[1]
        got_low = lax.ppermute(low, "inner", XS)
        got_high = lax.ppermute(high, "inner", YS)

        def first(x, y, a, z, out_x, out_y):
            out_x[:, :h] = x[:, :h]
            out_x[:, h:] = (x[:, h:].astype(F32) + z[...].astype(F32)).astype(BF16)
            out_y[:, :h] = (y[:, :h].astype(F32) + a[...].astype(F32)).astype(BF16)
            out_y[:, h:] = y[:, h:]

        to_x, to_y = run(first, [(own.shape, BF16)] * 2, [], to_x, to_y, got_low, got_high)
        by_x = lax.ppermute(to_x, "inner", XS)
        by_y = lax.ppermute(to_y, "inner", YS)

        def second(x, y, z, out):
            out[...] = (
                x[...].astype(F32) + y[...].astype(F32) + z[...].astype(F32)
            ).astype(BF16)

        (summed,) = run(second, [(own.shape, BF16)], [], own, by_x, by_y)
        parts = to_images(summed)
        return over_batch(jnp.sum(parts.astype(F32), axis=0))

    first_img = ((b - c) * ni + i) * img_dev + o * m
    ext = jnp.concatenate(
        [
            lax.dynamic_slice_in_dim(extents, first_img, m, 0),
            lax.dynamic_slice_in_dim(extents, first_img + ni * img_dev, m, 0),
        ],
        0,
    )
    geo = jnp.concatenate([jnp.stack([i, o, c]), ext[:, 0], ext[:, 1]]).astype(jnp.int32)
    area = jnp.sum(extents[:, 0] * extents[:, 1]).astype(F32)
    counts = jnp.stack([4.0 * area, area])

    def iota(shape, axis):
        return lax.broadcasted_iota(jnp.int32, shape, axis)

    def out_mask(geo):
        row, col = halves(iota((cout, 1), 0), wo)
        return jnp.concatenate(
            [
                ((row < geo[GEO + k]) & (col < geo[GEO + pair + k])).astype(F32)
                for k in range(pair)
            ],
            0,
        )

    def phase_cells(shape, axis):
        phase, cell = halves(iota(shape, axis), cout)
        row, col = halves(cell, wo)
        up, left = halves(phase, 2)
        return 2 * row + up, 2 * col + left

    def in_mask(geo):
        row, col = phase_cells((cin, 1), 0)
        return jnp.concatenate(
            [
                ((row < 2 * geo[GEO + k]) & (col < 2 * geo[GEO + pair + k])).astype(F32)
                for k in range(pair)
            ],
            0,
        )

    def order(geo, k, axis):
        shape = (cin, 1) if axis == 0 else (1, cin)
        row, col = phase_cells(shape, axis)
        inside = (row < 2 * geo[GEO + k]) & (col < 2 * geo[GEO + pair + k])
        source = jnp.where(inside, row * wi + col, -1)
        return (source == iota((cin, cin), 1 - axis)).astype(F32).astype(BF16)

    def shift(dr, dc):
        row, col = halves(iota((cout, 1), 0), wo)
        row, col = row + dr, col + dc
        inside = (row >= 0) & (row < ho) & (col >= 0) & (col < wo)
        source = jnp.where(inside, row * wo + col, -1)
        return (source == iota((cout, cout), 1)).astype(F32).astype(BF16)

    def taps_shard(w):
        return mine(w, 2).transpose(0, 1, 3, 2).reshape(9 * mid_io, mh)

    def side_by_side(w):
        h = w.shape[0] // 2
        return jnp.concatenate([w[:h], w[h:]], 1)

    got_in = to_images(images.reshape(img_dev, cin, in_part)).reshape(no, m, cin, in_part)
    make_r1, make_r2 = down_entries(in_h), down_entries(out_h)
    shape_t = (mid, 9 * mh)
    (w_r1,) = gather(side_by_side(mine(first_reduce, 0)), [make_r1], [(kin, mid)])
    (w_t1,) = gather(taps_shard(first_taps), [taps_entries], [shape_t])
    w_e1, w_s = gather(
        jnp.concatenate([mine(first_expand, 1), mine(first_shortcut, 1)], 0),
        [up_entries, short_entries],
        [(mid, wide), (no * in_part, wide)],
    )
    w_r2, w_t2, w_e2 = gather(
        jnp.concatenate(
            [
                side_by_side(mine(second_reduce, 0)),
                taps_shard(second_taps),
                mine(second_expand, 1),
            ],
            0,
        ),
        [make_r2, taps_entries, up_entries],
        [(wide, mid), shape_t, (mid, wide)],
    )

    pm = mine(jnp.concatenate([mid_gains, mid_shifts], 0), 1)
    pw = mine(
        jnp.concatenate([wide_gains, wide_shifts], 0).reshape(6, no, out_part), 2
    ).reshape(6, wide)

    def moments(got, counts, which, row=0):
        total = jnp.sum(got[...], 0)
        mean = total[row : row + 1] / counts[which]
        square = total[row + 1 : row + 2] / counts[which]
        return mean, lax.rsqrt(square - mean * mean + EPS)

    def send_all(copies, rows):
        value = jnp.concatenate(rows, 0)
        for k in range(peers):
            copies[k] = value

    def sums(z, valid=None):
        zv = z if valid is None else z * valid
        return [jnp.sum(zv, 0, keepdims=True), jnp.sum(zv * z, 0, keepdims=True)]

    def copies_shape(rows, width):
        return ((peers, rows, width), F32)

    mid_f = ((rout, mh), F32)
    wide_f = ((rout, wide), F32)
    wide_b = ((rout, wide), BF16)
    mid_b = ((rout, mh), BF16)

    swap_in = core_swap(other(got_in, 3))

    def one_kernel(geo, got, recv, w, masked, own, oth, raw):
        me = geo[2]
        for k in range(m):
            for j in range(no):
                at_lane = slice(j * in_h, (j + 1) * in_h)
                raw[me * m + k, :, at_lane] = got[j, k, :, at(in_h, me)]
                raw[(1 - me) * m + k, :, at_lane] = recv[j, k]
        for k in range(pair):
            rows = slice(k * cin, (k + 1) * cin)
            masked[rows, :] = mm(order(geo, k, 0), raw[k]).astype(BF16)
        own[...] = mm(masked[...], w[:, at(mh, me)])
        oth[...] = mm(masked[...], w[:, at(mh, 1 - me)])

    masked, z_own, z_oth = run(
        one_kernel,
        [((rin, kin), BF16), ((rin, mh), F32), ((rin, mh), F32)],
        [geo],
        got_in,
        swap_in,
        w_r1,
        scratch=[pltpu.VMEM((pair, cin, kin), BF16)],
    )

    def one_sums(x, y, z, copies):
        z[...] = x[...] + y[...]
        send_all(copies, sums(z[...]))

    z_one, copies = run(
        one_sums, [((rin, mh), F32), copies_shape(2, mh)], [], z_own, core_swap(z_oth)
    )
    got_one = sync(copies)

    def mid_sums(geo, x, y, z, copies):
        z[...] = x[...] + y[...]
        send_all(copies, sums(z[...], out_mask(geo)))

    def mid_partial(kernel, z, got, w):
        win, own, oth = run(
            kernel,
            [((rout, 9 * mh), BF16), mid_f, mid_f],
            [geo, counts],
            z,
            got,
            pm,
            w,
            scratch=[pltpu.VMEM(z.shape, BF16)],
        )
        z_next, copies = run(
            mid_sums, [mid_f, copies_shape(2, mh)], [geo], own, core_swap(oth)
        )
        return win, z_next, sync(copies)

    def normed(z, st, gains, g, s):
        return (z - st[0]) * st[1] * gains[g : g + 1] + gains[s : s + 1]

    def two_kernel(geo, counts, z, got, pm, w, win, own, oth, act):
        st = moments(got, counts, 0)
        act[...] = (gelu(normed(z[...], st, pm, 0, 4)) * in_mask(geo)).astype(BF16)
        moves = {}
        for tap, (p, r) in enumerate(TAPS):
            key = (-int(p == 0), -int(r == 0))
            plane = 2 * int(p != 1) + int(r != 1)
            if key != (0, 0) and key not in moves:
                moves[key] = shift(*key)
            for k in range(pair):
                x = act[k * cin + plane * cout : k * cin + (plane + 1) * cout, :]
                if key != (0, 0):
                    x = mm(moves[key], x).astype(BF16)
                win[k * cout : (k + 1) * cout, tap * mh : (tap + 1) * mh] = x
        own[...] = mm_nt(win[...], w[at(mh, geo[2]), :])
        oth[...] = mm_nt(win[...], w[at(mh, 1 - geo[2]), :])

    win_one, z_two, got_two = mid_partial(two_kernel, z_one, got_one, w_t1)

    strided_h = masked.reshape(pair, cin, kin)[:, :cout].reshape(rout, kin)
    strided_r = core_swap(strided_h)

    def short_kernel(geo, x, y, w, full, z):
        me = geo[2]
        for j in range(no):
            part = slice(j * in_h, (j + 1) * in_h)
            full[:, pl.ds(pl.multiple_of(j * in_part + me * in_h, in_h), in_h)] = x[:, part]
            full[:, pl.ds(pl.multiple_of(j * in_part + (1 - me) * in_h, in_h), in_h)] = y[:, part]
        z[...] = mm(full[...], w[...])

    strided, z_short = run(
        short_kernel, [((rout, no * in_part), BF16), wide_f], [geo], strided_h, strided_r, w_s
    )

    def act_of(row, z, got):
        def kernel(geo, counts, z, got, pm, act):
            st = moments(got, counts, 1)
            act[...] = (gelu(normed(z[...], st, pm, row, row + 4)) * out_mask(geo)).astype(BF16)

        (act,) = run(kernel, [mid_b], [geo, counts], z, got, pm)
        return act, core_swap(act)

    def join_to(full, geo, x, y):
        full[:, at(mh, geo[2])] = x[...]
        full[:, at(mh, 1 - geo[2])] = y[...]

    def three_kernel(geo, x, y, w, zs, full, z, copies):
        join_to(full, geo, x, y)
        z[...] = mm(full[...], w[...])
        send_all(copies, sums(z[...]) + sums(zs[...]))

    act_own, act_recv = act_of(1, z_two, got_two)
    act_two, z_three, copies = run(
        three_kernel,
        [((rout, mid), BF16), wide_f, copies_shape(4, wide)],
        [geo],
        act_own,
        act_recv,
        w_e1,
        z_short,
    )
    got_three = sync(copies)

    def four_kernel(geo, counts, z3, zs, got, pw, w, hidden, slope, low, own, oth):
        st3, sts = moments(got, counts, 1), moments(got, counts, 1, 2)
        joined = normed(z3[...], st3, pw, 0, 3) + normed(zs[...], sts, pw, 1, 4)
        value, rise = gelu_both(joined)
        valid = out_mask(geo)
        hidden[...] = value * valid
        slope[...] = rise * valid
        low[...] = hidden[...].astype(BF16)
        own[...] = mm(low[...], w[:, at(mh, geo[2])])
        oth[...] = mm(low[...], w[:, at(mh, 1 - geo[2])])

    hidden, slope_one, hidden_low, z_own, z_oth = run(
        four_kernel,
        [wide_f, wide_f, wide_b, mid_f, mid_f],
        [geo, counts],
        z_three,
        z_short,
        got_three,
        pw,
        w_r2,
    )
    z_four, copies = run(
        mid_sums, [mid_f, copies_shape(2, mh)], [geo], z_own, core_swap(z_oth)
    )
    got_four = sync(copies)

    def five_kernel(geo, counts, z, got, pm, w, win, own, oth, act):
        st = moments(got, counts, 1)
        act[...] = (gelu(normed(z[...], st, pm, 2, 6)) * out_mask(geo)).astype(BF16)
        for tap, (p, r) in enumerate(TAPS):
            key = (p - 1, r - 1)
            move = None if key == (0, 0) else shift(*key)
            for k in range(pair):
                x = act[k * cout : (k + 1) * cout, :]
                if move is not None:
                    x = mm(move, x).astype(BF16)
                win[k * cout : (k + 1) * cout, tap * mh : (tap + 1) * mh] = x
        own[...] = mm_nt(win[...], w[at(mh, geo[2]), :])
        oth[...] = mm_nt(win[...], w[at(mh, 1 - geo[2]), :])

    win_two, z_five, got_five = mid_partial(five_kernel, z_four, got_four, w_t2)
    act_own, act_recv = act_of(3, z_five, got_five)

    def six_kernel(geo, x, y, w, full, z, copies):
        join_to(full, geo, x, y)
        z[...] = mm(full[...], w[...])
        send_all(copies, sums(z[...]))

    act_five, z_six, copies = run(
        six_kernel,
        [((rout, mid), BF16), wide_f, copies_shape(2, wide)],
        [geo],
        act_own,
        act_recv,
        w_e2,
    )
    got_six = sync(copies)

    got_cot = to_images(cotangent.reshape(img_dev, cout, out_part)).reshape(
        no, m, cout, out_part
    )
    swap_cot = core_swap(other(got_cot, 3))

    def loss_kernel(geo, counts, z, got, pw, hidden, cot, recv, own, oth, dy, copies, value):
        me = geo[2]
        st = moments(got, counts, 1)
        xhat = (z[...] - st[0]) * st[1]
        out, rise = gelu_both(xhat * pw[2:3] + pw[5:6] + hidden[...])
        valid = out_mask(geo)
        value[...] = (out * valid).astype(BF16)
        own[...] = value[at(m * cout, me), :]
        oth[...] = value[at(m * cout, 1 - me), :]
        for k in range(m):
            for j in range(no):
                part = slice(j * out_h, (j + 1) * out_h)
                dy[at(cout, me * m + k), part] = cot[j, k, :, at(out_h, me)].astype(F32)
                dy[at(cout, (1 - me) * m + k), part] = recv[j, k].astype(F32)
        dy[...] = dy[...] * (rise * valid)
        send_all(copies, dy_sums(dy[...], xhat))

    def dy_sums(dy, *xhats):
        return [jnp.sum(dy, 0, keepdims=True)] + [
            jnp.sum(dy * x, 0, keepdims=True) for x in xhats
        ]

    out_own, out_oth, dy_six, copies = run(
        loss_kernel,
        [((m * cout, wide), BF16), ((m * cout, wide), BF16), wide_f, copies_shape(2, wide)],
        [geo, counts],
        z_six,
        got_six,
        pw,
        hidden,
        got_cot,
        swap_cot,
        scratch=[pltpu.VMEM((rout, wide), BF16)],
    )
    got_g6 = sync(copies)

    def home(own, recv, cells, part_h):
        def kernel(geo, x, y, out):
            for k in range(m):
                rows = slice(k * cells, (k + 1) * cells)
                for j in range(no):
                    part = slice(j * part_h, (j + 1) * part_h)
                    out[j, k, :, at(part_h, geo[2])] = x[rows, part]
                    out[j, k, :, at(part_h, 1 - geo[2])] = y[rows, part]

        (full,) = run(kernel, [((no, m, cells, 2 * part_h), BF16)], [geo], own, recv)
        return to_images(full.reshape(img_dev, cells, 2 * part_h))

    block_output = home(out_own, core_swap(out_oth), cout, out_h).reshape(
        img_dev, ho, wo, out_part
    )

    def back(dy, xhat, gain, st, valid, total, row, shift_row, count):
        shift_sum, gain_sum = total[shift_row : shift_row + 1], total[row : row + 1]
        return (
            gain * st[1] * (dy - valid * ((shift_sum + xhat * gain_sum) / count))
        ).astype(BF16)

    def back_six(geo, counts, dy, z, got, grads, pw, w, dz, own, oth, total):
        st = moments(got, counts, 1)
        total[...] = jnp.sum(grads[...], 0)
        xhat = (z[...] - st[0]) * st[1]
        dz[...] = back(dy[...], xhat, pw[2:3], st, out_mask(geo), total, 1, 0, counts[1])
        own[...] = mm_nt(dz[...], w[at(mh, geo[2]), :])
        oth[...] = mm_nt(dz[...], w[at(mh, 1 - geo[2]), :])

    dz_six, da_own, da_oth, sum_six = run(
        back_six,
        [wide_b, mid_f, mid_f, ((2, wide), F32)],
        [geo, counts],
        dy_six,
        z_six,
        got_six,
        got_g6,
        pw,
        w_e2,
    )

    def mid_dy(row, own, recv, z, got):
        def kernel(geo, counts, x, y, z, got, pm, dy, copies):
            st = moments(got, counts, 1)
            xhat = (z[...] - st[0]) * st[1]
            rise = gelu_slope(xhat * pm[row : row + 1] + pm[row + 4 : row + 5])
            dy[...] = (x[...] + y[...]) * (out_mask(geo) * rise)
            send_all(copies, dy_sums(dy[...], xhat))

        dy, copies = run(
            kernel, [mid_f, copies_shape(2, mh)], [geo, counts], own, recv, z, got, pm
        )
        return dy, sync(copies)

    def mid_dz(row, dy, z, got, grads):
        which = 0 if row == 0 else 1

        def kernel(geo, counts, dy, z, got, grads, pm, dz, total):
            st = moments(got, counts, which)
            total[...] = jnp.sum(grads[...], 0)
            xhat = (z[...] - st[0]) * st[1]
            valid = in_mask(geo) if row == 0 else out_mask(geo)
            dz[...] = back(
                dy[...], xhat, pm[row : row + 1], st, valid, total, 1, 0, counts[which]
            )

        dz, total = run(
            kernel, [(z.shape, BF16), ((2, mh), F32)], [geo, counts], dy, z, got, grads, pm
        )
        return dz, core_swap(dz), total

    dy_five, got_g5 = mid_dy(3, da_own, core_swap(da_oth), z_five, got_five)
    dz_own, dz_recv, sum_five = mid_dz(3, dy_five, z_five, got_five, got_g5)

    def four_dy(geo, counts, x, y, z, got, pm, w, full, dy, copies, moved):
        join_to(full, geo, x, y)
        total = None
        for tap, (p, r) in enumerate(TAPS):
            key = (1 - p, 1 - r)
            if key == (0, 0):
                left = full[...]
            else:
                move = shift(*key)
                for k in range(pair):
                    rows = slice(k * cout, (k + 1) * cout)
                    moved[rows, :] = mm(move, full[rows, :]).astype(BF16)
                left = moved[...]
            term = mm(left, w[:, tap * mh : (tap + 1) * mh])
            total = term if total is None else total + term
        st = moments(got, counts, 1)
        xhat = (z[...] - st[0]) * st[1]
        dy[...] = total * (out_mask(geo) * gelu_slope(xhat * pm[2:3] + pm[6:7]))
        send_all(copies, dy_sums(dy[...], xhat))

    dz_five, dy_four, copies = run(
        four_dy,
        [((rout, mid), BF16), mid_f, copies_shape(2, mh)],
        [geo, counts],
        dz_own,
        dz_recv,
        z_four,
        got_four,
        pm,
        w_t2,
        scratch=[pltpu.VMEM((rout, mid), BF16)],
    )
    got_g4 = sync(copies)
    dz_own, dz_recv, sum_four = mid_dz(2, dy_four, z_four, got_four, got_g4)

    def joined_dy(geo, counts, x, y, w, dy6, slope, z3, zs, got, full, dy, copies):
        join_to(full, geo, x, y)
        dy[...] = (dy6[...] + mm_nt(full[...], w[...])) * slope[...]
        st3, sts = moments(got, counts, 1), moments(got, counts, 1, 2)
        send_all(
            copies,
            dy_sums(dy[...], (z3[...] - st3[0]) * st3[1], (zs[...] - sts[0]) * sts[1]),
        )

    dz_four, dy_joined, copies = run(
        joined_dy,
        [((rout, mid), BF16), wide_f, copies_shape(3, wide)],
        [geo, counts],
        dz_own,
        dz_recv,
        w_r2,
        dy_six,
        slope_one,
        z_three,
        z_short,
        got_three,
    )
    got_g3 = sync(copies)
    grads_second = scatter(
        *blocks_of(
            [((wide, mid), 0, 1), (shape_t, 2, 3), ((mid, wide), 4, 5)],
            [make_r2, taps_entries, up_entries],
            [hidden_low, dz_four, dz_five, win_two, act_five, dz_six],
        )
    )

    def back_three(geo, counts, dy, z3, zs, got, grads, pw, w, dz3, dzs, own, oth, total):
        st3, sts = moments(got, counts, 1), moments(got, counts, 1, 2)
        total[...] = jnp.sum(grads[...], 0)
        valid = out_mask(geo)
        x3, xs = (z3[...] - st3[0]) * st3[1], (zs[...] - sts[0]) * sts[1]
        dz3[...] = back(dy[...], x3, pw[0:1], st3, valid, total, 1, 0, counts[1])
        dzs[...] = back(dy[...], xs, pw[1:2], sts, valid, total, 2, 0, counts[1])
        own[...] = mm_nt(dz3[...], w[at(mh, geo[2]), :])
        oth[...] = mm_nt(dz3[...], w[at(mh, 1 - geo[2]), :])

    dz_three, dz_short, da_own, da_oth, sum_three = run(
        back_three,
        [wide_b, wide_b, mid_f, mid_f, ((3, wide), F32)],
        [geo, counts],
        dy_joined,
        z_three,
        z_short,
        got_three,
        got_g3,
        pw,
        w_e1,
    )
    dy_two, got_g2 = mid_dy(1, da_own, core_swap(da_oth), z_two, got_two)
    grads_es = scatter(
        *blocks_of(
            [((mid, wide), 0, 1), ((no * in_part, wide), 2, 3)],
            [up_entries, short_entries],
            [act_two, dz_three, strided, dz_short],
        )
    )

    def short_back(geo, dz, w, own, oth):
        me = geo[2]
        for j in range(no):
            part = slice(j * in_h, (j + 1) * in_h)
            rows = pl.ds(pl.multiple_of(j * in_part + me * in_h, in_h), in_h)
            own[:, part] = mm_nt(dz[...], w[rows, :])
            rows = pl.ds(pl.multiple_of(j * in_part + (1 - me) * in_h, in_h), in_h)
            oth[:, part] = mm_nt(dz[...], w[rows, :])

    ds_own, ds_oth = run(short_back, [((rout, kin), F32)] * 2, [geo], dz_short, w_s)
    ds_recv = core_swap(ds_oth)
    dz_own, dz_recv, sum_two = mid_dz(1, dy_two, z_two, got_two, got_g2)

    def one_dy(geo, counts, x, y, z, got, pm, w, full, dy, copies, moved):
        join_to(full, geo, x, y)
        for n, key in enumerate([(0, 1), (1, 0), (1, 1)]):
            move = shift(*key)
            for k in range(pair):
                rows = slice(k * cout, (k + 1) * cout)
                moved[n, rows, :] = mm(move, full[rows, :]).astype(BF16)
        for plane in range(4):
            total = None
            for p in (1,) if plane < 2 else (0, 2):
                for r in (1,) if plane % 2 == 0 else (0, 2):
                    n = 2 * int(p == 0) + int(r == 0)
                    left = full[...] if n == 0 else moved[n - 1]
                    tap = 3 * p + r
                    term = mm(left, w[:, tap * mh : (tap + 1) * mh])
                    total = term if total is None else total + term
            for k in range(pair):
                dy[k * cin + plane * cout : k * cin + (plane + 1) * cout, :] = total[
                    k * cout : (k + 1) * cout
                ]
        st = moments(got, counts, 0)
        xhat = (z[...] - st[0]) * st[1]
        dy[...] = dy[...] * (in_mask(geo) * gelu_slope(xhat * pm[0:1] + pm[4:5]))
        send_all(copies, dy_sums(dy[...], xhat))

    dz_two, dy_one, copies = run(
        one_dy,
        [((rout, mid), BF16), ((rin, mh), F32), copies_shape(2, mh)],
        [geo, counts],
        dz_own,
        dz_recv,
        z_one,
        got_one,
        pm,
        w_t1,
        scratch=[pltpu.VMEM((3, rout, mid), BF16)],
    )
    got_g1 = sync(copies)
    grads_t1 = scatter(*blocks_of([(shape_t, 0, 1)], [taps_entries], [dz_two, win_one]))
    dz_own, dz_recv, sum_one = mid_dz(0, dy_one, z_one, got_one, got_g1)

    def images_kernel(geo, x, y, w, ds, dr, full, own, oth, rows_in):
        join_to(full, geo, x, y)
        me = geo[2]
        for k in range(pair):
            rows = slice(k * cin, (k + 1) * cin)
            first = slice(k * cin, k * cin + cout)
            rest = slice(k * cin + cout, (k + 1) * cin)
            outs = slice(k * cout, (k + 1) * cout)
            rows_in[first, :] = (
                mm_nt(full[first, :], w[...]) + (ds[outs, :] + dr[outs, :])
            ).astype(BF16)
            rows_in[rest, :] = mm_nt(full[rest, :], w[...]).astype(BF16)
        for k in range(m):
            rows = slice(k * cin, (k + 1) * cin)
            for ref, img in ((oth, (1 - me) * m + k), (own, me * m + k)):
                ref[rows, :] = mm(order(geo, img, 1), rows_in[at(cin, img), :]).astype(BF16)

    dz_one, d_own, d_oth = run(
        images_kernel,
        [((rin, mid), BF16), ((m * cin, kin), BF16), ((m * cin, kin), BF16)],
        [geo],
        dz_own,
        dz_recv,
        w_r1,
        ds_own,
        ds_recv,
        scratch=[pltpu.VMEM((rin, kin), BF16)],
    )
    grad_images = home(d_own, core_swap(d_oth), cin, in_h).astype(F32).reshape(images.shape)
    grads_r1 = scatter(*blocks_of([((kin, mid), 0, 1)], [make_r1], [masked, dz_one]))

    def stacked(x):
        w = x.shape[1] // 2
        return jnp.concatenate([x[:, :w], x[:, w:]], 0)

    def taps_out(rows):
        both = swap_full(rows.reshape(9, mid_io, mh), 2)
        return both.transpose(0, 2, 1).reshape(first_taps.shape)

    rows_r2, rows_t = out_h // 2, 9 * mid_io
    grad_e1_s = swap_full(grads_es, 1)
    mids = jnp.stack([sum_one, sum_two, sum_four, sum_five], 1)
    mids = swap_full(mids, 2)
    wides = jnp.concatenate([sum_three, sum_six], 0).reshape(5, no, out_h)
    wides = swap_full(wides, 2).reshape(5, no * out_part)
    return (
        block_output,
        grad_images,
        swap_full(stacked(grads_r1), 0),
        taps_out(grads_t1),
        grad_e1_s[:mid_i],
        grad_e1_s[mid_i:],
        swap_full(stacked(grads_second[:rows_r2]), 0),
        taps_out(grads_second[rows_r2 : rows_r2 + rows_t]),
        swap_full(grads_second[rows_r2 + rows_t :], 1),
        mids[1],
        mids[0],
        jnp.stack([wides[1], wides[2], wides[4]]),
        jnp.stack([wides[0], wides[0], wides[3]]),
    )


def solution(mesh):
    wide = P(("batch", "inner"), None, None, "outer")
    down = P("outer", "inner")
    up = P("inner", "outer")
    taps = P(None, None, None, ("inner", "outer"))
    whole = P()
    return jax.shard_map(
        shards,
        mesh=mesh,
        in_specs=(wide, whole, down, taps, up, down, down, taps, up)
        + (whole, whole, whole, whole, wide),
        out_specs=(wide, wide, down, taps, up, down, down, taps, up, whole, whole, whole, whole),
        check_vma=False,
    )
```

time: 629 us -> 555 us (0.88)
  other arithmetic: 119 us -> 20.6 us
  blocking collectives: 0 us -> 76 us
  waiting for transfers between devices: 130 us -> 203 us
  starting transfers between devices: 186 us -> 114 us
  local copies, waits for them, and re-layouts: 122 us -> 58.7 us
  Pallas kernels: 6.52 us -> 69.2 us
  matrix products: 46.8 us -> 0 us
    ppermute x66 -> x44, waiting for transfers between devices: 46.5 us -> 127 us  [the longest x4 47.3 us: gather(): low = lax.ppermute(by_x[:, :h], 'inner', YS)]
    all_to_all x0 -> x7, blocking collectives: none -> 76 us  [sync(): lax.all_to_all(copies, ('inner', 'outer'), split_axis=0, concat_axis=0, t...]
    all_to_all x18 -> x5, starting transfers between devices: 85.9 us -> 18.4 us  [sync(): lax.all_to_all(copies, ('inner', 'outer'), split_axis=0, concat_axis=0, t...]
    pallas_call x6 -> x45, Pallas kernels: 6.52 us -> 69.2 us  [run(): pl.pallas_call(kernel, out_shape=shapes, in_specs=[pl.BlockSpec(memory_sp...]
    dot_general x63 -> x0, matrix products: 46.8 us -> none  [the longest x23 12.3 us: mm(): return jnp.dot(left, right, preferred_element_type=F32)]
    convert_element_type x30 -> x0, other arithmetic: 33.7 us -> none  [the longest x6 12.2 us: scatter_blocks(): mine_i.astype(BF16)]
    all_to_all x18 -> x5, waiting for transfers between devices: 49.3 us -> 18.6 us  [sync(): lax.all_to_all(copies, ('inner', 'outer'), split_axis=0, concat_axis=0, t...]
    reduce_sum x27 -> x5, other arithmetic: 25.1 us -> 3.26 us  [the longest x4 2.63 us: scatter(): return over_batch(jnp.sum(parts.astype(F32), axis=0))]
  transfers between devices with their start and end apart: 114 -> 83, of which waited for: 30 -> 38; matrix products, arithmetic and copies ran while one was open for 39% -> 6% of each run, Pallas kernels for 1% -> 9%
where the time goes in v3:
time: 555 us; the launch traced here: 545 us
  waiting for transfers between devices  203 us (37%)
  starting transfers between devices  114 us (21%)
  blocking collectives  76 us (14%)
  Pallas kernels  69.2 us (12%)
  local copies, waits for them, and re-layouts  58.7 us (11%)
  other arithmetic  20.6 us (4%)
    all_to_all x7, blocking collectives, sync(): lax.all_to_all(copies, ('inner', 'outer'), split_axis=0, concat_axis=0, t...  76 us
    pallas_call x45, Pallas kernels, run(): pl.pallas_call(kernel, out_shape=shapes, in_specs=[pl.BlockSpec(memory_sp...  69.2 us
    unnamed x264, local copies, waits for them, and re-layouts  49.1 us
    ppermute x4, waiting for transfers between devices, gather(): low = lax.ppermute(by_x[:, :h], 'inner', YS)  47.3 us
    all_to_all x8, waiting for transfers between devices, to_images(): return lax.all_to_all(x, 'outer', split_axis=0, concat_axis=0, tiled=True)  44.9 us
    all_to_all x8, starting transfers between devices, to_images(): return lax.all_to_all(x, 'outer', split_axis=0, concat_axis=0, tiled=True)  36.5 us
    ppermute x12, waiting for transfers between devices, gather(): pieces.append(lax.ppermute(pieces[-1], 'outer', ring))  33.3 us
    ppermute x4, waiting for transfers between devices, scatter(): by_x = lax.ppermute(to_x, 'inner', XS)  29.3 us
  transfers between devices with their start and end apart: 83, of which 38 were waited for; matrix products, arithmetic and copies ran while one was open for 6% of the time, Pallas kernels for 9%

profile of v3, /device:TPU:0, one launch (start us, length us, event | category | flops | bytes accessed | tf_op | source)
XLA Modules:
  0.0 544.6 jit_solution(15315068936019719889)
XLA Ops:
  0.7 6.5 %all-to-all-start = ((bf16[4,512,256]{2,1,0:T(8,128)(2,1)}), bf16[4,512,256]{2,1,0:T(8,128)(2,1)S(1)}, u32[]{:S(2)}, u32[]{:S(2)}) async-start(bf16[4,512,256]{2,1,0:T(8,128)(2,1)} %bitcast.104), calls=%async_computation | async-start | bytes 2097152 | tf_op jit(solution)/shard_map/all_to_all | solution.py:145
  13.1 17.3 %collective-permute-done.1 = bf16[64,256]{1,0:T(8,128)(2,1)S(1)} collective-permute-done((bf16[64,256]{1,0:T(8,128)(2,1)S(1)}, bf16[64,256]{1,0:T(8,128)(2,1)S(1)}, u32[]{:S(2)}, u32[]{:S(2)}) %collective-permute-start.1) | collective-permute-done | bytes 32800 | tf_op jit(solution)/shard_map/ppermute | solution.py:206
  38.3 3.5 collective-permute-start.3
  63.3 10.9 %collective-permute-done.6.refs_3_ = bf16[4,32,256]{2,1,0:T(8,128)(2,1)S(1)} collective-permute-done((bf16[4,32,256]{2,1,0:T(8,128)(2,1)}, bf16[4,32,256]{2,1,0:T(8,128)(2,1)S(1)}, u32[]{:S(2)}, u32[]{:S(2)}) %collective-permute-start.6) | collective-permute-done | bytes 65568 | tf_op jit(solution)/shard_map/ppermute | solution.py:211
  79.6 8.4 %collective-permute-done.20 = bf16[384,256]{1,0:T(8,128)(2,1)S(1)} collective-permute-done((bf16[384,256]{1,0:T(8,128)(2,1)}, bf16[384,256]{1,0:T(8,128)(2,1)S(1)}, u32[]{:S(2)}, u32[]{:S(2)}) %collective-permute-start.20) | collective-permute-done | bytes 196640 | tf_op jit(solution)/shard_map/ppermute | solution.py:206
  109.9 35.1 %collective-permute-done.14.refs_3_ = bf16[4,144,256]{2,1,0:T(8,128)(2,1)S(1)} collective-permute-done((bf16[4,144,256]{2,1,0:T(8,128)(2,1)S(1)}, bf16[4,144,256]{2,1,0:T(8,128)(2,1)S(1)}, u32[]{:S(2)}, u32[]{:S(2)}) %collective-permute-start.14) | collective-permute-done | bytes 294944 | tf_op jit(solution)/shard_map/ppermute | solution.py:211
  160.5 9.9 %all_to_all.100.got = f32[16,2,256]{2,1,0:T(2,128)S(1)} all-to-all(f32[16,2,256]{2,1,0:T(2,128)S(1)} %get-tuple-element.122), channel_id=1, replica_groups=mesh['batch'=2,'inner'=4,'outer'=4] {'inner','outer'}, dimensions={0} | all-to-all | bytes 65536 | tf_op jit(solution)/shard_map/all_to_all | solution.py:141
  184.3 4.4 all-to-all-start.3
  208.8 10.9 %all_to_all.101.got = f32[16,2,256]{2,1,0:T(2,128)S(1)} all-to-all(f32[16,2,256]{2,1,0:T(2,128)S(1)} %get-tuple-element.133), channel_id=1, replica_groups=mesh['batch'=2,'inner'=4,'outer'=4] {'inner','outer'}, dimensions={0} | all-to-all | bytes 65536 | tf_op jit(solution)/shard_map/all_to_all | solution.py:141
  225.5 10.6 %all_to_all.102.got = f32[16,2,256]{2,1,0:T(2,128)} all-to-all(f32[16,2,256]{2,1,0:T(2,128)S(1)} %get-tuple-element.138), channel_id=1, replica_groups=mesh['batch'=2,'inner'=4,'outer'=4] {'inner','outer'}, dimensions={0} | all-to-all | bytes 65536 | tf_op jit(solution)/shard_map/all_to_all | solution.py:141
  236.1 4.1 all-to-all-start.7
  242.8 11.6 %all-to-all-done.7 = bf16[4,128,512]{2,1,0:T(8,128)(2,1)} async-done(((bf16[4,128,512]{2,1,0:T(8,128)(2,1)}), bf16[4,128,512]{2,1,0:T(8,128)(2,1)}, u32[]{:S(2)}, u32[]{:S(2)}) %all-to-all-start.7) | async-done | bytes 524320 | tf_op jit(solution)/shard_map/all_to_all | solution.py:145
  264.6 8.3 %all-to-all-done.6.got = f32[16,2,1024]{2,1,0:T(2,128)S(1)} async-done(((f32[16,2,1024]{2,1,0:T(2,128)}), f32[16,2,1024]{2,1,0:T(2,128)S(1)}, u32[]{:S(2)}, u32[]{:S(2)}) %all-to-all-start.6) | async-done | bytes 131104 | tf_op jit(solution)/shard_map/all_to_all | solution.py:141
  276.1 3.6 shard_map.254
  279.8 10.6 %all_to_all.103.grads = f32[16,2,1024]{2,1,0:T(2,128)S(1)} all-to-all(f32[16,2,1024]{2,1,0:T(2,128)S(1)} %get-tuple-element.146), channel_id=1, replica_groups=mesh['batch'=2,'inner'=4,'outer'=4] {'inner','outer'}, dimensions={0} | all-to-all | bytes 262144 | tf_op jit(solution)/shard_map/all_to_all | solution.py:141
  294.5 10.1 %all_to_all.104.grads = f32[16,2,256]{2,1,0:T(2,128)S(1)} all-to-all(f32[16,2,256]{2,1,0:T(2,128)S(1)} %get-tuple-element.150), channel_id=1, replica_groups=mesh['batch'=2,'inner'=4,'outer'=4] {'inner','outer'}, dimensions={0} | all-to-all | bytes 65536 | tf_op jit(solution)/shard_map/all_to_all | solution.py:141
  309.6 10.1 %all_to_all.105.grads = f32[16,2,256]{2,1,0:T(2,128)S(1)} all-to-all(f32[16,2,256]{2,1,0:T(2,128)S(1)} %get-tuple-element.153), channel_id=1, replica_groups=mesh['batch'=2,'inner'=4,'outer'=4] {'inner','outer'}, dimensions={0} | all-to-all | bytes 65536 | tf_op jit(solution)/shard_map/all_to_all | solution.py:141
  324.4 13.7 %all_to_all.106.grads = f32[16,3,1024]{2,1,0:T(4,128)S(1)} all-to-all(f32[16,3,1024]{2,1,0:T(4,128)S(1)} %get-tuple-element.157), channel_id=1, replica_groups=mesh['batch'=2,'inner'=4,'outer'=4] {'inner','outer'}, dimensions={0} | all-to-all | bytes 393216 | tf_op jit(solution)/shard_map/all_to_all | solution.py:141
  348.4 7.1 %all-to-all-done.13.grads = f32[16,2,256]{2,1,0:T(2,128)S(1)} async-done(((f32[16,2,256]{2,1,0:T(2,128)}), f32[16,2,256]{2,1,0:T(2,128)S(1)}, u32[]{:S(2)}, u32[]{:S(2)}) %all-to-all-start.13) | async-done | bytes 32800 | tf_op jit(solution)/shard_map/all_to_all | solution.py:141
  379.0 4.1 all-to-all-start.8
  387.6 6.5 %collective-permute-done.51.a = bf16[4,144,256]{2,1,0:T(8,128)(2,1)S(1)} collective-permute-done((bf16[4,144,256]{2,1,0:T(8,128)(2,1)S(1)}, bf16[4,144,256]{2,1,0:T(8,128)(2,1)S(1)}, u32[]{:S(2)}, u32[]{:S(2)}) %collective-permute-start.51) | collective-permute-done | bytes 294944 | tf_op jit(solution)/shard_map/ppermute | solution.py:257
  406.0 5.7 %collective-permute-done.46.a = bf16[4,32,256]{2,1,0:T(8,128)(2,1)S(1)} collective-permute-done((bf16[4,32,256]{2,1,0:T(8,128)(2,1)S(1)}, bf16[4,32,256]{2,1,0:T(8,128)(2,1)S(1)}, u32[]{:S(2)}, u32[]{:S(2)}) %collective-permute-start.46) | collective-permute-done | bytes 65568 | tf_op jit(solution)/shard_map/ppermute | solution.py:257
  421.3 4.4 all-to-all-start.16
  426.7 4.9 all-to-all-done.16
  431.6 4.2 all-to-all-start.17
  447.3 10.6 %collective-permute-done.58.y = bf16[4,384,256]{2,1,0:T(8,128)(2,1)S(1)} collective-permute-done((bf16[4,384,256]{2,1,0:T(8,128)(2,1)S(1)}, bf16[4,384,256]{2,1,0:T(8,128)(2,1)S(1)}, u32[]{:S(2)}, u32[]{:S(2)}) %collective-permute-start.58) | collective-permute-done | bytes 786464 | tf_op jit(solution)/shard_map/ppermute | solution.py:267
  459.4 4.7 all-to-all-start.18
  469.1 18.7 %collective-permute-done.63.y = bf16[4,544,256]{2,1,0:T(8,128)(2,1)S(1)} collective-permute-done((bf16[4,544,256]{2,1,0:T(8,128)(2,1)S(1)}, bf16[4,544,256]{2,1,0:T(8,128)(2,1)S(1)}, u32[]{:S(2)}, u32[]{:S(2)}) %collective-permute-start.63) | collective-permute-done | bytes 1114144 | tf_op jit(solution)/shard_map/ppermute | solution.py:267
  489.5 4.9 all-to-all-start.19
  501.0 13.5 %all-to-all-done.19 = bf16[4,544,256]{2,1,0:T(8,128)(2,1)S(1)} async-done(((bf16[4,544,256]{2,1,0:T(8,128)(2,1)}), bf16[4,544,256]{2,1,0:T(8,128)(2,1)S(1)}, u32[]{:S(2)}, u32[]{:S(2)}) %all-to-all-start.19) | async-done | bytes 1114144 | tf_op jit(solution)/shard_map/all_to_all | solution.py:145
  514.5 3.5 all-to-all-start.15
  527.8 12.0 %all-to-all-done.15 = bf16[4,512,256]{2,1,0:T(8,128)(2,1)S(1)} async-done(((bf16[4,512,256]{2,1,0:T(8,128)(2,1)}), bf16[4,512,256]{2,1,0:T(8,128)(2,1)S(1)}, u32[]{:S(2)}, u32[]{:S(2)}) %all-to-all-start.15) | async-done | bytes 1048608 | tf_op jit(solution)/shard_map/all_to_all | solution.py:145
  (514 shorter events, 246.7 us)
Async XLA Ops:
  0.7 52.4 %all-to-all-start = ((bf16[4,512,256]{2,1,0:T(8,128)(2,1)}), bf16[4,512,256]{2,1,0:T(8,128)(2,1)S(1)}, u32[]{:S(2)}, u32[]{:S(2)}) async-start(bf16[4,512,256]{2,1,0:T(8,128)(2,1)} %bitcast.104), calls=%async_computation | async-start | bytes 2097152 | tf_op jit(solution)/shard_map/all_to_all | solution.py:145
  7.2 23.2 %collective-permute-start.1 = (bf16[64,256]{1,0:T(8,128)(2,1)S(1)}, bf16[64,256]{1,0:T(8,128)(2,1)S(1)}, u32[]{:S(2)}, u32[]{:S(2)}) collective-permute-start(bf16[64,256]{1,0:T(8,128)(2,1)S(1)} %get-tuple-element.233), channel_id=1, source_target_pairs={{0,1},{1,2},{2,3},{3,0},{4,5},{5,6},{6,7},{7,4},{8,9},{9,10},{10,1... | collective-permute-start | bytes 98312 | tf_op jit(solution)/shard_map/ppermute | solution.py:206
  9.3 32.5 %collective-permute-start.9 = (bf16[288,256]{1,0:T(8,128)(2,1)S(1)}, bf16[288,256]{1,0:T(8,128)(2,1)S(1)}, u32[]{:S(2)}, u32[]{:S(2)}) collective-permute-start(bf16[288,256]{1,0:T(8,128)(2,1)S(1)} %bitcast.105), channel_id=1, source_target_pairs={{0,1},{1,2},{2,3},{3,0},{4,5},{5,6},{6,7},{7,4},{8,9},{9,10},{10,1... | collective-permute-start | bytes 442376 | tf_op jit(solution)/shard_map/ppermute | solution.py:206
  11.6 46.8 %collective-permute-start.18 = (bf16[384,256]{1,0:T(8,128)(2,1)S(1)}, bf16[384,256]{1,0:T(8,128)(2,1)}, u32[]{:S(2)}, u32[]{:S(2)}) collective-permute-start(bf16[384,256]{1,0:T(8,128)(2,1)S(1)} %get-tuple-element.222), channel_id=1, source_target_pairs={{0,1},{1,2},{2,3},{3,0},{4,5},{5,6},{6,7},{7,4},{8,9},{9,10},{10,1... | collective-permute-start | bytes 589832 | tf_op jit(solution)/shard_map/ppermute | solution.py:206
  34.5 26.5 %collective-permute-start.26 = (bf16[544,256]{1,0:T(8,128)(2,1)S(1)}, bf16[544,256]{1,0:T(8,128)(2,1)}, u32[]{:S(2)}, u32[]{:S(2)}) collective-permute-start(bf16[544,256]{1,0:T(8,128)(2,1)S(1)} %get-tuple-element.220), channel_id=1, source_target_pairs={{0,1},{1,2},{2,3},{3,0},{4,5},{5,6},{6,7},{7,4},{8,9},{9,10},{10,1... | collective-permute-start | bytes 835592 | tf_op jit(solution)/shard_map/ppermute | solution.py:206
  53.9 20.9 %collective-permute-start = (bf16[4,1,512,128]{3,2,1,0:T(8,128)(2,1)}, bf16[4,1,512,128]{3,2,1,0:T(8,128)(2,1)S(1)}, u32[]{:S(2)}, u32[]{:S(2)}) collective-permute-start(bf16[4,1,512,128]{3,2,1,0:T(8,128)(2,1)} %slice_select_fusion), channel_id=1, source_target_pairs={{0,16},{16,0},{1,17},{17,1},{2,18},{18,2},{3,19},{19,3},{4,20},{20... | collective-permute-start | bytes 1572872 | tf_op jit(solution)/shard_map/ppermute | solution.py:117
  58.4 20.1 %collective-permute-start.13 = (bf16[4,288,256]{2,1,0:T(8,128)(2,1)S(1)}, bf16[4,288,256]{2,1,0:T(8,128)(2,1)S(1)}, u32[]{:S(2)}, u32[]{:S(2)}) collective-permute-start(bf16[4,288,256]{2,1,0:T(8,128)(2,1)S(1)} %pad_maximum_fusion.2.refs_0_), channel_id=1, source_target_pairs={{0,8},{4,12},{8,0},{12,4},{1,9},{5,13},{9,1},{13,5},{2,10},{6,14},... | collective-permute-start | bytes 1769480 | tf_op jit(solution)/shard_map/ppermute | solution.py:210
  76.9 24.4 %collective-permute-start.8 = (f32[1024,256]{1,0:T(8,128)S(1)}, f32[1024,256]{1,0:T(8,128)S(1)}, u32[]{:S(2)}, u32[]{:S(2)}) collective-permute-start(f32[1024,256]{1,0:T(8,128)S(1)} %get-tuple-element.116), channel_id=1, source_target_pairs={{0,16},{16,0},{1,17},{17,1},{2,18},{18,2},{3,19},{19,3},{4,20},{20... | collective-permute-start | bytes 3145736 | tf_op jit(solution)/shard_map/ppermute | solution.py:117
  77.0 20.5 %collective-permute-start.12 = (bf16[4,288,256]{2,1,0:T(8,128)(2,1)S(1)}, bf16[4,288,256]{2,1,0:T(8,128)(2,1)S(1)}, u32[]{:S(2)}, u32[]{:S(2)}) collective-permute-start(bf16[4,288,256]{2,1,0:T(8,128)(2,1)S(1)} %pad_maximum_fusion.2.refs_0_), channel_id=1, source_target_pairs={{0,4},{4,0},{8,12},{12,8},{1,5},{5,1},{9,13},{13,9},{2,6},{6,2},{1... | collective-permute-start | bytes 1769480 | tf_op jit(solution)/shard_map/ppermute | solution.py:209
  78.5 20.6 %collective-permute-start.15 = (bf16[4,144,256]{2,1,0:T(8,128)(2,1)S(1)}, bf16[4,144,256]{2,1,0:T(8,128)(2,1)S(1)}, u32[]{:S(2)}, u32[]{:S(2)}) collective-permute-start(bf16[4,144,256]{2,1,0:T(8,128)(2,1)S(1)} %slice.249), channel_id=1, source_target_pairs={{0,4},{4,0},{8,12},{12,8},{1,5},{5,1},{9,13},{13,9},{2,6},{6,2},{1... | collective-permute-start | bytes 884744 | tf_op jit(solution)/shard_map/ppermute | solution.py:212
  95.4 75.8 %collective-permute-start.30 = (bf16[4,544,256]{2,1,0:T(8,128)(2,1)}, bf16[4,544,256]{2,1,0:T(8,128)(2,1)}, u32[]{:S(2)}, u32[]{:S(2)}) collective-permute-start(bf16[4,544,256]{2,1,0:T(8,128)(2,1)} %pad_maximum_fusion.refs_0_), channel_id=1, source_target_pairs={{0,8},{4,12},{8,0},{12,4},{1,9},{5,13},{9,1},{13,5},{2,10},{6,14},... | collective-permute-start | bytes 3342344 | tf_op jit(solution)/shard_map/ppermute | solution.py:210
  97.0 56.9 %collective-permute-start.22 = (bf16[4,384,256]{2,1,0:T(8,128)(2,1)}, bf16[4,384,256]{2,1,0:T(8,128)(2,1)}, u32[]{:S(2)}, u32[]{:S(2)}) collective-permute-start(bf16[4,384,256]{2,1,0:T(8,128)(2,1)} %pad_maximum_fusion.1.refs_0_), channel_id=1, source_target_pairs={{0,8},{4,12},{8,0},{12,4},{1,9},{5,13},{9,1},{13,5},{2,10},{6,14},... | collective-permute-start | bytes 2359304 | tf_op jit(solution)/shard_map/ppermute | solution.py:210
  97.5 58.7 %collective-permute-start.21 = (bf16[4,384,256]{2,1,0:T(8,128)(2,1)}, bf16[4,384,256]{2,1,0:T(8,128)(2,1)}, u32[]{:S(2)}, u32[]{:S(2)}) collective-permute-start(bf16[4,384,256]{2,1,0:T(8,128)(2,1)} %pad_maximum_fusion.1.refs_0_), channel_id=1, source_target_pairs={{0,4},{4,0},{8,12},{12,8},{1,5},{5,1},{9,13},{13,9},{2,6},{6,2},{1... | collective-permute-start | bytes 2359304 | tf_op jit(solution)/shard_map/ppermute | solution.py:209
  99.1 74.1 %collective-permute-start.29 = (bf16[4,544,256]{2,1,0:T(8,128)(2,1)}, bf16[4,544,256]{2,1,0:T(8,128)(2,1)}, u32[]{:S(2)}, u32[]{:S(2)}) collective-permute-start(bf16[4,544,256]{2,1,0:T(8,128)(2,1)} %pad_maximum_fusion.refs_0_), channel_id=1, source_target_pairs={{0,4},{4,0},{8,12},{12,8},{1,5},{5,1},{9,13},{13,9},{2,6},{6,2},{1... | collective-permute-start | bytes 3342344 | tf_op jit(solution)/shard_map/ppermute | solution.py:209
  101.3 43.7 %collective-permute-start.14 = (bf16[4,144,256]{2,1,0:T(8,128)(2,1)S(1)}, bf16[4,144,256]{2,1,0:T(8,128)(2,1)S(1)}, u32[]{:S(2)}, u32[]{:S(2)}) collective-permute-start(bf16[4,144,256]{2,1,0:T(8,128)(2,1)S(1)} %slice.248), channel_id=1, source_target_pairs={{0,8},{4,12},{8,0},{12,4},{1,9},{5,13},{9,1},{13,5},{2,10},{6,14},... | collective-permute-start | bytes 884744 | tf_op jit(solution)/shard_map/ppermute | solution.py:211
  106.3 45.2 %all-to-all-start.1 = ((f32[16,2,256]{2,1,0:T(2,128)}), f32[16,2,256]{2,1,0:T(2,128)S(1)}, u32[]{:S(2)}, u32[]{:S(2)}) async-start(f32[16,2,256]{2,1,0:T(2,128)} %get-tuple-element.118), calls=%async_computation.1 | async-start | bytes 65536 | tf_op jit(solution)/shard_map/all_to_all | solution.py:141
  155.2 20.5 %collective-permute-start.24 = (bf16[4,192,256]{2,1,0:T(8,128)(2,1)S(1)}, bf16[4,192,256]{2,1,0:T(8,128)(2,1)S(1)}, u32[]{:S(2)}, u32[]{:S(2)}) collective-permute-start(bf16[4,192,256]{2,1,0:T(8,128)(2,1)S(1)} %slice.251), channel_id=1, source_target_pairs={{0,4},{4,0},{8,12},{12,8},{1,5},{5,1},{9,13},{13,9},{2,6},{6,2},{1... | collective-permute-start | bytes 1179656 | tf_op jit(solution)/shard_map/ppermute | solution.py:212
  348.2 28.9 %collective-permute-start.37 = (bf16[128,1024]{1,0:T(8,128)(2,1)}, bf16[128,1024]{1,0:T(8,128)(2,1)}, u32[]{:S(2)}, u32[]{:S(2)}) collective-permute-start(bf16[128,1024]{1,0:T(8,128)(2,1)} %copy-done.112), channel_id=1, source_target_pairs={{0,16},{16,0},{1,17},{17,1},{2,18},{18,2},{3,19},{19,3},{4,20},{20... | collective-permute-start | bytes 786440 | tf_op jit(solution)/shard_map/ppermute | solution.py:117
  373.9 23.8 %collective-permute-start.44 = (f32[256,512]{1,0:T(8,128)}, f32[256,512]{1,0:T(8,128)}, u32[]{:S(2)}, u32[]{:S(2)}) collective-permute-start(f32[256,512]{1,0:T(8,128)} %get-tuple-element.168), channel_id=1, source_target_pairs={{0,16},{16,0},{1,17},{17,1},{2,18},{18,2},{3,19},{19,3},{4,20},{20... | collective-permute-start | bytes 1572872 | tf_op jit(solution)/shard_map/ppermute | solution.py:117
  377.1 20.7 %collective-permute-start.43 = (bf16[1024,256]{1,0:T(8,128)(2,1)}, bf16[1024,256]{1,0:T(8,128)(2,1)}, u32[]{:S(2)}, u32[]{:S(2)}) collective-permute-start(bf16[1024,256]{1,0:T(8,128)(2,1)} %get-tuple-element.165.x), channel_id=1, source_target_pairs={{0,16},{16,0},{1,17},{17,1},{2,18},{18,2},{3,19},{19,3},{4,20},{20... | collective-permute-start | bytes 1572872 | tf_op jit(solution)/shard_map/ppermute | solution.py:117
  379.0 42.3 %all-to-all-start.8 = ((bf16[4,128,512]{2,1,0:T(8,128)(2,1)}), bf16[4,128,512]{2,1,0:T(8,128)(2,1)}, u32[]{:S(2)}, u32[]{:S(2)}) async-start(bf16[4,128,512]{2,1,0:T(8,128)(2,1)} %bitcast.33), calls=%async_computation.8 | async-start | bytes 1048576 | tf_op jit(solution)/shard_map/all_to_all | solution.py:145
  395.7 30.0 %collective-permute-start.53 = (bf16[4,288,256]{2,1,0:T(8,128)(2,1)}, bf16[4,288,256]{2,1,0:T(8,128)(2,1)S(1)}, u32[]{:S(2)}, u32[]{:S(2)}) collective-permute-start(bf16[4,288,256]{2,1,0:T(8,128)(2,1)} %get-tuple-element.186), channel_id=1, source_target_pairs={{0,4},{4,0},{8,12},{12,8},{1,5},{5,1},{9,13},{13,9},{2,6},{6,2},{1... | collective-permute-start | bytes 1769480 | tf_op jit(solution)/shard_map/ppermute | solution.py:267
  396.9 28.7 %collective-permute-start.54 = (bf16[4,288,256]{2,1,0:T(8,128)(2,1)}, bf16[4,288,256]{2,1,0:T(8,128)(2,1)S(1)}, u32[]{:S(2)}, u32[]{:S(2)}) collective-permute-start(bf16[4,288,256]{2,1,0:T(8,128)(2,1)} %get-tuple-element.187), channel_id=1, source_target_pairs={{0,8},{4,12},{8,0},{12,4},{1,9},{5,13},{9,1},{13,5},{2,10},{6,14},... | collective-permute-start | bytes 1769480 | tf_op jit(solution)/shard_map/ppermute | solution.py:268
  431.6 27.8 %all-to-all-start.17 = ((bf16[4,288,256]{2,1,0:T(8,128)(2,1)}), bf16[4,288,256]{2,1,0:T(8,128)(2,1)}, u32[]{:S(2)}, u32[]{:S(2)}) async-start(bf16[4,288,256]{2,1,0:T(8,128)(2,1)} %shard_map.275), calls=%async_computation.17 | async-start | bytes 1179648 | tf_op jit(solution)/shard_map/all_to_all | solution.py:145
  437.3 20.5 %collective-permute-start.58 = (bf16[4,384,256]{2,1,0:T(8,128)(2,1)S(1)}, bf16[4,384,256]{2,1,0:T(8,128)(2,1)S(1)}, u32[]{:S(2)}, u32[]{:S(2)}) collective-permute-start(bf16[4,384,256]{2,1,0:T(8,128)(2,1)S(1)} %get-tuple-element.196), channel_id=1, source_target_pairs={{0,4},{4,0},{8,12},{12,8},{1,5},{5,1},{9,13},{13,9},{2,6},{6,2},{1... | collective-permute-start | bytes 2359304 | tf_op jit(solution)/shard_map/ppermute | solution.py:267
  438.0 20.3 %collective-permute-start.59 = (bf16[4,384,256]{2,1,0:T(8,128)(2,1)S(1)}, bf16[4,384,256]{2,1,0:T(8,128)(2,1)S(1)}, u32[]{:S(2)}, u32[]{:S(2)}) collective-permute-start(bf16[4,384,256]{2,1,0:T(8,128)(2,1)S(1)} %get-tuple-element.197), channel_id=1, source_target_pairs={{0,8},{4,12},{8,0},{12,4},{1,9},{5,13},{9,1},{13,5},{2,10},{6,14},... | collective-permute-start | bytes 2359304 | tf_op jit(solution)/shard_map/ppermute | solution.py:268
  445.0 20.4 %collective-permute-start.61 = (bf16[4,272,256]{2,1,0:T(8,128)(2,1)}, bf16[4,272,256]{2,1,0:T(8,128)(2,1)}, u32[]{:S(2)}, u32[]{:S(2)}) collective-permute-start(bf16[4,272,256]{2,1,0:T(8,128)(2,1)} %get-tuple-element.207), channel_id=1, source_target_pairs={{0,4},{4,0},{8,12},{12,8},{1,5},{5,1},{9,13},{13,9},{2,6},{6,2},{1... | collective-permute-start | bytes 1671176 | tf_op jit(solution)/shard_map/ppermute | solution.py:257
  459.4 30.1 %all-to-all-start.18 = ((bf16[4,384,256]{2,1,0:T(8,128)(2,1)}), bf16[4,384,256]{2,1,0:T(8,128)(2,1)}, u32[]{:S(2)}, u32[]{:S(2)}) async-start(bf16[4,384,256]{2,1,0:T(8,128)(2,1)} %shard_map.278), calls=%async_computation.18 | async-start | bytes 1572864 | tf_op jit(solution)/shard_map/all_to_all | solution.py:145
  466.9 20.9 %collective-permute-start.63 = (bf16[4,544,256]{2,1,0:T(8,128)(2,1)S(1)}, bf16[4,544,256]{2,1,0:T(8,128)(2,1)S(1)}, u32[]{:S(2)}, u32[]{:S(2)}) collective-permute-start(bf16[4,544,256]{2,1,0:T(8,128)(2,1)S(1)} %get-tuple-element.209), channel_id=1, source_target_pairs={{0,4},{4,0},{8,12},{12,8},{1,5},{5,1},{9,13},{13,9},{2,6},{6,2},{1... | collective-permute-start | bytes 3342344 | tf_op jit(solution)/shard_map/ppermute | solution.py:267
  489.5 25.0 %all-to-all-start.19 = ((bf16[4,544,256]{2,1,0:T(8,128)(2,1)}), bf16[4,544,256]{2,1,0:T(8,128)(2,1)S(1)}, u32[]{:S(2)}, u32[]{:S(2)}) async-start(bf16[4,544,256]{2,1,0:T(8,128)(2,1)} %shard_map.281), calls=%async_computation.19 | async-start | bytes 2228224 | tf_op jit(solution)/shard_map/all_to_all | solution.py:145
  497.8 22.7 %collective-permute-start.50 = (f32[128,128]{1,0:T(8,128)S(1)}, f32[128,128]{1,0:T(8,128)S(1)}, u32[]{:S(2)}, u32[]{:S(2)}) collective-permute-start(f32[128,128]{1,0:T(8,128)S(1)} %pad_maximum_fusion.8), channel_id=1, source_target_pairs={{0,16},{16,0},{1,17},{17,1},{2,18},{18,2},{3,19},{19,3},{4,20},{20... | collective-permute-start | bytes 196616 | tf_op jit(solution)/shard_map/ppermute | solution.py:117
  514.5 25.4 %all-to-all-start.15 = ((bf16[4,512,256]{2,1,0:T(8,128)(2,1)}), bf16[4,512,256]{2,1,0:T(8,128)(2,1)S(1)}, u32[]{:S(2)}, u32[]{:S(2)}) async-start(bf16[4,512,256]{2,1,0:T(8,128)(2,1)} %bitcast.35), calls=%async_computation.15 | async-start | bytes 2097152 | tf_op jit(solution)/shard_map/all_to_all | solution.py:145
  (178 other events, 1410.9 us)
